TPU v7x, 512 devices: a whole 4x4x16 slice. The times are simulated.
512 devices in a mesh: expert: 128 (over x, z, core), dp: 4 (over y).
Axes of the slice: x: 4, y: 4, z: 16, core: 2. Of those that a mesh axis runs over, the one named last changes fastest.
Arguments:
- tokens_in: bfloat16 [16384, 3584], P('expert', 'dp'), may hold values from -6 to 6
- out_grad: bfloat16 [16384, 3584], P('expert', 'dp'), may hold values from -0.31 to 0.31
- expert_ids: int32 [16384, 8], P('expert'), may hold values from 0 to 383, all different within a row; in each aligned block of 128 rows (0 to 127, 128 to 255, ...) at most 6 rows name the same one
- combine: bfloat16 [16384, 8], P('expert'), may hold values from 0.049804688 to 0.5
- down_weight: bfloat16 [128, 1024, 3584], P('expert', 'dp'), may hold values from -2 to 2
- gate_saved: bfloat16 [128, 768, 1024], P('expert', None, 'dp'), may hold values from -6 to 6
- up_saved: bfloat16 [128, 768, 1024], P('expert', None, 'dp'), may hold values from -6 to 6
Outputs:
- update: bfloat16 [128, 3584, 1024], P('expert', 'dp')
- dcombine: float32 [16384, 8], P('expert')
Inputs may be any that keep to these rules, and one draw needn't show every extreme that they name: `expert_ids`: each row names 8 different experts. In each aligned block of 128 rows no expert is named by more than 6 rows, a bound that some block reaches.
All inputs are finite; a program needn't handle non-finite values.
Results may differ from a plain program's by a relative error of at most 0.018.
Values may be sent and summed in bfloat16 or wider, within the bound.
No kernel may reach another device: no remote copies, remote signals or barrier semaphores. Data moves between devices by JAX's collectives and lax.ppermute only.
A program may use at most 64 MiB of HBM per device.

v0:
```python
import math

import jax
import jax.numpy as jnp
from jax import lax
from jax.sharding import PartitionSpec as P

D = 3584


poly_first = 8.28721201814563
poly_third = -23.595886519098837
poly_fifth = 17.300387312530933


def block_positions(block_routes):
    flat_ids = block_routes.reshape(-1)
    pair_count = flat_ids.shape[0]
    same_id = flat_ids[:, None] == flat_ids[None, :]
    earlier = jnp.arange(pair_count)[None, :] < jnp.arange(pair_count)[:, None]
    return jnp.sum(jnp.logical_and(same_id, earlier), axis=1)


def return_grad(values):
    return lax.all_to_all(values, "expert", split_axis=0, concat_axis=0, tiled=True)


def on_device(tokens_in, out_grad, expert_ids, combine, down_weight, gate_saved, up_saved):
    experts = lax.axis_size("expert")
    slot_total = gate_saved.shape[1]
    capacity = slot_total // experts
    tok_rows, top_count = expert_ids.shape
    flat_ids = expert_ids.reshape(-1)
    position = block_positions(expert_ids)
    is_live = flat_ids < experts
    target = jnp.where(is_live, flat_ids * capacity + position, -1)
    slot_iota = jnp.arange(slot_total, dtype=jnp.int32)
    matches = (target[None, :] == slot_iota[:, None]).reshape(slot_total, tok_rows, top_count)
    selector = jnp.any(matches, axis=2).astype(jnp.bfloat16)
    weight_send = jnp.sum(
        jnp.where(matches, combine.astype(jnp.float32)[None], 0.0), axis=(1, 2)
    ).astype(jnp.bfloat16)
    row_send = jnp.dot(selector, tokens_in, preferred_element_type=jnp.float32).astype(jnp.bfloat16)
    matrix = down_weight[0]
    grad_send = jnp.dot(selector, out_grad, preferred_element_type=jnp.float32).astype(jnp.bfloat16)
    row_recv, grad_recv, weight_recv = (
        lax.all_to_all(row_send, "expert", split_axis=0, concat_axis=0, tiled=True),
        lax.all_to_all(grad_send, "expert", split_axis=0, concat_axis=0, tiled=True),
        lax.all_to_all(weight_send, "expert", split_axis=0, concat_axis=0, tiled=True),
    )
    hidden_grad = lax.dot_general(
        lax.all_gather(grad_recv, "dp", axis=1, tiled=True),
        matrix,
        (((1,), (1,)), ((), ())),
        preferred_element_type=jnp.float32,
    )
    gate_act = jax.nn.silu(gate_saved[0].astype(jnp.float32))
    hidden_act = gate_act * up_saved[0].astype(jnp.float32)
    weight_part = jnp.sum(hidden_grad * hidden_act, axis=1)
    up_grad = (weight_recv.astype(jnp.float32)[:, None] * hidden_grad * gate_act).astype(
        jnp.bfloat16
    )
    weight_total = lax.psum(weight_part, "dp")
    returned = return_grad(weight_total)
    gradient = lax.dot_general(
        row_recv,
        lax.all_gather(up_grad, "dp", axis=1, tiled=True),
        (((0,), (0,)), ((), ())),
        preferred_element_type=jnp.float32,
    )
    squares = jnp.sum(gradient * gradient)
    norm_total = lax.psum(squares, "dp")
    start_iter = (gradient / (1.01 * jnp.sqrt(norm_total) + 1e-07)).astype(jnp.bfloat16)
    gram_part = lax.dot_general(
        start_iter, start_iter, (((0,), (0,)), ((), ())), preferred_element_type=jnp.float32
    )
    gram = lax.psum(gram_part.astype(jnp.bfloat16), "dp")
    part_rows = gram.shape[0] // lax.axis_size("dp")
    own_rows = lax.dynamic_slice_in_dim(gram, lax.axis_index("dp") * part_rows, part_rows, 0)
    square = jnp.dot(own_rows, gram, preferred_element_type=jnp.float32)
    quartic = lax.psum(jnp.sum(square * square), "dp")
    bound = jnp.sqrt(jnp.sqrt(quartic)) + 1e-06
    first_scale = poly_third / bound
    second_scale = poly_fifth / (bound * bound)
    poly_rows = (first_scale * own_rows.astype(jnp.float32) + second_scale * square).astype(
        jnp.bfloat16
    )
    mixed = jnp.dot(
        start_iter,
        lax.all_gather(poly_rows, "dp", axis=0, tiled=True),
        preferred_element_type=jnp.float32,
    )
    update = (math.sqrt(D) * (poly_first * start_iter.astype(jnp.float32) + mixed)).astype(
        jnp.bfloat16
    )
    picked = returned[jnp.maximum(target, 0)]
    dcombine = jnp.where(is_live, picked, jnp.float32(0.0)).reshape(tok_rows, top_count)
    return (update[None], dcombine)


def solution(mesh):
    in_specs = (
        P("expert", "dp"),
        P("expert", "dp"),
        P("expert", None),
        P("expert", None),
        P("expert", "dp", None),
        P("expert", None, "dp"),
        P("expert", None, "dp"),
    )
    out_specs = (P("expert", "dp", None), P("expert", None))
    return jax.shard_map(
        on_device, mesh=mesh, in_specs=in_specs, out_specs=out_specs, check_vma=False
    )
```

profile of v0, /device:TPU:1, one launch (start us, length us, event | category | flops | bytes accessed | tf_op | source)
XLA Modules:
  0.0 414.3 jit_solution(8499630758901773175)
XLA Ops:
  10.4 1.4 convolution_convert_fusion.1
  11.8 1.5 all_to_all.32
  13.3 108.5 %all_to_all.42 = bf16[128,6,896]{2,1,0:T(8,128)(2,1)} all-to-all(bf16[128,6,896]{2,1,0:T(8,128)(2,1)} %all_to_all.32), channel_id=1, replica_groups=mesh['expert'=128,'dp'=4] {'expert'}, dimensions={0} | all-to-all | bytes 2752512 | tf_op jit(solution)/shard_map/all_to_all | solution.py:48
  121.8 3.6 all_to_all.34
  127.7 8.6 %all-to-all-start.1 = ((bf16[128,6,1]{1,2,0:T(2,128)(2,1)}), bf16[128,6,1]{1,2,0:T(2,128)(2,1)S(1)}, u32[]{:S(2)}, u32[]{:S(2)}) async-start(bf16[128,6,1]{1,2,0:T(2,128)(2,1)} %convert_element_type.91), calls=%async_computation.1 | async-start | bytes 131072 | tf_op jit(solution)/shard_map/all_to_all | solution.py:49
  136.3 1.5 convolution_convert_fusion.2
  137.8 1.5 all_to_all.28
  139.3 12.0 %all-to-all-done.1 = bf16[128,6,1]{1,2,0:T(2,128)(2,1)S(1)} async-done(((bf16[128,6,1]{1,2,0:T(2,128)(2,1)}), bf16[128,6,1]{1,2,0:T(2,128)(2,1)S(1)}, u32[]{:S(2)}, u32[]{:S(2)}) %all-to-all-start.1) | async-done | bytes 1568 | tf_op jit(solution)/shard_map/all_to_all | solution.py:49
  151.3 7.6 %all-to-all-start = ((bf16[128,6,896]{2,1,0:T(8,128)(2,1)}), bf16[128,6,896]{2,1,0:T(8,128)(2,1)}, u32[]{:S(2)}, u32[]{:S(2)}) async-start(bf16[128,6,896]{2,1,0:T(8,128)(2,1)} %all_to_all.28), calls=%async_computation | async-start | bytes 3670016 | tf_op jit(solution)/shard_map/all_to_all | solution.py:47
  159.8 26.1 %all-gather.4.cloned.1.call-done = bf16[768,3584]{1,0:T(8,128)(2,1)} async-done(((bf16[768,896]{1,0:T(8,128)(2,1)}), bf16[768,3584]{1,0:T(8,128)(2,1)}) %all-gather.4.cloned.1.call-update) | async-done | bytes 5505040 | tf_op jit(solution)/shard_map/all_gather | solution.py:52
  185.9 5.0 %fusion.9 = (f32[768]{0:T(1024)S(1)}, bf16[768,256]{0,1:T(8,128)(2,1)}) fusion(bf16[1,768,256]{1,2,0:T(8,128)(2,1)S(1)} %copy.35, bf16[1,768,256]{1,2,0:T(8,128)(2,1)S(1)} %copy.34, f32[768]{0:T(1024)S(1)} %reshape.97, bf16[768,3584]{1,0:T(8,128)(2,1)} %all-gather.4.cloned.1.call-done, bf16[1,256,3584]{2,1,0:T(8,128)(2,1)S(1)} %copy-done), kind=kOutput, calls=%fused_computation.25 | convolution fusion | flops 1411644672 | bytes 8525824 | tf_op jit(solution)/shard_map/dot_general | solution.py:51
  191.0 55.7 %all-to-all-done = bf16[128,6,896]{2,1,0:T(8,128)(2,1)} async-done(((bf16[128,6,896]{2,1,0:T(8,128)(2,1)}), bf16[128,6,896]{2,1,0:T(8,128)(2,1)}, u32[]{:S(2)}, u32[]{:S(2)}) %all-to-all-start) | async-done | bytes 1376288 | tf_op jit(solution)/shard_map/all_to_all | solution.py:47
  246.7 2.5 all_to_all.30
  249.2 5.5 %multiply_reduce_fusion = (f32[]{:T(128)}, f32[896,1024]{1,0:T(8,128)}) fusion(bf16[768,896]{1,0:T(8,128)(2,1)S(1)} %all_to_all.30, bf16[768,1024]{0,1:T(8,128)(2,1)} %all-gather.6.cloned.1.call-done), kind=kOutput, calls=%fused_computation.6 | convolution fusion | flops 1411121152 | bytes 6619140 | tf_op jit(solution)/shard_map/dot_general | solution.py:65
  254.7 9.3 %psum.28 = f32[]{:T(128)} all-reduce(f32[]{:T(128)} %get-tuple-element.15), channel_id=1, replica_groups=mesh['expert'=128,'dp'=4] {'dp'}, use_global_device_ids=true, to_apply=%region_4.5 | all-reduce | flops 1 | bytes 8 | tf_op jit(solution)/shard_map/psum | solution.py:72
  264.8 6.9 %convolution_convert_fusion = bf16[1024,1024]{1,0:T(8,128)(2,1)} fusion(f32[896,1024]{1,0:T(8,128)} %get-tuple-element.16, f32[]{:T(128)S(6)} %add.47), kind=kOutput, calls=%fused_computation.10 | convolution fusion | flops 1881931776 | bytes 5767172 | tf_op jit(solution)/shard_map/dot_general | solution.py:74
  271.9 67.3 %all-reduce.3.cloned.1.call-done = bf16[1024,1024]{1,0:T(8,128)(2,1)} async-done(((bf16[1024,1024]{1,0:T(8,128)(2,1)}), bf16[1024,1024]{1,0:T(8,128)(2,1)}) %all-reduce.3.cloned.1.call-update) | async-done | bytes 2097168 | tf_op jit(solution)/shard_map/psum | solution.py:77
  339.2 3.2 multiply_reduce_fusion.1
  342.3 13.1 %all-reduce = (f32[]{:T(128)}, f32[128,6,1]{1,0,2:T(8,128)}) all-reduce(f32[]{:T(128)} %get-tuple-element.17, f32[128,6,1]{1,0,2:T(8,128)S(1)} %all_to_all.35), channel_id=1, replica_groups=mesh['expert'=128,'dp'=4] {'dp'}, use_global_device_ids=true, to_apply=%region_7.8 | all-reduce | flops 769 | bytes 6152 | tf_op jit(solution)/shard_map/psum | solution.py:81
  356.2 2.0 add_convert_fusion
  358.5 20.4 %all-to-all-start.3 = ((f32[128,6,1]{1,2,0:T(1,128)}), f32[128,6,1]{1,2,0:T(1,128)S(1)}, u32[]{:S(2)}, u32[]{:S(2)}) async-start(f32[128,6,1]{1,2,0:T(1,128)} %bitcast.5), calls=%async_computation.3 | async-start | bytes 131072 | tf_op jit(solution)/shard_map/all_to_all | solution.py:25
  378.9 14.9 %all-to-all-done.3 = f32[128,6,1]{1,2,0:T(1,128)S(1)} async-done(((f32[128,6,1]{1,2,0:T(1,128)}), f32[128,6,1]{1,2,0:T(1,128)S(1)}, u32[]{:S(2)}, u32[]{:S(2)}) %all-to-all-start.3) | async-done | bytes 3104 | tf_op jit(solution)/shard_map/all_to_all | solution.py:25
  395.3 4.5 %gather_fusion = f32[1024]{0:T(1024)S(1)} fusion(f32[768]{0:T(1024)S(1)} %all_to_all.37, s32[1024]{0:T(1024)S(1)} %broadcast_clamp_fusion), kind=kCustom, calls=%fused_computation | custom fusion | bytes 12288 | tf_op jit(solution)/shard_map/gather | solution.py:96
  400.6 7.2 %fusion.2 = bf16[1,896,1024]{2,1,0:T(8,128)(2,1)} fusion(bf16[1024,1024]{1,0:T(8,128)(2,1)} %all-gather.8.cloned.1.call-done, f32[896,1024]{1,0:T(8,128)} %get-tuple-element.16, f32[]{:T(128)S(6)} %add.47), kind=kOutput, calls=%fused_computation.11 | convolution fusion | flops 1887305728 | bytes 7602180 | tf_op jit(solution)/shard_map/dot_general | solution.py:88
  (43 shorter events, 9.0 us)
Async XLA Ops:
  7.2 178.8 %copy-start = (bf16[1,256,3584]{2,1,0:T(8,128)(2,1)S(1)}, bf16[1,256,3584]{2,1,0:T(8,128)(2,1)}, u32[]{:S(2)}) copy-start(bf16[1,256,3584]{2,1,0:T(8,128)(2,1)} %param.11) | copy-start | bytes 5505028
  7.2 178.7 %all-gather.4.cloned.1.call-start = ((), (), s32[]{:S(2)}) async-start(), calls=%async_computation.4 | async-start | bytes 6881280 | tf_op jit(solution)/shard_map/all_gather | solution.py:52
  121.8 3.7 copy-start.3
  127.7 23.6 %all-to-all-start.1 = ((bf16[128,6,1]{1,2,0:T(2,128)(2,1)}), bf16[128,6,1]{1,2,0:T(2,128)(2,1)S(1)}, u32[]{:S(2)}, u32[]{:S(2)}) async-start(bf16[128,6,1]{1,2,0:T(2,128)(2,1)} %convert_element_type.91), calls=%async_computation.1 | async-start | bytes 131072 | tf_op jit(solution)/shard_map/all_to_all | solution.py:49
  139.3 19.9 %copy-start.1 = (bf16[1,768,256]{2,1,0:T(8,128)(2,1)S(1)}, bf16[1,768,256]{2,1,0:T(8,128)(2,1)}, u32[]{:S(2)}) copy-start(bf16[1,768,256]{2,1,0:T(8,128)(2,1)} %param.12) | copy-start | bytes 1179652
  139.3 20.0 %copy-start.2 = (bf16[1,768,256]{2,1,0:T(8,128)(2,1)S(1)}, bf16[1,768,256]{2,1,0:T(8,128)(2,1)}, u32[]{:S(2)}) copy-start(bf16[1,768,256]{2,1,0:T(8,128)(2,1)} %param.13) | copy-start | bytes 1179652
  151.3 95.4 %all-to-all-start = ((bf16[128,6,896]{2,1,0:T(8,128)(2,1)}), bf16[128,6,896]{2,1,0:T(8,128)(2,1)}, u32[]{:S(2)}, u32[]{:S(2)}) async-start(bf16[128,6,896]{2,1,0:T(8,128)(2,1)} %all_to_all.28), calls=%async_computation | async-start | bytes 3670016 | tf_op jit(solution)/shard_map/all_to_all | solution.py:47
  158.9 90.3 %all-gather.6.cloned.1.call-start = ((), (), s32[]{:S(2)}) async-start(), calls=%async_computation.5 | async-start | bytes 1966080 | tf_op jit(solution)/shard_map/all_gather | solution.py:67
  191.0 148.2 %all-reduce.3.cloned.1.call-start = ((), (), s32[]{:S(2)}) async-start(), calls=%async_computation.6 | async-start | bytes 4194304 | tf_op jit(solution)/shard_map/psum | solution.py:77
  271.7 128.9 %all-gather.8.cloned.1.call-start = ((), (), s32[]{:S(2)}) async-start(), calls=%async_computation.7 | async-start | bytes 2621440 | tf_op jit(solution)/shard_map/all_gather | solution.py:90
  358.5 35.3 %all-to-all-start.3 = ((f32[128,6,1]{1,2,0:T(1,128)}), f32[128,6,1]{1,2,0:T(1,128)S(1)}, u32[]{:S(2)}, u32[]{:S(2)}) async-start(f32[128,6,1]{1,2,0:T(1,128)} %bitcast.5), calls=%async_computation.3 | async-start | bytes 131072 | tf_op jit(solution)/shard_map/all_to_all | solution.py:25
Sparse Core Ops, SparseCore 0:
  125.5 60.3 all-gather.3
  191.1 34.8 all-gather.5
  271.8 67.3 all-reduce.2
  358.4 42.0 all-gather.7
where the time goes:
time: 415 us; the launch traced here: 414 us
  waiting for transfers between devices  176 us (42%)
  blocking collectives  131 us (32%)
  starting transfers between devices  36.9 us (9%)
  matrix products  30.7 us (7%)
  local copies, waits for them, and re-layouts  17.7 us (4%)
  between operations  15.5 us (4%)
  other arithmetic  6.44 us (2%)
    all_to_all x1, blocking collectives, on_device(): lax.all_to_all(grad_send, 'expert', split_axis=0, concat_axis=0, tiled=True)  108 us
    psum x1, waiting for transfers between devices, on_device(): gram = lax.psum(gram_part.astype(jnp.bfloat16), 'dp')  67.3 us
    all_to_all x1, waiting for transfers between devices, on_device(): lax.all_to_all(row_send, 'expert', split_axis=0, concat_axis=0, tiled=True)  55.7 us
    all_gather x1, waiting for transfers between devices, on_device(): lax.all_gather(grad_recv, 'dp', axis=1, tiled=True)  26.1 us
    all_to_all x1, starting transfers between devices, return_grad(): lax.all_to_all(values, 'expert', split_axis=0, concat_axis=0, tiled=True)  20.4 us
    all_to_all x1, waiting for transfers between devices, return_grad(): lax.all_to_all(values, 'expert', split_axis=0, concat_axis=0, tiled=True)  14.9 us
    psum x1, blocking collectives, on_device(): quartic = lax.psum(jnp.sum(square * square), 'dp')  13.1 us
    all_to_all x1, waiting for transfers between devices, on_device(): lax.all_to_all(weight_send, 'expert', split_axis=0, concat_axis=0, tiled=...  12 us
  transfers between devices with their start and end apart: 7, of which 5 were waited for; matrix products, arithmetic and copies ran while one was open for 4% of the time, Pallas kernels for 0%

commit v1 on v0

v1 whole, which is shorter than its diff:
```python
import math

import jax
import jax.numpy as jnp
from jax import lax
from jax.sharding import Mesh
from jax.sharding import PartitionSpec as P

D = 3584
CAP = 6
PLANE = (4, 16, 2)

poly_first = 8.28721201814563
poly_third = -23.595886519098837
poly_fifth = 17.300387312530933

f32, bf16 = jnp.float32, jnp.bfloat16


def dot(a, b, contract):
    return lax.dot_general(a, b, (contract, ((), ())), preferred_element_type=f32)


def block_positions(flat_ids):
    pair_count = flat_ids.shape[0]
    same_id = flat_ids[:, None] == flat_ids[None, :]
    earlier = jnp.arange(pair_count)[None, :] < jnp.arange(pair_count)[:, None]
    return jnp.sum(jnp.logical_and(same_id, earlier), axis=1)


def shift(values, step):
    size = lax.axis_size("y")
    return lax.ppermute(values, "y", [(i, (i + step) % size) for i in range(size)])


def gather_weights(own):
    size, rank = lax.axis_size("y"), lax.axis_index("y")
    half = own.shape[0] // 2
    before = shift(own, 1)
    after = shift(own, -1)
    far_low = shift(before[:half], 1)
    far_high = shift(after[half:], -1)
    whole = jnp.zeros((size,) + own.shape, own.dtype)
    parts = ((own, 0, 0), (before, -1, 0), (after, 1, 0), (far_low, 2, 0), (far_high, 2, half))
    for part, step, row in parts:
        place = lax.rem(rank + size + step, size)
        whole = lax.dynamic_update_slice(whole, part[None], (place, row, 0))
    return whole.reshape(size * own.shape[0], own.shape[1])


def on_device(tokens_in, out_grad, expert_ids, combine, down_weight, gate_saved, up_saved):
    nx, nz, nc = (lax.axis_size(name) for name in ("x", "z", "c"))
    ny = lax.axis_size("y")
    experts = nx * nz * nc
    near = nx * nc
    zl = nz // ny
    slots = experts * CAP
    own_slots = slots // ny
    tok_rows, top_count = expert_ids.shape
    feats = tokens_in.shape[1]
    hidden_part = gate_saved.shape[2]
    hidden_all = hidden_part * ny

    column = lax.all_gather(
        jnp.concatenate([tokens_in, out_grad], axis=1), "z", axis=0, tiled=True
    )
    matrix = gather_weights(down_weight[0])

    flat_ids = expert_ids.reshape(-1)
    position = block_positions(flat_ids)
    is_live = flat_ids < experts
    ez = (flat_ids // nc) % nz
    exc = (flat_ids // (nc * nz)) * nc + flat_ids % nc
    target = jnp.where(is_live, (ez * near + exc) * CAP + position, -1)
    matches = target[None, :] == jnp.arange(slots, dtype=jnp.int32)[:, None]
    token_of = (jnp.arange(tok_rows * top_count, dtype=jnp.int32) // top_count).astype(f32) + 1.0
    index_send = jnp.sum(jnp.where(matches, token_of[None, :], 0.0), axis=1)
    weight_send = jnp.sum(
        jnp.where(matches, combine.astype(f32).reshape(1, -1), 0.0), axis=1
    )
    routes = lax.all_to_all(
        jnp.stack([index_send.reshape(nz, near * CAP), weight_send.reshape(nz, near * CAP)], 1),
        "z", 0, 0, tiled=True,
    )
    routes = routes.reshape(nz, 2, near, CAP)
    start = (jnp.arange(nz, dtype=jnp.int32) * tok_rows).astype(f32)[:, None, None]
    index = jnp.where(routes[:, 0] > 0.0, routes[:, 0] + start, 0.0)
    split = index.reshape(ny, zl, near, CAP)
    index_tok = index.transpose(1, 0, 2).reshape(-1)
    index_grad = split.transpose(0, 2, 1, 3).reshape(-1)
    columns = (jnp.arange(nz * tok_rows, dtype=jnp.int32) + 1).astype(f32)
    select_tok = (index_tok[:, None] == columns[None, :]).astype(bf16)
    select_grad = (index_grad[:, None] == columns[None, :]).astype(bf16)
    weight_order = routes[:, 1].reshape(ny, zl, near, CAP).transpose(0, 2, 1, 3)
    weight = lax.all_to_all(
        weight_order.reshape(ny * near, zl * CAP), ("y", "x", "c"), 0, 0, tiled=True
    )
    weight = weight.reshape(ny, own_slots)[0]

    row = jnp.arange(slots, dtype=jnp.int32)
    rest = row // CAP
    block = rest % zl
    rest = rest // zl
    row_c = rest % nc
    rest = rest // nc
    row_x = rest % nx
    row_q = rest // nx
    source = ((row_x * nz + row_q * zl + block) * nc + row_c) * CAP + row % CAP
    order = (source[:, None] == row[None, :]).astype(bf16)
    saved = jnp.concatenate([gate_saved[0], up_saved[0]], axis=1)
    saved = dot(order, saved, ((1,), (0,))).astype(bf16)
    saved = lax.all_to_all(
        saved.reshape(ny, own_slots, 2 * hidden_part), "y", 0, 0, tiled=True
    )
    gate = saved[:, :, :hidden_part].transpose(1, 0, 2).reshape(own_slots, hidden_all)
    up = saved[:, :, hidden_part:].transpose(1, 0, 2).reshape(own_slots, hidden_all)
    gate_act = jax.nn.silu(gate.astype(f32))
    hidden_act = gate_act * up.astype(f32)

    rows = dot(select_tok, column[:, :feats], ((1,), (0,))).astype(bf16)
    rows = lax.all_to_all(
        rows.reshape(near, nz * CAP, feats), ("x", "c"), 0, 0, tiled=True
    )
    rows = rows.reshape(near, ny, zl * CAP, feats).transpose(1, 0, 2, 3).reshape(slots, feats)
    inner = lax.psum(dot(rows, rows, ((1,), (1,))).astype(bf16), "y")

    grads = dot(select_grad, column[:, feats:], ((1,), (0,))).astype(bf16)
    grads = lax.all_to_all(
        grads.reshape(ny * near, zl * CAP, feats), ("y", "x", "c"), 0, 0, tiled=True
    )
    grads = grads.reshape(ny, own_slots, feats).transpose(1, 0, 2).reshape(own_slots, ny * feats)
    hidden_grad = dot(grads, matrix, ((1,), (1,)))
    slot_dw = jnp.sum(hidden_grad * hidden_act, axis=1)
    up_own = (weight[:, None] * hidden_grad * gate_act).astype(bf16)
    up_grad = lax.all_to_all(
        jnp.broadcast_to(up_own[None], (ny, own_slots, hidden_all)), "y", 0, 0, tiled=True
    ).reshape(slots, hidden_all)

    back = jnp.broadcast_to(slot_dw.reshape(1, near, zl * CAP), (ny, near, zl * CAP))
    back = lax.all_to_all(
        back.reshape(ny * near, zl * CAP), ("y", "x", "c"), 0, 0, tiled=True
    )
    back = back.reshape(ny, near, zl, CAP).transpose(0, 2, 1, 3).reshape(nz, near * CAP)
    back = lax.all_to_all(back, "z", 0, 0, tiled=True).reshape(-1)
    dcombine = jnp.sum(jnp.where(matches, back[:, None], 0.0), axis=0)
    dcombine = dcombine.reshape(tok_rows, top_count)

    gradient = dot(rows, up_grad, ((0,), (0,)))
    carried = dot(inner, up_grad, ((1,), (0,)))
    norm_total = jnp.sum(carried * up_grad.astype(f32))
    scale = 1.0 / (1.01 * jnp.sqrt(jnp.maximum(norm_total, 0.0)) + 1e-07)
    gram = dot(up_grad, carried.astype(bf16), ((0,), (0,)))
    gram_low = (gram * scale * scale).astype(bf16)
    start_iter = (gradient * scale).astype(bf16)
    square = dot(gram_low, gram_low, ((1,), (0,)))
    quartic = jnp.sum(square * square)
    bound = jnp.sqrt(jnp.sqrt(quartic)) + 1e-06
    first_scale = poly_third / bound
    second_scale = poly_fifth / (bound * bound)
    poly = (first_scale * gram_low.astype(f32) + second_scale * square).astype(bf16)
    mixed = dot(start_iter, poly, ((1,), (0,)))
    update = (math.sqrt(D) * (poly_first * start_iter.astype(f32) + mixed)).astype(bf16)
    return (update[None], dcombine)


def build(mesh, plane):
    split_mesh = Mesh(
        mesh.devices.reshape(plane + (mesh.devices.shape[1],)), ("x", "z", "c", "y")
    )
    expert = ("x", "z", "c")
    in_specs = (
        P(expert, "y"),
        P(expert, "y"),
        P(expert, None),
        P(expert, None),
        P(expert, "y", None),
        P(expert, None, "y"),
        P(expert, None, "y"),
    )
    out_specs = (P(expert, "y", None), P(expert, None))
    return jax.shard_map(
        on_device, mesh=split_mesh, in_specs=in_specs, out_specs=out_specs, check_vma=False
    )


def solution(mesh):
    return build(mesh, PLANE)
```

time: 415 us -> 288 us (0.69)
  blocking collectives: 131 us -> 0 us
  waiting for transfers between devices: 176 us -> 123 us
  starting transfers between devices: 36.9 us -> 70.5 us
  matrix products: 30.7 us -> 45.4 us
  local copies, waits for them, and re-layouts: 17.7 us -> 27.2 us
    all_to_all x1 -> x0, blocking collectives: 108 us -> none  [on_device(): lax.all_to_all(grad_send, 'expert', split_axis=0, concat_axis=0, tiled=True)]
    all_to_all x3 -> x8, waiting for transfers between devices: 82.7 us -> 56.4 us  [the longest x1 11.1 us: on_device(): lax.all_to_all(grads.reshape(ny * near, zl * CAP, feats), ('y', 'x', 'c')...]
    psum x2 -> x0, blocking collectives: 22.5 us -> none  [the longest x1 13.1 us: on_device(): quartic = lax.psum(jnp.sum(square * square), 'dp')]
    all_to_all x3 -> x8, starting transfers between devices: 36.6 us -> 56.6 us  [the longest x1 14.9 us: on_device(): lax.all_to_all(jnp.stack([index_send.reshape(nz, near * CAP), weight_send...]
    psum x1, waiting for transfers between devices: 67.3 us -> 47.7 us  [on_device(): inner = lax.psum(dot(rows, rows, ((1,), (1,))).astype(bf16), 'y')]
    dot_general x7 -> x10, matrix products: 30.7 us -> 45.4 us  [dot(): lax.dot_general(a, b, (contract, ((), ())), preferred_element_type=f32)]
    ppermute x0 -> x4, starting transfers between devices: none -> 13.9 us  [shift(): lax.ppermute(values, 'y', [(i, (i + step) % size) for i in range(size)])]
    dynamic_update_slice x0 -> x5, local copies, waits for them, and re-layouts: none -> 10.1 us  [gather_weights(): whole = lax.dynamic_update_slice(whole, part[None], (place, row, 0))]
  transfers between devices with their start and end apart: 7 -> 14, of which waited for: 5 -> 9; matrix products, arithmetic and copies ran while one was open for 4% -> 19% of each run, Pallas kernels for 0% -> 0%
where the time goes in v1:
time: 288 us; the launch traced here: 286 us
  waiting for transfers between devices  123 us (43%)
  starting transfers between devices  70.5 us (24%)
  matrix products  45.4 us (16%)
  local copies, waits for them, and re-layouts  27.2 us (9%)
  between operations  15.9 us (6%)
  other arithmetic  4.75 us (2%)
    psum x1, waiting for transfers between devices, on_device(): inner = lax.psum(dot(rows, rows, ((1,), (1,))).astype(bf16), 'y')  47.7 us
    dot_general x10, matrix products, dot(): lax.dot_general(a, b, (contract, ((), ())), preferred_element_type=f32)  45.4 us
    all_gather x1, waiting for transfers between devices, on_device(): lax.all_gather(jnp.concatenate([tokens_in, out_grad], axis=1), 'z', axis=...  18.5 us
    all_to_all x1, starting transfers between devices, on_device(): lax.all_to_all(jnp.stack([index_send.reshape(nz, near * CAP), weight_send...  14.9 us
    ppermute x4, starting transfers between devices, shift(): lax.ppermute(values, 'y', [(i, (i + step) % size) for i in range(size)])  13.9 us
    all_to_all x1, waiting for transfers between devices, on_device(): lax.all_to_all(grads.reshape(ny * near, zl * CAP, feats), ('y', 'x', 'c')...  11.1 us
    dynamic_update_slice x5, local copies, waits for them, and re-layouts, gather_weights(): whole = lax.dynamic_update_slice(whole, part[None], (place, row, 0))  10.1 us
    all_to_all x1, waiting for transfers between devices, on_device(): lax.all_to_all(rows.reshape(near, nz * CAP, feats), ('x', 'c'), 0, 0, til...  9.64 us
  transfers between devices with their start and end apart: 14, of which 9 were waited for; matrix products, arithmetic and copies ran while one was open for 19% of the time, Pallas kernels for 0%

profile of v1, /device:TPU:1, one launch (start us, length us, event | category | flops | bytes accessed | tf_op | source)
XLA Modules:
  0.0 286.4 jit_solution(14271669290937720116)
XLA Ops:
  9.1 4.0 %collective-permute-start = (bf16[256,3584]{1,0:T(8,128)(2,1)}, bf16[256,3584]{1,0:T(8,128)(2,1)S(1)}, u32[]{:S(2)}, u32[]{:S(2)}) collective-permute-start(bf16[256,3584]{1,0:T(8,128)(2,1)} %bitcast.78), channel_id=1, source_target_pairs={{0,1},{1,2},{2,3},{3,0},{4,5},{5,6},{6,7},{7,4},{8,9},{9,10},{10,1... | collective-permute-start | bytes 5505032 | tf_op jit(solution)/shard_map/ppermute | solution.py:33
  20.6 14.9 %all-to-all-start = ((f32[16,2,48]{2,1,0:T(2,128)}), f32[16,2,48]{2,1,0:T(2,128)S(1)}, u32[]{:S(2)}, u32[]{:S(2)}) async-start(f32[16,2,48]{2,1,0:T(2,128)} %copy.57), calls=%async_computation | async-start | bytes 32768 | tf_op jit(solution)/shard_map/all_to_all | solution.py:81
  38.4 3.6 %broadcast_in_dim.85 = bf16[4,256,3584]{2,1,0:T(8,128)(2,1)} broadcast(bf16[]{:T(256)} %constant.167.clone.1), dimensions={} | broadcast | bytes 7340034 | tf_op jit(solution)/shard_map/broadcast_in_dim | solution.py:43
  43.3 3.6 %all-to-all-done = f32[16,2,48]{2,1,0:T(2,128)S(1)} async-done(((f32[16,2,48]{2,1,0:T(2,128)}), f32[16,2,48]{2,1,0:T(2,128)S(1)}, u32[]{:S(2)}, u32[]{:S(2)}) %all-to-all-start) | async-done | bytes 6176 | tf_op jit(solution)/shard_map/all_to_all | solution.py:81
  48.0 8.6 %all-to-all-start.2 = ((f32[32,1,24]{2,1,0:T(1,128)}), f32[32,1,24]{2,1,0:T(1,128)S(1)}, u32[]{:S(2)}, u32[]{:S(2)}) async-start(f32[32,1,24]{2,1,0:T(1,128)} %reshape.310), calls=%async_computation.2 | async-start | bytes 32768 | tf_op jit(solution)/shard_map/all_to_all | solution.py:95
  56.6 6.9 %all-to-all-done.2 = f32[32,1,24]{2,1,0:T(1,128)S(1)} async-done(((f32[32,1,24]{2,1,0:T(1,128)}), f32[32,1,24]{2,1,0:T(1,128)S(1)}, u32[]{:S(2)}, u32[]{:S(2)}) %all-to-all-start.2) | async-done | bytes 3104 | tf_op jit(solution)/shard_map/all_to_all | solution.py:95
  69.1 9.6 %all-to-all-done.4 = bf16[4,192,512]{2,1,0:T(8,128)(2,1)S(1)} async-done(((bf16[4,192,512]{2,1,0:T(8,128)(2,1)}), bf16[4,192,512]{2,1,0:T(8,128)(2,1)S(1)}, u32[]{:S(2)}, u32[]{:S(2)}) %all-to-all-start.4) | async-done | bytes 786464 | tf_op jit(solution)/shard_map/all_to_all | solution.py:112
  84.5 4.2 %collective-permute-start.3 = (bf16[128,3584]{1,0:T(8,128)(2,1)}, bf16[128,3584]{1,0:T(8,128)(2,1)}, u32[]{:S(2)}, u32[]{:S(2)}) collective-permute-start(bf16[128,3584]{1,0:T(8,128)(2,1)} %slice.45), channel_id=1, source_target_pairs={{0,3},{1,0},{2,1},{3,2},{4,7},{5,4},{6,5},{7,6},{8,11},{9,8},{10,9... | collective-permute-start | bytes 2752520 | tf_op jit(solution)/shard_map/ppermute | solution.py:33
  93.0 18.5 %all-gather.2.cloned.1.call-done = bf16[2048,1792]{1,0:T(8,128)(2,1)} async-done(((bf16[128,1792]{1,0:T(8,128)(2,1)}), bf16[2048,1792]{1,0:T(8,128)(2,1)}) %all-gather.2.cloned.1.call-update) | async-done | bytes 7340048 | tf_op jit(solution)/shard_map/all_gather | solution.py:64
  111.5 6.7 %fusion.20 = bf16[768,896]{1,0:T(8,128)(2,1)} fusion(bf16[2048,1792]{1,0:T(8,128)(2,1)} %all-gather.2.cloned.1.call-done, f32[2048]{0:T(1024)S(1)} %add_convert_fusion.6, f32[768]{0:T(1024)S(1)} %copy-done.3), kind=kOutput, calls=%fused_computation.31 | convolution fusion | flops 2820833280 | bytes 5057536 | tf_op jit(solution)/shard_map/dot_general | solution.py:21
  118.2 7.5 %all-to-all-start.3 = ((bf16[32,24,896]{2,1,0:T(8,128)(2,1)}), bf16[32,24,896]{2,1,0:T(8,128)(2,1)S(1)}, u32[]{:S(2)}, u32[]{:S(2)}) async-start(bf16[32,24,896]{2,1,0:T(8,128)(2,1)} %bitcast.11), calls=%async_computation.3 | async-start | bytes 2752512 | tf_op jit(solution)/shard_map/all_to_all | solution.py:128
  127.9 6.6 %fusion.15 = bf16[768,896]{1,0:T(8,128)(2,1)} fusion(bf16[2048,1792]{1,0:T(8,128)(2,1)} %all-gather.2.cloned.1.call-done, f32[2048]{0:T(1024)S(1)} %add_convert_fusion.6, f32[768]{0:T(1024)S(1)} %eq.83), kind=kOutput, calls=%fused_computation.30 | convolution fusion | flops 2820833280 | bytes 5057536 | tf_op jit(solution)/shard_map/dot_general | solution.py:21
  134.5 11.1 %all-to-all-done.3 = bf16[32,24,896]{2,1,0:T(8,128)(2,1)S(1)} async-done(((bf16[32,24,896]{2,1,0:T(8,128)(2,1)}), bf16[32,24,896]{2,1,0:T(8,128)(2,1)S(1)}, u32[]{:S(2)}, u32[]{:S(2)}) %all-to-all-start.3) | async-done | bytes 1376288 | tf_op jit(solution)/shard_map/all_to_all | solution.py:128
  145.6 5.4 %all-to-all-start.1 = ((bf16[8,96,896]{2,1,0:T(8,128)(2,1)}), bf16[8,96,896]{2,1,0:T(8,128)(2,1)S(1)}, u32[]{:S(2)}, u32[]{:S(2)}) async-start(bf16[8,96,896]{2,1,0:T(8,128)(2,1)} %bitcast.85), calls=%async_computation.1 | async-start | bytes 2752512 | tf_op jit(solution)/shard_map/all_to_all | solution.py:121
  153.4 6.5 %multiply_reduce_fusion.2 = (f32[192]{0:T(256)S(1)}, bf16[192,1024]{1,0:T(8,128)(2,1)}) fusion(f32[192,1024]{1,0:T(8,128)S(1)} %bitcast.88, f32[192,1024]{1,0:T(8,128)S(1)} %bitcast.87, f32[192]{0:T(256)S(1)} %copy-done.4, bf16[192,3584]{1,0:T(8,128)(2,1)S(1)} %bitcast.86, bf16[1024,3584]{1,0:T(8,128)(2,1)} %bitcast.19), kind=kOutput, calls=%fused_computation.44 | convolution fusion | flops 1411251968 | bytes 10683904 | tf_op jit(solution)/shard_map/dot_general | solution.py:21
  160.0 9.6 %all-to-all-done.1 = bf16[8,96,896]{2,1,0:T(8,128)(2,1)S(1)} async-done(((bf16[8,96,896]{2,1,0:T(8,128)(2,1)}), bf16[8,96,896]{2,1,0:T(8,128)(2,1)S(1)}, u32[]{:S(2)}, u32[]{:S(2)}) %all-to-all-start.1) | async-done | bytes 1376288 | tf_op jit(solution)/shard_map/all_to_all | solution.py:121
  170.3 4.5 %all-to-all-start.6 = ((f32[32,1,24]{2,1,0:T(1,128)}), f32[32,1,24]{2,1,0:T(1,128)S(1)}, u32[]{:S(2)}, u32[]{:S(2)}) async-start(f32[32,1,24]{2,1,0:T(1,128)} %bitcast.28), calls=%async_computation.6 | async-start | bytes 32768 | tf_op jit(solution)/shard_map/all_to_all | solution.py:140
  174.9 6.8 %all-to-all-done.6 = f32[32,1,24]{2,1,0:T(1,128)S(1)} async-done(((f32[32,1,24]{2,1,0:T(1,128)}), f32[32,1,24]{2,1,0:T(1,128)S(1)}, u32[]{:S(2)}, u32[]{:S(2)}) %all-to-all-start.6) | async-done | bytes 3104 | tf_op jit(solution)/shard_map/all_to_all | solution.py:140
  182.8 8.6 %all-to-all-start.7 = ((f32[16,1,48]{2,1,0:T(1,128)}), f32[16,1,48]{2,1,0:T(1,128)S(1)}, u32[]{:S(2)}, u32[]{:S(2)}) async-start(f32[16,1,48]{2,1,0:T(1,128)} %bitcast.30), calls=%async_computation.7 | async-start | bytes 16384 | tf_op jit(solution)/shard_map/all_to_all | solution.py:144
  193.9 8.7 %all-to-all-done.7 = f32[16,1,48]{2,1,0:T(1,128)S(1)} async-done(((f32[16,1,48]{2,1,0:T(1,128)}), f32[16,1,48]{2,1,0:T(1,128)S(1)}, u32[]{:S(2)}, u32[]{:S(2)}) %all-to-all-start.7) | async-done | bytes 3104 | tf_op jit(solution)/shard_map/all_to_all | solution.py:144
  210.0 47.7 %all-reduce.2.cloned.1.call-done = bf16[768,768]{1,0:T(8,128)(2,1)} async-done(((bf16[768,768]{1,0:T(8,128)(2,1)}), bf16[768,768]{1,0:T(8,128)(2,1)}) %all-reduce.2.cloned.1.call-update) | async-done | bytes 1179664 | tf_op jit(solution)/shard_map/psum | solution.py:125
  257.7 4.4 %multiply_reduce_fusion.1 = (f32[]{:T(128)}, bf16[768,1024]{1,0:T(8,128)(2,1)}) fusion(bf16[4,192,1024]{2,1,0:T(8,128)(2,1)S(1)} %all-to-all-done.5, bf16[768,768]{1,0:T(8,128)(2,1)} %all-reduce.2.cloned.1.call-done, bf16[768,1024]{1,0:T(8,128)(2,1)S(1)} %bitcast.80), kind=kOutput, calls=%fused_computation.15 | convolution fusion | flops 1211105280 | bytes 5898244 | tf_op jit(solution)/shard_map/dot_general | solution.py:21
  267.6 4.9 %multiply_reduce_fusion = (f32[]{:T(128)}, f32[1024,1024]{1,0:T(8,128)}) fusion(bf16[1024,1024]{1,0:T(8,128)(2,1)S(1)} %multiply_convert_fusion), kind=kOutput, calls=%fused_computation.5 | convolution fusion | flops 2149580800 | bytes 6291460 | tf_op jit(solution)/shard_map/dot_general | solution.py:21
  273.3 6.3 %fusion.26 = bf16[1,896,1024]{2,1,0:T(8,128)(2,1)} fusion(bf16[896,1024]{1,0:T(8,128)(2,1)S(1)} %copy-done.7, f32[1024,1024]{1,0:T(8,128)} %get-tuple-element.21, bf16[1024,1024]{1,0:T(8,128)(2,1)} %copy-done.6, f32[]{:T(128)S(6)} %div.98, f32[]{:T(128)S(6)} %div.97), kind=kOutput, calls=%fused_computation.33 | convolution fusion | flops 1888878592 | bytes 9961480 | tf_op jit(solution)/shard_map/dot_general | solution.py:21
  (89 shorter events, 51.2 us)
Async XLA Ops:
  7.2 104.4 %all-gather.2.cloned.1.call-start = ((), (), s32[]{:S(2)}) async-start(), calls=%async_computation.8 | async-start | bytes 7798784 | tf_op jit(solution)/shard_map/all_gather | solution.py:64
  9.1 70.9 %collective-permute-start = (bf16[256,3584]{1,0:T(8,128)(2,1)}, bf16[256,3584]{1,0:T(8,128)(2,1)S(1)}, u32[]{:S(2)}, u32[]{:S(2)}) collective-permute-start(bf16[256,3584]{1,0:T(8,128)(2,1)} %bitcast.78), channel_id=1, source_target_pairs={{0,1},{1,2},{2,3},{3,0},{4,5},{5,6},{6,7},{7,4},{8,9},{9,10},{10,1... | collective-permute-start | bytes 5505032 | tf_op jit(solution)/shard_map/ppermute | solution.py:33
  13.1 69.2 %collective-permute-start.1 = (bf16[256,3584]{1,0:T(8,128)(2,1)}, bf16[256,3584]{1,0:T(8,128)(2,1)}, u32[]{:S(2)}, u32[]{:S(2)}) collective-permute-start(bf16[256,3584]{1,0:T(8,128)(2,1)} %bitcast.79), channel_id=1, source_target_pairs={{0,3},{1,0},{2,1},{3,2},{4,7},{5,4},{6,5},{7,6},{8,11},{9,8},{10,9... | collective-permute-start | bytes 5505032 | tf_op jit(solution)/shard_map/ppermute | solution.py:33
  20.6 26.4 %all-to-all-start = ((f32[16,2,48]{2,1,0:T(2,128)}), f32[16,2,48]{2,1,0:T(2,128)S(1)}, u32[]{:S(2)}, u32[]{:S(2)}) async-start(f32[16,2,48]{2,1,0:T(2,128)} %copy.57), calls=%async_computation | async-start | bytes 32768 | tf_op jit(solution)/shard_map/all_to_all | solution.py:81
  38.4 3.6 %copy-start = (bf16[1,256,3584]{2,1,0:T(8,128)(2,1)S(1)}, bf16[1,256,3584]{2,1,0:T(8,128)(2,1)}, u32[]{:S(2)}) copy-start(bf16[1,256,3584]{2,1,0:T(8,128)(2,1)} %param.11) | copy-start | bytes 5505028
  48.0 15.5 %all-to-all-start.2 = ((f32[32,1,24]{2,1,0:T(1,128)}), f32[32,1,24]{2,1,0:T(1,128)S(1)}, u32[]{:S(2)}, u32[]{:S(2)}) async-start(f32[32,1,24]{2,1,0:T(1,128)} %reshape.310), calls=%async_computation.2 | async-start | bytes 32768 | tf_op jit(solution)/shard_map/all_to_all | solution.py:95
  63.6 15.2 %all-to-all-start.4 = ((bf16[4,192,512]{2,1,0:T(8,128)(2,1)}), bf16[4,192,512]{2,1,0:T(8,128)(2,1)S(1)}, u32[]{:S(2)}, u32[]{:S(2)}) async-start(bf16[4,192,512]{2,1,0:T(8,128)(2,1)} %bitcast.22), calls=%async_computation.4 | async-start | bytes 1572864 | tf_op jit(solution)/shard_map/all_to_all | solution.py:112
  80.0 45.7 %collective-permute-start.2 = (bf16[128,3584]{1,0:T(8,128)(2,1)S(1)}, bf16[128,3584]{1,0:T(8,128)(2,1)}, u32[]{:S(2)}, u32[]{:S(2)}) collective-permute-start(bf16[128,3584]{1,0:T(8,128)(2,1)S(1)} %slice.44), channel_id=1, source_target_pairs={{0,1},{1,2},{2,3},{3,0},{4,5},{5,6},{6,7},{7,4},{8,9},{9,10},{10,1... | collective-permute-start | bytes 2752520 | tf_op jit(solution)/shard_map/ppermute | solution.py:33
  84.5 66.5 %collective-permute-start.3 = (bf16[128,3584]{1,0:T(8,128)(2,1)}, bf16[128,3584]{1,0:T(8,128)(2,1)}, u32[]{:S(2)}, u32[]{:S(2)}) collective-permute-start(bf16[128,3584]{1,0:T(8,128)(2,1)} %slice.45), channel_id=1, source_target_pairs={{0,3},{1,0},{2,1},{3,2},{4,7},{5,4},{6,5},{7,6},{8,11},{9,8},{10,9... | collective-permute-start | bytes 2752520 | tf_op jit(solution)/shard_map/ppermute | solution.py:33
  90.1 21.4 %copy-start.3 = (f32[768]{0:T(1024)S(1)}, f32[768]{0:T(1024)}, u32[]{:S(2)}) copy-start(f32[768]{0:T(1024)} %eq.87) | copy-start | bytes 9220
  118.2 27.4 %all-to-all-start.3 = ((bf16[32,24,896]{2,1,0:T(8,128)(2,1)}), bf16[32,24,896]{2,1,0:T(8,128)(2,1)S(1)}, u32[]{:S(2)}, u32[]{:S(2)}) async-start(bf16[32,24,896]{2,1,0:T(8,128)(2,1)} %bitcast.11), calls=%async_computation.3 | async-start | bytes 2752512 | tf_op jit(solution)/shard_map/all_to_all | solution.py:128
  145.6 24.0 %all-to-all-start.1 = ((bf16[8,96,896]{2,1,0:T(8,128)(2,1)}), bf16[8,96,896]{2,1,0:T(8,128)(2,1)S(1)}, u32[]{:S(2)}, u32[]{:S(2)}) async-start(bf16[8,96,896]{2,1,0:T(8,128)(2,1)} %bitcast.85), calls=%async_computation.1 | async-start | bytes 2752512 | tf_op jit(solution)/shard_map/all_to_all | solution.py:121
  151.0 2.4 copy-start.1
  151.0 2.4 copy-start.4
  170.3 11.5 %all-to-all-start.6 = ((f32[32,1,24]{2,1,0:T(1,128)}), f32[32,1,24]{2,1,0:T(1,128)S(1)}, u32[]{:S(2)}, u32[]{:S(2)}) async-start(f32[32,1,24]{2,1,0:T(1,128)} %bitcast.28), calls=%async_computation.6 | async-start | bytes 32768 | tf_op jit(solution)/shard_map/all_to_all | solution.py:140
  182.8 19.8 %all-to-all-start.7 = ((f32[16,1,48]{2,1,0:T(1,128)}), f32[16,1,48]{2,1,0:T(1,128)S(1)}, u32[]{:S(2)}, u32[]{:S(2)}) async-start(f32[16,1,48]{2,1,0:T(1,128)} %bitcast.30), calls=%async_computation.7 | async-start | bytes 16384 | tf_op jit(solution)/shard_map/all_to_all | solution.py:144
  191.4 66.3 %all-reduce.2.cloned.1.call-start = ((), (), s32[]{:S(2)}) async-start(), calls=%async_computation.9 | async-start | bytes 2359296 | tf_op jit(solution)/shard_map/psum | solution.py:125
  191.4 11.2 %copy-start.2 = (bf16[192,1024]{1,0:T(8,128)(2,1)S(1)}, bf16[192,1024]{1,0:T(8,128)(2,1)}, u32[]{:S(2)}) copy-start(bf16[192,1024]{1,0:T(8,128)(2,1)} %get-tuple-element.13) | copy-start | bytes 1179652
  204.0 53.7 %all-to-all-start.5 = ((bf16[4,192,1024]{2,1,0:T(8,128)(2,1)}), bf16[4,192,1024]{2,1,0:T(8,128)(2,1)S(1)}, u32[]{:S(2)}, u32[]{:S(2)}) async-start(bf16[4,192,1024]{2,1,0:T(8,128)(2,1)} %broadcast_in_dim.90), calls=%async_computation.5 | async-start | bytes 3145728 | tf_op jit(solution)/shard_map/all_to_all | solution.py:135
  262.8 2.9 %copy-start.5 = (bf16[768,1024]{1,0:T(8,128)(2,1)S(1)}, bf16[768,1024]{1,0:T(8,128)(2,1)}, u32[]{:S(2)}) copy-start(bf16[768,1024]{1,0:T(8,128)(2,1)} %get-tuple-element.19) | copy-start | bytes 4718596
  267.6 4.9 %copy-start.6 = (bf16[1024,1024]{1,0:T(8,128)(2,1)}, bf16[1024,1024]{1,0:T(8,128)(2,1)S(1)}, u32[]{:S(2)}) copy-start(bf16[1024,1024]{1,0:T(8,128)(2,1)S(1)} %multiply_convert_fusion) | copy-start | bytes 6291460
  267.6 5.7 %copy-start.7 = (bf16[896,1024]{1,0:T(8,128)(2,1)S(1)}, bf16[896,1024]{1,0:T(8,128)(2,1)}, u32[]{:S(2)}) copy-start(bf16[896,1024]{1,0:T(8,128)(2,1)} %multiply_convert_fusion.2) | copy-start | bytes 5505028
Sparse Core Ops, SparseCore 0:
  10.1 101.4 all-gather.1
  194.6 63.0 all-reduce.1

commit v2 on v1

--- a/solution.py
+++ b/solution.py
@@ -3,6 +3,8 @@
 import jax
 import jax.numpy as jnp
 from jax import lax
+from jax.experimental import pallas as pl
+from jax.experimental.pallas import tpu as pltpu
 from jax.sharding import Mesh
 from jax.sharding import PartitionSpec as P
 
@@ -15,6 +17,7 @@
 poly_fifth = 17.300387312530933
 
 f32, bf16 = jnp.float32, jnp.bfloat16
+VMEM = 48 * 1024 * 1024
 
 
 def dot(a, b, contract):
@@ -45,7 +48,211 @@
     for part, step, row in parts:
         place = lax.rem(rank + size + step, size)
         whole = lax.dynamic_update_slice(whole, part[None], (place, row, 0))
-    return whole.reshape(size * own.shape[0], own.shape[1])
+    return whole
+
+
+def total(values):
+    return jnp.sum(jnp.sum(values, axis=0, keepdims=True), axis=1, keepdims=True)
+
+
+def swap(values, partner):
+    size = lax.axis_size("y")
+    return lax.ppermute(values, "y", [(i, partner(i)) for i in range(size)])
+
+
+def pick_kernel(index_ref, column_ref, tok_ref, grad_ref):
+    near, _, rows, feats = tok_ref.shape
+    count = column_ref.shape[1]
+    columns = lax.broadcasted_iota(jnp.int32, (near * rows, count), 1).astype(f32) + 1.0
+    chosen = jnp.where(index_ref[0] == columns, 1.0, 0.0).astype(bf16)
+    for part, out in ((0, tok_ref), (1, grad_ref)):
+        values = column_ref[0, :, part * feats : (part + 1) * feats]
+        picked = dot(chosen, values, ((1,), (0,))).reshape(near, rows, feats).astype(bf16)
+        if part:
+            out[0] = picked
+        else:
+            out[:, 0] = picked
+
+
+def pick_rows(index, column, near):
+    quarters, rows, _ = index.shape
+    feats = column.shape[2] // 2
+    piece = rows // near
+    return pl.pallas_call(
+        pick_kernel,
+        grid=(quarters,),
+        in_specs=[
+            pl.BlockSpec((1, rows, 1), lambda q: (q, 0, 0)),
+            pl.BlockSpec((1,) + column.shape[1:], lambda q: (q, 0, 0)),
+        ],
+        out_specs=[
+            pl.BlockSpec((near, 1, piece, feats), lambda q: (0, q, 0, 0)),
+            pl.BlockSpec((1, near, piece, feats), lambda q: (q, 0, 0, 0)),
+        ],
+        out_shape=[
+            jax.ShapeDtypeStruct((near, quarters, piece, feats), bf16),
+            jax.ShapeDtypeStruct((quarters, near, piece, feats), bf16),
+        ],
+        compiler_params=pltpu.CompilerParams(vmem_limit_bytes=VMEM),
+        name="pick_rows",
+    )(index, column)
+
+
+def inner_kernel(recv_ref, rows_t_ref, low_ref, high_ref, rows_ref):
+    near, quarters, piece, feats = recv_ref.shape
+    own = near * piece
+    for q in range(quarters):
+        rows_ref[q * own : (q + 1) * own] = (
+            recv_ref[:, q].astype(f32).reshape(own, feats).astype(bf16)
+        )
+    half = quarters * own // 2
+    top, end = rows_ref[:half], rows_ref[half:]
+    low_ref[:half] = dot(top, top, ((1,), (1,))).astype(bf16)
+    cross = dot(top, end, ((1,), (1,))).astype(bf16)
+    low_ref[half:] = cross[: half // 2]
+    high_ref[: half // 2] = cross[half // 2 :]
+    high_ref[half // 2 :] = dot(end, end, ((1,), (1,))).astype(bf16)
+    rows_t_ref[...] = rows_ref[...].T
+
+
+def inner_products(recv):
+    near, quarters, piece, feats = recv.shape
+    slots = near * quarters * piece
+    half = slots // 2
+    pack = jax.ShapeDtypeStruct((half + half // 2, half), bf16)
+    return pl.pallas_call(
+        inner_kernel,
+        out_shape=[jax.ShapeDtypeStruct((feats, slots), bf16), pack, pack],
+        scratch_shapes=[pltpu.VMEM((slots, feats), bf16)],
+        compiler_params=pltpu.CompilerParams(vmem_limit_bytes=VMEM),
+        name="inner_products",
+    )(recv)
+
+
+def hidden_kernel(grads_ref, matrix_ref, saved_ref, weight_ref, up_ref, dw_ref):
+    parts, rows, feats = grads_ref.shape
+    width = matrix_ref.shape[1]
+    hidden = jnp.zeros((rows, width), f32)
+    for part in range(parts):
+        block = matrix_ref[0, :, part * feats : (part + 1) * feats]
+        hidden = hidden + dot(grads_ref[part], block, ((1,), (1,)))
+    gate = saved_ref[0, :, :width].astype(f32)
+    up = saved_ref[0, :, width:].astype(f32)
+    act = gate / (1.0 + jnp.exp(-gate))
+    scaled = hidden * act
+    up_ref[...] = (weight_ref[...] * scaled).astype(bf16)
+    share = jnp.sum(scaled * up, axis=1, keepdims=True)
+
+    @pl.when(pl.program_id(0) == 0)
+    def _():
+        dw_ref[...] = share
+
+    @pl.when(pl.program_id(0) != 0)
+    def _():
+        dw_ref[...] += share
+
+
+def hidden_step(grads, matrix, saved, weight):
+    parts, rows, feats = grads.shape
+    blocks, width, depth = matrix.shape
+    return pl.pallas_call(
+        hidden_kernel,
+        grid=(blocks,),
+        in_specs=[
+            pl.BlockSpec((parts, rows, feats), lambda j: (0, 0, 0)),
+            pl.BlockSpec((1, width, depth), lambda j: (j, 0, 0)),
+            pl.BlockSpec((1, rows, 2 * width), lambda j: (j, 0, 0)),
+            pl.BlockSpec((rows, 1), lambda j: (0, 0)),
+        ],
+        out_specs=[
+            pl.BlockSpec((rows, width), lambda j: (0, j)),
+            pl.BlockSpec((rows, 1), lambda j: (0, 0)),
+        ],
+        out_shape=[
+            jax.ShapeDtypeStruct((rows, blocks * width), bf16),
+            jax.ShapeDtypeStruct((rows, 1), f32),
+        ],
+        compiler_params=pltpu.CompilerParams(vmem_limit_bytes=VMEM),
+        name="hidden_step",
+    )(grads, matrix, saved, weight)
+
+
+def last_kernel(
+    rank_ref, rows_t_ref, low_a, low_b, high_a, high_b, up_0, up_1, up_2, up_3, out_ref,
+    up_ref, inner_ref, carried_ref, gram_ref, square_ref, poly_ref, start_ref,
+):
+    rank = rank_ref[0]
+    own = up_0.shape[0]
+    slots, hidden = up_ref.shape
+    feats = rows_t_ref.shape[0]
+    half = slots // 2
+    for step, part in ((0, up_0), (3, up_1), (1, up_2), (2, up_3)):
+        place = pl.multiple_of(lax.rem(rank + step, 4) * own, own)
+        up_ref[pl.ds(place, own)] = part[...]
+    low = low_a[...].astype(f32) + low_b[...].astype(f32)
+    high = high_a[...].astype(f32) + high_b[...].astype(f32)
+    inner_ref[:half, :half] = low[:half].astype(bf16)
+    inner_ref[half:, half:] = high[half // 2 :].astype(bf16)
+    cross = jnp.concatenate([low[half:], high[: half // 2]], axis=0)
+    inner_ref[:half, half:] = cross.astype(bf16)
+    inner_ref[half:, :half] = cross.T.astype(bf16)
+    norm = jnp.zeros((1, 1), f32)
+    step = slots // 3
+    for i in range(0, slots, step):
+        carried = dot(inner_ref[i : i + step], up_ref[...], ((1,), (0,)))
+        norm = norm + total(carried * up_ref[i : i + step].astype(f32))
+        carried_ref[i : i + step] = carried.astype(bf16)
+    scale = 1.0 / (1.01 * jnp.sqrt(jnp.maximum(norm, 0.0)) + 1e-07)
+    step = hidden // 4
+    for i in range(0, hidden, step):
+        gram = dot(up_ref[:, i : i + step], carried_ref[...], ((0,), (0,)))
+        gram_ref[i : i + step] = (gram * scale * scale).astype(bf16)
+    quartic = jnp.zeros((1, 1), f32)
+    for i in range(0, hidden, step):
+        square = dot(gram_ref[i : i + step], gram_ref[...], ((1,), (0,)))
+        quartic = quartic + total(square * square)
+        square_ref[i : i + step] = square
+    rows = feats // 4
+    for i in range(0, feats, rows):
+        gradient = dot(rows_t_ref[i : i + rows], up_ref[...], ((1,), (0,)))
+        start_ref[i : i + rows] = (gradient * scale).astype(bf16)
+    bound = jnp.sqrt(jnp.sqrt(quartic)) + 1e-06
+    first_scale = poly_third / bound
+    second_scale = poly_fifth / (bound * bound)
+    for i in range(0, hidden, step):
+        poly_ref[i : i + step] = (
+            first_scale * gram_ref[i : i + step].astype(f32)
+            + second_scale * square_ref[i : i + step]
+        ).astype(bf16)
+    for i in range(0, feats, rows):
+        start = start_ref[i : i + rows]
+        mixed = dot(start, poly_ref[...], ((1,), (0,)))
+        out_ref[0, i : i + rows] = (
+            math.sqrt(D) * (poly_first * start.astype(f32) + mixed)
+        ).astype(bf16)
+
+
+def last_step(rank, rows_t, packs, ups):
+    feats, slots = rows_t.shape
+    hidden = ups[0].shape[1]
+    vmem = pl.BlockSpec(memory_space=pltpu.VMEM)
+    return pl.pallas_call(
+        last_kernel,
+        in_specs=[pl.BlockSpec(memory_space=pltpu.SMEM)] + [vmem] * 9,
+        out_specs=vmem,
+        out_shape=jax.ShapeDtypeStruct((1, feats, hidden), bf16),
+        scratch_shapes=[
+            pltpu.VMEM((slots, hidden), bf16),
+            pltpu.VMEM((slots, slots), bf16),
+            pltpu.VMEM((slots, hidden), bf16),
+            pltpu.VMEM((hidden, hidden), bf16),
+            pltpu.VMEM((hidden, hidden), f32),
+            pltpu.VMEM((hidden, hidden), bf16),
+            pltpu.VMEM((feats, hidden), bf16),
+        ],
+        compiler_params=pltpu.CompilerParams(vmem_limit_bytes=VMEM),
+        name="last_step",
+    )(rank, rows_t, *packs, *ups)
 
 
 def on_device(tokens_in, out_grad, expert_ids, combine, down_weight, gate_saved, up_saved):
@@ -59,7 +266,6 @@
     tok_rows, top_count = expert_ids.shape
     feats = tokens_in.shape[1]
     hidden_part = gate_saved.shape[2]
-    hidden_all = hidden_part * ny
 
     column = lax.all_gather(
         jnp.concatenate([tokens_in, out_grad], axis=1), "z", axis=0, tiled=True
@@ -83,19 +289,14 @@
         "z", 0, 0, tiled=True,
     )
     routes = routes.reshape(nz, 2, near, CAP)
-    start = (jnp.arange(nz, dtype=jnp.int32) * tok_rows).astype(f32)[:, None, None]
+    start = (jnp.arange(nz, dtype=jnp.int32) % zl * tok_rows).astype(f32)[:, None, None]
     index = jnp.where(routes[:, 0] > 0.0, routes[:, 0] + start, 0.0)
-    split = index.reshape(ny, zl, near, CAP)
-    index_tok = index.transpose(1, 0, 2).reshape(-1)
-    index_grad = split.transpose(0, 2, 1, 3).reshape(-1)
-    columns = (jnp.arange(nz * tok_rows, dtype=jnp.int32) + 1).astype(f32)
-    select_tok = (index_tok[:, None] == columns[None, :]).astype(bf16)
-    select_grad = (index_grad[:, None] == columns[None, :]).astype(bf16)
+    index = index.reshape(ny, zl, near, CAP).transpose(0, 2, 1, 3).reshape(ny, own_slots, 1)
     weight_order = routes[:, 1].reshape(ny, zl, near, CAP).transpose(0, 2, 1, 3)
     weight = lax.all_to_all(
         weight_order.reshape(ny * near, zl * CAP), ("y", "x", "c"), 0, 0, tiled=True
     )
-    weight = weight.reshape(ny, own_slots)[0]
+    weight = weight.reshape(ny, own_slots)[0][:, None]
 
     row = jnp.arange(slots, dtype=jnp.int32)
     rest = row // CAP
@@ -112,29 +313,27 @@
     saved = lax.all_to_all(
         saved.reshape(ny, own_slots, 2 * hidden_part), "y", 0, 0, tiled=True
     )
-    gate = saved[:, :, :hidden_part].transpose(1, 0, 2).reshape(own_slots, hidden_all)
-    up = saved[:, :, hidden_part:].transpose(1, 0, 2).reshape(own_slots, hidden_all)
-    gate_act = jax.nn.silu(gate.astype(f32))
-    hidden_act = gate_act * up.astype(f32)
-
-    rows = dot(select_tok, column[:, :feats], ((1,), (0,))).astype(bf16)
+
+    column, matrix, saved = lax.optimization_barrier((column, matrix, saved))
+    token_send, grad_send = pick_rows(
+        index, column.reshape(ny, zl * tok_rows, 2 * feats), near
+    )
     rows = lax.all_to_all(
-        rows.reshape(near, nz * CAP, feats), ("x", "c"), 0, 0, tiled=True
-    )
-    rows = rows.reshape(near, ny, zl * CAP, feats).transpose(1, 0, 2, 3).reshape(slots, feats)
-    inner = lax.psum(dot(rows, rows, ((1,), (1,))).astype(bf16), "y")
-
-    grads = dot(select_grad, column[:, feats:], ((1,), (0,))).astype(bf16)
+        token_send.reshape(near, nz * CAP, feats), ("x", "c"), 0, 0, tiled=True
+    ).reshape(near, ny, zl * CAP, feats)
+    rows_t, low, high = inner_products(rows)
+    beside, across = (lambda i: i ^ 1), (lambda i: ny - 1 - i)
+    low_near, high_near = swap(low, beside), swap(high, across)
+
+    grad_send, _ = lax.optimization_barrier((grad_send, rows))
     grads = lax.all_to_all(
-        grads.reshape(ny * near, zl * CAP, feats), ("y", "x", "c"), 0, 0, tiled=True
-    )
-    grads = grads.reshape(ny, own_slots, feats).transpose(1, 0, 2).reshape(own_slots, ny * feats)
-    hidden_grad = dot(grads, matrix, ((1,), (1,)))
-    slot_dw = jnp.sum(hidden_grad * hidden_act, axis=1)
-    up_own = (weight[:, None] * hidden_grad * gate_act).astype(bf16)
-    up_grad = lax.all_to_all(
-        jnp.broadcast_to(up_own[None], (ny, own_slots, hidden_all)), "y", 0, 0, tiled=True
-    ).reshape(slots, hidden_all)
+        grad_send.reshape(ny * near, zl * CAP, feats), ("y", "x", "c"), 0, 0, tiled=True
+    ).reshape(ny, own_slots, feats)
+    low_near, high_near, grads = lax.optimization_barrier((low_near, high_near, grads))
+    low, high = low + low_near, high + high_near
+    packs = (low, swap(low, across), high, swap(high, beside))
+    up_own, slot_dw = hidden_step(grads, matrix, saved, weight)
+    ups = (up_own, shift(up_own, 1), shift(up_own, -1), shift(up_own, 2))
 
     back = jnp.broadcast_to(slot_dw.reshape(1, near, zl * CAP), (ny, near, zl * CAP))
     back = lax.all_to_all(
@@ -145,22 +344,9 @@
     dcombine = jnp.sum(jnp.where(matches, back[:, None], 0.0), axis=0)
     dcombine = dcombine.reshape(tok_rows, top_count)
 
-    gradient = dot(rows, up_grad, ((0,), (0,)))
-    carried = dot(inner, up_grad, ((1,), (0,)))
-    norm_total = jnp.sum(carried * up_grad.astype(f32))
-    scale = 1.0 / (1.01 * jnp.sqrt(jnp.maximum(norm_total, 0.0)) + 1e-07)
-    gram = dot(up_grad, carried.astype(bf16), ((0,), (0,)))
-    gram_low = (gram * scale * scale).astype(bf16)
-    start_iter = (gradient * scale).astype(bf16)
-    square = dot(gram_low, gram_low, ((1,), (0,)))
-    quartic = jnp.sum(square * square)
-    bound = jnp.sqrt(jnp.sqrt(quartic)) + 1e-06
-    first_scale = poly_third / bound
-    second_scale = poly_fifth / (bound * bound)
-    poly = (first_scale * gram_low.astype(f32) + second_scale * square).astype(bf16)
-    mixed = dot(start_iter, poly, ((1,), (0,)))
-    update = (math.sqrt(D) * (poly_first * start_iter.astype(f32) + mixed)).astype(bf16)
-    return (update[None], dcombine)
+    rank = lax.axis_index("y").reshape(1)
+    update = last_step(rank, rows_t, packs, ups)
+    return (update, dcombine)
 
 
 def build(mesh, plane):

time: 288 us -> 260 us (0.903)
  waiting for transfers between devices: 123 us -> 59 us
  blocking collectives: 0 us -> 56.3 us
  matrix products: 45.4 us -> 2.82 us
  Pallas kernels: 0 us -> 25.3 us
  starting transfers between devices: 70.5 us -> 67.2 us
  other arithmetic: 4.75 us -> 7.96 us
    all_to_all x0 -> x3, blocking collectives: none -> 56.3 us  [the longest x1 23.6 us: on_device(): lax.all_to_all(token_send.reshape(near, nz * CAP, feats), ('x', 'c'), 0,...]
    psum x1 -> x0, waiting for transfers between devices: 47.7 us -> none  [on_device(): inner = lax.psum(dot(rows, rows, ((1,), (1,))).astype(bf16), 'y')]
    dot_general x10 -> x1, matrix products: 45.4 us -> 2.82 us  [dot(): lax.dot_general(a, b, (contract, ((), ())), preferred_element_type=f32)]
    all_to_all x5 -> x1, waiting for transfers between devices: 36.3 us -> 8.08 us  [on_device(): lax.all_to_all(grad_send.reshape(ny * near, zl * CAP, feats), ('y', 'x',...]
    pallas_call x0 -> x4, Pallas kernels: none -> 25.3 us  [the longest x1 11.7 us: last_step(): pl.pallas_call(last_kernel, in_specs=[pl.BlockSpec(memory_space=pltpu.SME...]
    all_to_all x5 -> x1, starting transfers between devices: 29.6 us -> 5.79 us  [on_device(): lax.all_to_all(grad_send.reshape(ny * near, zl * CAP, feats), ('y', 'x',...]
    ppermute x4 -> x7, waiting for transfers between devices: 0.01 us -> 17.3 us  [shift(): lax.ppermute(values, 'y', [(i, (i + step) % size) for i in range(size)])]
    ppermute x0 -> x4, starting transfers between devices: none -> 11.9 us  [swap(): return lax.ppermute(values, 'y', [(i, partner(i)) for i in range(size)])]
  transfers between devices with their start and end apart: 14 -> 16, of which waited for: 9 -> 6; matrix products, arithmetic and copies ran while one was open for 19% -> 11% of each run, Pallas kernels for 0% -> 3%
where the time goes in v2:
time: 260 us; the launch traced here: 258 us
  starting transfers between devices  67.2 us (26%)
  waiting for transfers between devices  59 us (23%)
  blocking collectives  56.3 us (22%)
  local copies, waits for them, and re-layouts  25.5 us (10%)
  Pallas kernels  25.3 us (10%)
  between operations  14.3 us (6%)
  other arithmetic  7.96 us (3%)
  matrix products  2.82 us (1%)
    all_gather x1, waiting for transfers between devices, on_device(): lax.all_gather(jnp.concatenate([tokens_in, out_grad], axis=1), 'z', axis=...  27.1 us
    ppermute x7, starting transfers between devices, shift(): lax.ppermute(values, 'y', [(i, (i + step) % size) for i in range(size)])  25.7 us
    all_to_all x1, blocking collectives, on_device(): lax.all_to_all(token_send.reshape(near, nz * CAP, feats), ('x', 'c'), 0,...  23.6 us
    all_to_all x1, blocking collectives, on_device(): back = lax.all_to_all(back, 'z', 0, 0, tiled=True).reshape(-1)  19.7 us
    ppermute x7, waiting for transfers between devices, shift(): lax.ppermute(values, 'y', [(i, (i + step) % size) for i in range(size)])  17.3 us
    all_to_all x1, starting transfers between devices, on_device(): lax.all_to_all(jnp.stack([index_send.reshape(nz, near * CAP), weight_send...  14.9 us
    all_to_all x1, blocking collectives, on_device(): lax.all_to_all(back.reshape(ny * near, zl * CAP), ('y', 'x', 'c'), 0, 0,...  12.9 us
    ppermute x4, starting transfers between devices, swap(): return lax.ppermute(values, 'y', [(i, partner(i)) for i in range(size)])  11.9 us
  transfers between devices with their start and end apart: 16, of which 6 were waited for; matrix products, arithmetic and copies ran while one was open for 11% of the time, Pallas kernels for 3%

profile of v2, /device:TPU:1, one launch (start us, length us, event | category | flops | bytes accessed | tf_op | source)
XLA Modules:
  0.0 258.4 jit_solution(12886593991570297653)
XLA Ops:
  9.1 4.0 %collective-permute-start = (bf16[256,3584]{1,0:T(8,128)(2,1)}, bf16[256,3584]{1,0:T(8,128)(2,1)S(1)}, u32[]{:S(2)}, u32[]{:S(2)}) collective-permute-start(bf16[256,3584]{1,0:T(8,128)(2,1)} %bitcast.39), channel_id=1, source_target_pairs={{0,1},{1,2},{2,3},{3,0},{4,5},{5,6},{6,7},{7,4},{8,9},{9,10},{10,1... | collective-permute-start | bytes 5505032 | tf_op jit(solution)/shard_map/ppermute | solution.py:36
  13.1 3.4 %collective-permute-start.1 = (bf16[256,3584]{1,0:T(8,128)(2,1)}, bf16[256,3584]{1,0:T(8,128)(2,1)}, u32[]{:S(2)}, u32[]{:S(2)}) collective-permute-start(bf16[256,3584]{1,0:T(8,128)(2,1)} %bitcast.40), channel_id=1, source_target_pairs={{0,3},{1,0},{2,1},{3,2},{4,7},{5,4},{6,5},{7,6},{8,11},{9,8},{10,9... | collective-permute-start | bytes 5505032 | tf_op jit(solution)/shard_map/ppermute | solution.py:36
  20.5 14.9 %all-to-all-start = ((f32[16,2,48]{2,1,0:T(2,128)}), f32[16,2,48]{2,1,0:T(2,128)S(1)}, u32[]{:S(2)}, u32[]{:S(2)}) async-start(f32[16,2,48]{2,1,0:T(2,128)} %copy.52), calls=%async_computation | async-start | bytes 32768 | tf_op jit(solution)/shard_map/all_to_all | solution.py:287
  38.3 3.6 %broadcast_in_dim.74 = bf16[4,256,3584]{2,1,0:T(8,128)(2,1)} broadcast(bf16[]{:T(256)} %constant.166.clone.1), dimensions={} | broadcast | bytes 7340034 | tf_op jit(solution)/shard_map/broadcast_in_dim | solution.py:46
  43.3 3.6 %all-to-all-done = f32[16,2,48]{2,1,0:T(2,128)S(1)} async-done(((f32[16,2,48]{2,1,0:T(2,128)}), f32[16,2,48]{2,1,0:T(2,128)S(1)}, u32[]{:S(2)}, u32[]{:S(2)}) %all-to-all-start) | async-done | bytes 6176 | tf_op jit(solution)/shard_map/all_to_all | solution.py:287
  47.0 3.5 %all-to-all-start.1 = ((bf16[4,192,512]{2,1,0:T(8,128)(2,1)}), bf16[4,192,512]{2,1,0:T(8,128)(2,1)S(1)}, u32[]{:S(2)}, u32[]{:S(2)}) async-start(bf16[4,192,512]{2,1,0:T(8,128)(2,1)} %bitcast.41), calls=%async_computation.1 | async-start | bytes 1572864 | tf_op jit(solution)/shard_map/all_to_all | solution.py:313
  51.8 3.6 %collective-permute-start.2 = (bf16[128,3584]{1,0:T(8,128)(2,1)S(1)}, bf16[128,3584]{1,0:T(8,128)(2,1)S(1)}, u32[]{:S(2)}, u32[]{:S(2)}) collective-permute-start(bf16[128,3584]{1,0:T(8,128)(2,1)S(1)} %slice.24), channel_id=1, source_target_pairs={{0,1},{1,2},{2,3},{3,0},{4,5},{5,6},{6,7},{7,4},{8,9},{9,10},{10,1... | collective-permute-start | bytes 2752520 | tf_op jit(solution)/shard_map/ppermute | solution.py:36
  56.6 4.3 %collective-permute-start.3 = (bf16[128,3584]{1,0:T(8,128)(2,1)S(1)}, bf16[128,3584]{1,0:T(8,128)(2,1)S(1)}, u32[]{:S(2)}, u32[]{:S(2)}) collective-permute-start(bf16[128,3584]{1,0:T(8,128)(2,1)S(1)} %slice.25), channel_id=1, source_target_pairs={{0,3},{1,0},{2,1},{3,2},{4,7},{5,4},{6,5},{7,6},{8,11},{9,8},{10,9... | collective-permute-start | bytes 2752520 | tf_op jit(solution)/shard_map/ppermute | solution.py:36
  62.3 2.9 %bitcast_dynamic-update-slice_fusion = bf16[4,256,3584]{2,1,0:T(8,128)(2,1)} fusion(bf16[4,256,3584]{2,1,0:T(8,128)(2,1)} %bitcast_dynamic-update-slice_fusion.1, s32[]{:T(128)S(6)} %select_n.165, bf16[256,3584]{1,0:T(8,128)(2,1)} %collective-permute-done.1), kind=kLoop, calls=%fused_computation.9 | loop fusion | bytes 3670020 | tf_op jit(solution)/shard_map/dynamic_update_slice | solution.py:50
  65.1 17.3 %collective-permute-done.2 = bf16[128,3584]{1,0:T(8,128)(2,1)S(1)} collective-permute-done((bf16[128,3584]{1,0:T(8,128)(2,1)S(1)}, bf16[128,3584]{1,0:T(8,128)(2,1)S(1)}, u32[]{:S(2)}, u32[]{:S(2)}) %collective-permute-start.2) | collective-permute-done | bytes 917536 | tf_op jit(solution)/shard_map/ppermute | solution.py:36
  84.4 27.1 %all-gather.2.cloned.1.call-done = bf16[2048,1792]{1,0:T(8,128)(2,1)} async-done(((bf16[128,1792]{1,0:T(8,128)(2,1)}), bf16[2048,1792]{1,0:T(8,128)(2,1)}) %all-gather.2.cloned.1.call-update) | async-done | bytes 7340048 | tf_op jit(solution)/shard_map/all_gather | solution.py:270
  111.5 5.1 %pick_rows.1 = (bf16[8,4,24,896]{3,2,1,0:T(8,128)(2,1)S(1)}, bf16[4,8,24,896]{3,2,1,0:T(8,128)(2,1)S(1)}) custom-call(f32[4,192,1]{2,1,0:T(8,128)S(1)} %reshape.294.index_ref, bf16[4,512,1792]{2,1,0:T(8,128)(2,1)} %bitcast.38), custom_call_target="tpu_custom_call" | custom-call | tf_op jit(solution)/shard_map/pick_rows/pallas_call | solution.py:81
  117.7 23.6 %all_to_all.47 = bf16[8,96,896]{2,1,0:T(8,128)(2,1)S(1)} all-to-all(bf16[8,96,896]{2,1,0:T(8,128)(2,1)S(1)} %bitcast.37), channel_id=1, replica_groups=mesh['x'=4,'z'=16,'c'=2,'y'=4] {'x','c'}, dimensions={0} | all-to-all | bytes 2752512 | tf_op jit(solution)/shard_map/all_to_all | solution.py:321
  141.4 5.8 %all-to-all-start.3 = ((bf16[32,24,896]{2,1,0:T(8,128)(2,1)}), bf16[32,24,896]{2,1,0:T(8,128)(2,1)S(1)}, u32[]{:S(2)}, u32[]{:S(2)}) async-start(bf16[32,24,896]{2,1,0:T(8,128)(2,1)} %bitcast.36), calls=%async_computation.3 | async-start | bytes 2752512 | tf_op jit(solution)/shard_map/all_to_all | solution.py:329
  150.4 3.3 %collective-permute-start.4 = (bf16[576,384]{1,0:T(8,128)(2,1)}, bf16[576,384]{1,0:T(8,128)(2,1)}, u32[]{:S(2)}, u32[]{:S(2)}) collective-permute-start(bf16[576,384]{1,0:T(8,128)(2,1)} %get-tuple-element.19), channel_id=1, source_target_pairs={{0,1},{1,0},{2,3},{3,2},{4,5},{5,4},{6,7},{7,6},{8,9},{9,8},{10,11... | collective-permute-start | bytes 1327112 | tf_op jit(solution)/shard_map/ppermute | solution.py:60
  153.7 3.7 %collective-permute-start.5 = (bf16[576,384]{1,0:T(8,128)(2,1)}, bf16[576,384]{1,0:T(8,128)(2,1)S(1)}, u32[]{:S(2)}, u32[]{:S(2)}) collective-permute-start(bf16[576,384]{1,0:T(8,128)(2,1)} %get-tuple-element.20), channel_id=1, source_target_pairs={{0,3},{1,2},{2,1},{3,0},{4,7},{5,6},{6,5},{7,4},{8,11},{9,10},{10,... | collective-permute-start | bytes 1327112 | tf_op jit(solution)/shard_map/ppermute | solution.py:60
  159.1 8.1 %all-to-all-done.3 = bf16[32,24,896]{2,1,0:T(8,128)(2,1)S(1)} async-done(((bf16[32,24,896]{2,1,0:T(8,128)(2,1)}), bf16[32,24,896]{2,1,0:T(8,128)(2,1)S(1)}, u32[]{:S(2)}, u32[]{:S(2)}) %all-to-all-start.3) | async-done | bytes 1376288 | tf_op jit(solution)/shard_map/all_to_all | solution.py:329
  167.2 5.3 %all-to-all-start.4 = ((f32[32,1,24]{2,1,0:T(1,128)}), f32[32,1,24]{2,1,0:T(1,128)S(1)}, u32[]{:S(2)}, u32[]{:S(2)}) async-start(f32[32,1,24]{2,1,0:T(1,128)} %reshape.295), calls=%async_computation.4 | async-start | bytes 32768 | tf_op jit(solution)/shard_map/all_to_all | solution.py:296
  184.3 6.4 %hidden_step.1 = (bf16[192,1024]{1,0:T(8,128)(2,1)}, f32[192,1]{1,0:T(8,128)S(1)}) custom-call(bf16[4,192,896]{2,1,0:T(8,128)(2,1)S(1)} %bitcast.34, bf16[4,256,3584]{2,1,0:T(8,128)(2,1)} %bitcast_dynamic-update-slice_fusion.2.matrix_ref, bf16[4,192,512]{2,1,0:T(8,128)(2,1)S(1)} %all-to-all-done.1.saved_ref, f32[192,1]{1,0:T(8,128)S(1)} %copy-done.3), custom_call_target="tpu_custom_call" | custom-call | tf_op jit(solution)/shard_map/hidden_step/pallas_call | solution.py:158
  191.4 4.0 %collective-permute-start.10 = (bf16[192,1024]{1,0:T(8,128)(2,1)}, bf16[192,1024]{1,0:T(8,128)(2,1)S(1)}, u32[]{:S(2)}, u32[]{:S(2)}) collective-permute-start(bf16[192,1024]{1,0:T(8,128)(2,1)} %get-tuple-element.28.up_0), channel_id=1, source_target_pairs={{0,2},{1,3},{2,0},{3,1},{4,6},{5,7},{6,4},{7,5},{8,10},{9,11},{10,... | collective-permute-start | bytes 1179656 | tf_op jit(solution)/shard_map/ppermute | solution.py:36
  197.6 4.3 %collective-permute-start.9 = (bf16[192,1024]{1,0:T(8,128)(2,1)}, bf16[192,1024]{1,0:T(8,128)(2,1)S(1)}, u32[]{:S(2)}, u32[]{:S(2)}) collective-permute-start(bf16[192,1024]{1,0:T(8,128)(2,1)} %get-tuple-element.28.up_0), channel_id=1, source_target_pairs={{0,3},{1,0},{2,1},{3,2},{4,7},{5,4},{6,5},{7,6},{8,11},{9,8},{10,9... | collective-permute-start | bytes 1179656 | tf_op jit(solution)/shard_map/ppermute | solution.py:36
  203.0 12.9 %all_to_all.48 = f32[32,1,24]{2,1,0:T(1,128)S(1)} all-to-all(f32[32,1,24]{2,1,0:T(1,128)S(1)} %bitcast.46), channel_id=1, replica_groups=mesh['x'=4,'z'=16,'c'=2,'y'=4] {'y','x','c'}, dimensions={0} | all-to-all | bytes 6144 | tf_op jit(solution)/shard_map/all_to_all | solution.py:339
  216.4 19.7 %all_to_all.49 = f32[16,1,48]{2,1,0:T(1,128)S(1)} all-to-all(f32[16,1,48]{2,1,0:T(1,128)S(1)} %bitcast.47), channel_id=1, replica_groups=mesh['x'=4,'z'=16,'c'=2,'y'=4] {'z'}, dimensions={0} | all-to-all | bytes 6144 | tf_op jit(solution)/shard_map/all_to_all | solution.py:343
  239.9 11.7 %last_step.1 = bf16[1,896,1024]{2,1,0:T(8,128)(2,1)} custom-call(s32[1]{0:T(128)} %bitcast.rank_ref, bf16[896,768]{1,0:T(8,128)(2,1)S(1)} %copy-done.1, bf16[576,384]{1,0:T(8,128)(2,1)S(1)} %add.234.low_a, bf16[576,384]{1,0:T(8,128)(2,1)} %collective-permute-done.6.low_b, bf16[576,384]{1,0:T(8,128)(2,1)S(1)} %add.235.high_a, ...), custom_call_target="tpu_custom_call" | custom-call | tf_op jit(solution)/shard_map/last_step/pallas_call | solution.py:239
  (78 shorter events, 42.0 us)
Async XLA Ops:
  7.2 104.4 %all-gather.2.cloned.1.call-start = ((), (), s32[]{:S(2)}) async-start(), calls=%async_computation.7 | async-start | bytes 7798784 | tf_op jit(solution)/shard_map/all_gather | solution.py:270
  9.1 42.6 %collective-permute-start = (bf16[256,3584]{1,0:T(8,128)(2,1)}, bf16[256,3584]{1,0:T(8,128)(2,1)S(1)}, u32[]{:S(2)}, u32[]{:S(2)}) collective-permute-start(bf16[256,3584]{1,0:T(8,128)(2,1)} %bitcast.39), channel_id=1, source_target_pairs={{0,1},{1,2},{2,3},{3,0},{4,5},{5,6},{6,7},{7,4},{8,9},{9,10},{10,1... | collective-permute-start | bytes 5505032 | tf_op jit(solution)/shard_map/ppermute | solution.py:36
  13.1 42.3 %collective-permute-start.1 = (bf16[256,3584]{1,0:T(8,128)(2,1)}, bf16[256,3584]{1,0:T(8,128)(2,1)}, u32[]{:S(2)}, u32[]{:S(2)}) collective-permute-start(bf16[256,3584]{1,0:T(8,128)(2,1)} %bitcast.40), channel_id=1, source_target_pairs={{0,3},{1,0},{2,1},{3,2},{4,7},{5,4},{6,5},{7,6},{8,11},{9,8},{10,9... | collective-permute-start | bytes 5505032 | tf_op jit(solution)/shard_map/ppermute | solution.py:36
  20.5 26.4 %all-to-all-start = ((f32[16,2,48]{2,1,0:T(2,128)}), f32[16,2,48]{2,1,0:T(2,128)S(1)}, u32[]{:S(2)}, u32[]{:S(2)}) async-start(f32[16,2,48]{2,1,0:T(2,128)} %copy.52), calls=%async_computation | async-start | bytes 32768 | tf_op jit(solution)/shard_map/all_to_all | solution.py:287
  38.3 3.6 %copy-start.5 = (bf16[1,256,3584]{2,1,0:T(8,128)(2,1)S(1)}, bf16[1,256,3584]{2,1,0:T(8,128)(2,1)}, u32[]{:S(2)}) copy-start(bf16[1,256,3584]{2,1,0:T(8,128)(2,1)} %param.11) | copy-start | bytes 5505028
  47.0 37.4 %all-to-all-start.1 = ((bf16[4,192,512]{2,1,0:T(8,128)(2,1)}), bf16[4,192,512]{2,1,0:T(8,128)(2,1)S(1)}, u32[]{:S(2)}, u32[]{:S(2)}) async-start(bf16[4,192,512]{2,1,0:T(8,128)(2,1)} %bitcast.41), calls=%async_computation.1 | async-start | bytes 1572864 | tf_op jit(solution)/shard_map/all_to_all | solution.py:313
  51.8 30.6 %collective-permute-start.2 = (bf16[128,3584]{1,0:T(8,128)(2,1)S(1)}, bf16[128,3584]{1,0:T(8,128)(2,1)S(1)}, u32[]{:S(2)}, u32[]{:S(2)}) collective-permute-start(bf16[128,3584]{1,0:T(8,128)(2,1)S(1)} %slice.24), channel_id=1, source_target_pairs={{0,1},{1,2},{2,3},{3,0},{4,5},{5,6},{6,7},{7,4},{8,9},{9,10},{10,1... | collective-permute-start | bytes 2752520 | tf_op jit(solution)/shard_map/ppermute | solution.py:36
  56.6 26.8 %collective-permute-start.3 = (bf16[128,3584]{1,0:T(8,128)(2,1)S(1)}, bf16[128,3584]{1,0:T(8,128)(2,1)S(1)}, u32[]{:S(2)}, u32[]{:S(2)}) collective-permute-start(bf16[128,3584]{1,0:T(8,128)(2,1)S(1)} %slice.25), channel_id=1, source_target_pairs={{0,3},{1,0},{2,1},{3,2},{4,7},{5,4},{6,5},{7,6},{8,11},{9,8},{10,9... | collective-permute-start | bytes 2752520 | tf_op jit(solution)/shard_map/ppermute | solution.py:36
  116.6 1.1 copy-start.2
  141.4 25.9 %all-to-all-start.3 = ((bf16[32,24,896]{2,1,0:T(8,128)(2,1)}), bf16[32,24,896]{2,1,0:T(8,128)(2,1)S(1)}, u32[]{:S(2)}, u32[]{:S(2)}) async-start(bf16[32,24,896]{2,1,0:T(8,128)(2,1)} %bitcast.36), calls=%async_computation.3 | async-start | bytes 2752512 | tf_op jit(solution)/shard_map/all_to_all | solution.py:329
  149.4 1.1 copy-start
  150.4 23.3 %collective-permute-start.4 = (bf16[576,384]{1,0:T(8,128)(2,1)}, bf16[576,384]{1,0:T(8,128)(2,1)}, u32[]{:S(2)}, u32[]{:S(2)}) collective-permute-start(bf16[576,384]{1,0:T(8,128)(2,1)} %get-tuple-element.19), channel_id=1, source_target_pairs={{0,1},{1,0},{2,3},{3,2},{4,5},{5,4},{6,7},{7,6},{8,9},{9,8},{10,11... | collective-permute-start | bytes 1327112 | tf_op jit(solution)/shard_map/ppermute | solution.py:60
  153.7 21.6 %collective-permute-start.5 = (bf16[576,384]{1,0:T(8,128)(2,1)}, bf16[576,384]{1,0:T(8,128)(2,1)S(1)}, u32[]{:S(2)}, u32[]{:S(2)}) collective-permute-start(bf16[576,384]{1,0:T(8,128)(2,1)} %get-tuple-element.20), channel_id=1, source_target_pairs={{0,3},{1,2},{2,1},{3,0},{4,7},{5,6},{6,5},{7,4},{8,11},{9,10},{10,... | collective-permute-start | bytes 1327112 | tf_op jit(solution)/shard_map/ppermute | solution.py:60
  167.2 15.5 %all-to-all-start.4 = ((f32[32,1,24]{2,1,0:T(1,128)}), f32[32,1,24]{2,1,0:T(1,128)S(1)}, u32[]{:S(2)}, u32[]{:S(2)}) async-start(f32[32,1,24]{2,1,0:T(1,128)} %reshape.295), calls=%async_computation.4 | async-start | bytes 32768 | tf_op jit(solution)/shard_map/all_to_all | solution.py:296
  176.5 62.1 %collective-permute-start.7 = (bf16[576,384]{1,0:T(8,128)(2,1)S(1)}, bf16[576,384]{1,0:T(8,128)(2,1)S(1)}, u32[]{:S(2)}, u32[]{:S(2)}) collective-permute-start(bf16[576,384]{1,0:T(8,128)(2,1)S(1)} %add.235.high_a), channel_id=1, source_target_pairs={{0,1},{1,0},{2,3},{3,2},{4,5},{5,4},{6,7},{7,6},{8,9},{9,8},{10,11... | collective-permute-start | bytes 1327112 | tf_op jit(solution)/shard_map/ppermute | solution.py:60
  179.9 58.6 %collective-permute-start.6 = (bf16[576,384]{1,0:T(8,128)(2,1)S(1)}, bf16[576,384]{1,0:T(8,128)(2,1)}, u32[]{:S(2)}, u32[]{:S(2)}) collective-permute-start(bf16[576,384]{1,0:T(8,128)(2,1)S(1)} %add.234.low_a), channel_id=1, source_target_pairs={{0,3},{1,2},{2,1},{3,0},{4,7},{5,6},{6,5},{7,4},{8,11},{9,10},{10,... | collective-permute-start | bytes 1327112 | tf_op jit(solution)/shard_map/ppermute | solution.py:60
  183.5 0.9 copy-start.3
  190.7 0.6 copy-start.4
  191.4 47.2 %collective-permute-start.10 = (bf16[192,1024]{1,0:T(8,128)(2,1)}, bf16[192,1024]{1,0:T(8,128)(2,1)S(1)}, u32[]{:S(2)}, u32[]{:S(2)}) collective-permute-start(bf16[192,1024]{1,0:T(8,128)(2,1)} %get-tuple-element.28.up_0), channel_id=1, source_target_pairs={{0,2},{1,3},{2,0},{3,1},{4,6},{5,7},{6,4},{7,5},{8,10},{9,11},{10,... | collective-permute-start | bytes 1179656 | tf_op jit(solution)/shard_map/ppermute | solution.py:36
  195.4 43.1 %collective-permute-start.8 = (bf16[192,1024]{1,0:T(8,128)(2,1)}, bf16[192,1024]{1,0:T(8,128)(2,1)S(1)}, u32[]{:S(2)}, u32[]{:S(2)}) collective-permute-start(bf16[192,1024]{1,0:T(8,128)(2,1)} %get-tuple-element.28.up_0), channel_id=1, source_target_pairs={{0,1},{1,2},{2,3},{3,0},{4,5},{5,6},{6,7},{7,4},{8,9},{9,10},{10,1... | collective-permute-start | bytes 1179656 | tf_op jit(solution)/shard_map/ppermute | solution.py:36
  197.6 40.9 %collective-permute-start.9 = (bf16[192,1024]{1,0:T(8,128)(2,1)}, bf16[192,1024]{1,0:T(8,128)(2,1)S(1)}, u32[]{:S(2)}, u32[]{:S(2)}) collective-permute-start(bf16[192,1024]{1,0:T(8,128)(2,1)} %get-tuple-element.28.up_0), channel_id=1, source_target_pairs={{0,3},{1,0},{2,1},{3,2},{4,7},{5,4},{6,5},{7,6},{8,11},{9,8},{10,9... | collective-permute-start | bytes 1179656 | tf_op jit(solution)/shard_map/ppermute | solution.py:36
  238.6 1.3 copy-start.1
Sparse Core Ops, SparseCore 0:
  10.1 101.4 all-gather.1

commit v3 on v2

--- a/solution.py
+++ b/solution.py
@@ -38,6 +38,7 @@
 
 def gather_weights(own):
     size, rank = lax.axis_size("y"), lax.axis_index("y")
+    own = own.T
     half = own.shape[0] // 2
     before = shift(own, 1)
     after = shift(own, -1)
@@ -60,41 +61,36 @@
     return lax.ppermute(values, "y", [(i, partner(i)) for i in range(size)])
 
 
-def pick_kernel(index_ref, column_ref, tok_ref, grad_ref):
-    near, _, rows, feats = tok_ref.shape
-    count = column_ref.shape[1]
-    columns = lax.broadcasted_iota(jnp.int32, (near * rows, count), 1).astype(f32) + 1.0
+def pick_kernel(index_ref, column_ref, out_ref):
+    rows, count = index_ref.shape[1], column_ref.shape[1]
+    feats = out_ref.shape[-1]
+    columns = lax.broadcasted_iota(jnp.int32, (rows, count), 1).astype(f32) + 1.0
     chosen = jnp.where(index_ref[0] == columns, 1.0, 0.0).astype(bf16)
-    for part, out in ((0, tok_ref), (1, grad_ref)):
-        values = column_ref[0, :, part * feats : (part + 1) * feats]
-        picked = dot(chosen, values, ((1,), (0,))).reshape(near, rows, feats).astype(bf16)
-        if part:
-            out[0] = picked
-        else:
-            out[:, 0] = picked
-
-
-def pick_rows(index, column, near):
+    picked = dot(chosen, column_ref[0], ((1,), (0,)))
+    out_ref[...] = picked.reshape(out_ref.shape).astype(bf16)
+
+
+def pick_rows(index, column, near, part, by_quarter, name):
     quarters, rows, _ = index.shape
     feats = column.shape[2] // 2
     piece = rows // near
+    if by_quarter:
+        block, place = (1, near, piece, feats), (lambda q: (q, 0, 0, 0))
+        shape = (quarters, near, piece, feats)
+    else:
+        block, place = (near, 1, piece, feats), (lambda q: (0, q, 0, 0))
+        shape = (near, quarters, piece, feats)
     return pl.pallas_call(
         pick_kernel,
         grid=(quarters,),
         in_specs=[
             pl.BlockSpec((1, rows, 1), lambda q: (q, 0, 0)),
-            pl.BlockSpec((1,) + column.shape[1:], lambda q: (q, 0, 0)),
+            pl.BlockSpec((1, column.shape[1], feats), lambda q: (q, 0, part)),
         ],
-        out_specs=[
-            pl.BlockSpec((near, 1, piece, feats), lambda q: (0, q, 0, 0)),
-            pl.BlockSpec((1, near, piece, feats), lambda q: (q, 0, 0, 0)),
-        ],
-        out_shape=[
-            jax.ShapeDtypeStruct((near, quarters, piece, feats), bf16),
-            jax.ShapeDtypeStruct((quarters, near, piece, feats), bf16),
-        ],
+        out_specs=pl.BlockSpec(block, place),
+        out_shape=jax.ShapeDtypeStruct(shape, bf16),
         compiler_params=pltpu.CompilerParams(vmem_limit_bytes=VMEM),
-        name="pick_rows",
+        name=name,
     )(index, column)
 
 
@@ -129,18 +125,36 @@
     )(recv)
 
 
-def hidden_kernel(grads_ref, matrix_ref, saved_ref, weight_ref, up_ref, dw_ref):
+def hidden_kernel(
+    grads_ref, matrix_ref, saved_ref, weight_ref, low_a, low_b, high_a, high_b,
+    up_ref, west_ref, east_ref, dw_ref, rows_ref,
+):
     parts, rows, feats = grads_ref.shape
-    width = matrix_ref.shape[1]
-    hidden = jnp.zeros((rows, width), f32)
-    for part in range(parts):
-        block = matrix_ref[0, :, part * feats : (part + 1) * feats]
-        hidden = hidden + dot(grads_ref[part], block, ((1,), (1,)))
+    width = matrix_ref.shape[2]
+    hidden_all = up_ref.shape[1]
+    half = low_a.shape[1]
+
+    @pl.when(pl.program_id(0) == 0)
+    def _():
+        for part in range(parts):
+            rows_ref[:, part * feats : (part + 1) * feats] = grads_ref[part]
+        for one, two, out in ((low_a, low_b, west_ref), (high_a, high_b, east_ref)):
+            for i in range(3):
+                piece = one[i * rows : (i + 1) * rows].astype(f32)
+                piece = piece + two[i * rows : (i + 1) * rows].astype(f32)
+                first = hidden_all + i * half
+                out[:, first : first + half] = piece.astype(bf16)
+
+    hidden = dot(rows_ref[...], matrix_ref[0], ((1,), (0,)))
     gate = saved_ref[0, :, :width].astype(f32)
     up = saved_ref[0, :, width:].astype(f32)
     act = gate / (1.0 + jnp.exp(-gate))
     scaled = hidden * act
-    up_ref[...] = (weight_ref[...] * scaled).astype(bf16)
+    up_grad = (weight_ref[...] * scaled).astype(bf16)
+    place = pl.ds(pl.multiple_of(pl.program_id(0) * width, width), width)
+    up_ref[:, place] = up_grad
+    west_ref[:, place] = up_grad
+    east_ref[:, place] = up_grad
     share = jnp.sum(scaled * up, axis=1, keepdims=True)
 
     @pl.when(pl.program_id(0) == 0)
@@ -152,48 +166,59 @@
         dw_ref[...] += share
 
 
-def hidden_step(grads, matrix, saved, weight):
+def hidden_step(grads, matrix, saved, weight, sums):
     parts, rows, feats = grads.shape
-    blocks, width, depth = matrix.shape
+    blocks, depth, width = matrix.shape
+    half = sums[0].shape[1]
+    packed = jax.ShapeDtypeStruct((rows, blocks * width + 3 * half), bf16)
+    outs = [
+        jax.ShapeDtypeStruct((rows, blocks * width), bf16),
+        packed,
+        packed,
+        jax.ShapeDtypeStruct((rows, 1), f32),
+    ]
     return pl.pallas_call(
         hidden_kernel,
         grid=(blocks,),
         in_specs=[
             pl.BlockSpec((parts, rows, feats), lambda j: (0, 0, 0)),
-            pl.BlockSpec((1, width, depth), lambda j: (j, 0, 0)),
+            pl.BlockSpec((1, depth, width), lambda j: (j, 0, 0)),
             pl.BlockSpec((1, rows, 2 * width), lambda j: (j, 0, 0)),
             pl.BlockSpec((rows, 1), lambda j: (0, 0)),
-        ],
-        out_specs=[
-            pl.BlockSpec((rows, width), lambda j: (0, j)),
-            pl.BlockSpec((rows, 1), lambda j: (0, 0)),
-        ],
-        out_shape=[
-            jax.ShapeDtypeStruct((rows, blocks * width), bf16),
-            jax.ShapeDtypeStruct((rows, 1), f32),
-        ],
+        ]
+        + [pl.BlockSpec(part.shape, lambda j: (0, 0)) for part in sums],
+        out_specs=[pl.BlockSpec(out.shape, lambda j: (0, 0)) for out in outs],
+        out_shape=outs,
+        scratch_shapes=[pltpu.VMEM((rows, depth), bf16)],
         compiler_params=pltpu.CompilerParams(vmem_limit_bytes=VMEM),
         name="hidden_step",
-    )(grads, matrix, saved, weight)
+    )(grads, matrix, saved, weight, *sums)
 
 
 def last_kernel(
-    rank_ref, rows_t_ref, low_a, low_b, high_a, high_b, up_0, up_1, up_2, up_3, out_ref,
+    rank_ref, rows_t_ref, west_a, west_b, east_a, east_b, far_ref, out_ref,
     up_ref, inner_ref, carried_ref, gram_ref, square_ref, poly_ref, start_ref,
 ):
     rank = rank_ref[0]
-    own = up_0.shape[0]
+    own = far_ref.shape[0]
     slots, hidden = up_ref.shape
     feats = rows_t_ref.shape[0]
     half = slots // 2
-    for step, part in ((0, up_0), (3, up_1), (1, up_2), (2, up_3)):
-        place = pl.multiple_of(lax.rem(rank + step, 4) * own, own)
-        up_ref[pl.ds(place, own)] = part[...]
-    low = low_a[...].astype(f32) + low_b[...].astype(f32)
-    high = high_a[...].astype(f32) + high_b[...].astype(f32)
-    inner_ref[:half, :half] = low[:half].astype(bf16)
-    inner_ref[half:, half:] = high[half // 2 :].astype(bf16)
-    cross = jnp.concatenate([low[half:], high[: half // 2]], axis=0)
+    near = rank + 1 - 2 * lax.rem(rank, 2)
+    owners = ((rank, west_a), (3 - rank, west_b), (near, east_b), (3 - near, far_ref))
+    for owner, part in owners:
+        up_ref[pl.ds(pl.multiple_of(owner * own, own), own)] = part[:, :hidden]
+
+    def summed(one, two, i):
+        lanes = slice(hidden + i * half, hidden + (i + 1) * half)
+        return one[:, lanes].astype(f32) + two[:, lanes].astype(f32)
+
+    low = [summed(west_a, west_b, i) for i in range(3)]
+    high = [summed(east_a, east_b, i) for i in range(3)]
+    cross = jnp.concatenate([low[2], high[0]], axis=0)
+    for i in range(2):
+        inner_ref[i * own : (i + 1) * own, :half] = low[i].astype(bf16)
+        inner_ref[half + i * own : half + (i + 1) * own, half:] = high[1 + i].astype(bf16)
     inner_ref[:half, half:] = cross.astype(bf16)
     inner_ref[half:, :half] = cross.T.astype(bf16)
     norm = jnp.zeros((1, 1), f32)
@@ -232,13 +257,13 @@
         ).astype(bf16)
 
 
-def last_step(rank, rows_t, packs, ups):
+def last_step(rank, rows_t, parts):
     feats, slots = rows_t.shape
-    hidden = ups[0].shape[1]
+    hidden = parts[-1].shape[1]
     vmem = pl.BlockSpec(memory_space=pltpu.VMEM)
     return pl.pallas_call(
         last_kernel,
-        in_specs=[pl.BlockSpec(memory_space=pltpu.SMEM)] + [vmem] * 9,
+        in_specs=[pl.BlockSpec(memory_space=pltpu.SMEM)] + [vmem] * 6,
         out_specs=vmem,
         out_shape=jax.ShapeDtypeStruct((1, feats, hidden), bf16),
         scratch_shapes=[
@@ -252,7 +277,7 @@
         ],
         compiler_params=pltpu.CompilerParams(vmem_limit_bytes=VMEM),
         name="last_step",
-    )(rank, rows_t, *packs, *ups)
+    )(rank, rows_t, *parts)
 
 
 def on_device(tokens_in, out_grad, expert_ids, combine, down_weight, gate_saved, up_saved):
@@ -314,10 +339,10 @@
         saved.reshape(ny, own_slots, 2 * hidden_part), "y", 0, 0, tiled=True
     )
 
-    column, matrix, saved = lax.optimization_barrier((column, matrix, saved))
-    token_send, grad_send = pick_rows(
-        index, column.reshape(ny, zl * tok_rows, 2 * feats), near
-    )
+    column, matrix, saved, weight = lax.optimization_barrier((column, matrix, saved, weight))
+    column = column.reshape(ny, zl * tok_rows, 2 * feats)
+    token_send = pick_rows(index, column, near, 0, False, "pick_tokens")
+    grad_send = pick_rows(index, column, near, 1, True, "pick_grads")
     rows = lax.all_to_all(
         token_send.reshape(near, nz * CAP, feats), ("x", "c"), 0, 0, tiled=True
     ).reshape(near, ny, zl * CAP, feats)
@@ -329,23 +354,25 @@
     grads = lax.all_to_all(
         grad_send.reshape(ny * near, zl * CAP, feats), ("y", "x", "c"), 0, 0, tiled=True
     ).reshape(ny, own_slots, feats)
-    low_near, high_near, grads = lax.optimization_barrier((low_near, high_near, grads))
-    low, high = low + low_near, high + high_near
-    packs = (low, swap(low, across), high, swap(high, beside))
-    up_own, slot_dw = hidden_step(grads, matrix, saved, weight)
-    ups = (up_own, shift(up_own, 1), shift(up_own, -1), shift(up_own, 2))
+    up_own, west, east, slot_dw = hidden_step(
+        grads, matrix, saved, weight, (low, low_near, high, high_near)
+    )
+    parts = (west, swap(west, across), east, swap(east, beside), shift(up_own, 2))
 
     back = jnp.broadcast_to(slot_dw.reshape(1, near, zl * CAP), (ny, near, zl * CAP))
     back = lax.all_to_all(
         back.reshape(ny * near, zl * CAP), ("y", "x", "c"), 0, 0, tiled=True
     )
-    back = back.reshape(ny, near, zl, CAP).transpose(0, 2, 1, 3).reshape(nz, near * CAP)
-    back = lax.all_to_all(back, "z", 0, 0, tiled=True).reshape(-1)
+    back = back.reshape(ny, near, zl, CAP).transpose(0, 2, 1, 3).reshape(nz, near, CAP)
+    back = jnp.pad(back, ((0, 0), (0, 0), (0, 128 - CAP)))
+    back = lax.all_to_all(back, "z", 0, 0, tiled=True)
+
+    rank = lax.axis_index("y").reshape(1)
+    update = last_step(rank, rows_t, parts)
+    back, update = lax.optimization_barrier((back, update))
+    back = back[:, :, :CAP].reshape(-1)
     dcombine = jnp.sum(jnp.where(matches, back[:, None], 0.0), axis=0)
     dcombine = dcombine.reshape(tok_rows, top_count)
-
-    rank = lax.axis_index("y").reshape(1)
-    update = last_step(rank, rows_t, packs, ups)
     return (update, dcombine)
 
 

time: 260 us -> 252 us (0.969)
  blocking collectives: 56.3 us -> 24.9 us
  starting transfers between devices: 67.2 us -> 76.8 us
  local copies, waits for them, and re-layouts: 25.5 us -> 32.8 us
  waiting for transfers between devices: 59 us -> 64.5 us
  Pallas kernels: 25.3 us -> 30.6 us
  other arithmetic: 7.96 us -> 5 us
    all_to_all x2 -> x0, blocking collectives: 43.3 us -> none  [the longest x1 23.6 us: on_device(): lax.all_to_all(token_send.reshape(near, nz * CAP, feats), ('x', 'c'), 0,...]
    all_gather x1, waiting for transfers between devices: 27.1 us -> 8.23 us  [on_device(): lax.all_gather(jnp.concatenate([tokens_in, out_grad], axis=1), 'z', axis=...]
    all_to_all x0 -> x2, waiting for transfers between devices: none -> 13.8 us  [the longest x1 13.8 us: on_device(): lax.all_to_all(token_send.reshape(near, nz * CAP, feats), ('x', 'c'), 0,...]
    ppermute x4, waiting for transfers between devices: 2.82 us -> 16.4 us  [swap(): return lax.ppermute(values, 'y', [(i, partner(i)) for i in range(size)])]
    all_to_all x0 -> x2, starting transfers between devices: none -> 13.5 us  [the longest x1 8.59 us: on_device(): back = lax.all_to_all(back, 'z', 0, 0, tiled=True)]
    all_to_all x1, blocking collectives: 12.9 us -> 24.9 us  [on_device(): lax.all_to_all(back.reshape(ny * near, zl * CAP), ('y', 'x', 'c'), 0, 0,...]
    all_to_all x1, waiting for transfers between devices: 8.08 us -> 0.01 us  [on_device(): lax.all_to_all(grad_send.reshape(ny * near, zl * CAP, feats), ('y', 'x',...]
    ppermute x7 -> x5, starting transfers between devices: 25.7 us -> 18.5 us  [shift(): lax.ppermute(values, 'y', [(i, (i + step) % size) for i in range(size)])]
  transfers between devices with their start and end apart: 16 -> 16, of which waited for: 6 -> 7; matrix products, arithmetic and copies ran while one was open for 11% -> 12% of each run, Pallas kernels for 3% -> 8%
where the time goes in v3:
time: 252 us; the launch traced here: 251 us
  starting transfers between devices  76.8 us (30%)
  waiting for transfers between devices  64.5 us (26%)
  local copies, waits for them, and re-layouts  32.8 us (13%)
  Pallas kernels  30.6 us (12%)
  blocking collectives  24.9 us (10%)
  between operations  14.4 us (6%)
  other arithmetic  5 us (2%)
    all_to_all x1, blocking collectives, on_device(): lax.all_to_all(back.reshape(ny * near, zl * CAP), ('y', 'x', 'c'), 0, 0,...  24.9 us
    ppermute x5, starting transfers between devices, shift(): lax.ppermute(values, 'y', [(i, (i + step) % size) for i in range(size)])  18.5 us
    ppermute x4, waiting for transfers between devices, swap(): return lax.ppermute(values, 'y', [(i, partner(i)) for i in range(size)])  16.4 us
    ppermute x5, waiting for transfers between devices, shift(): lax.ppermute(values, 'y', [(i, (i + step) % size) for i in range(size)])  16.3 us
    all_to_all x1, starting transfers between devices, on_device(): lax.all_to_all(jnp.stack([index_send.reshape(nz, near * CAP), weight_send...  14.9 us
    all_to_all x1, waiting for transfers between devices, on_device(): lax.all_to_all(token_send.reshape(near, nz * CAP, feats), ('x', 'c'), 0,...  13.8 us
    ppermute x4, starting transfers between devices, swap(): return lax.ppermute(values, 'y', [(i, partner(i)) for i in range(size)])  12 us
    pallas_call x1, Pallas kernels, last_step(): pl.pallas_call(last_kernel, in_specs=[pl.BlockSpec(memory_space=pltpu.SME...  11.9 us
  transfers between devices with their start and end apart: 16, of which 7 were waited for; matrix products, arithmetic and copies ran while one was open for 12% of the time, Pallas kernels for 8%

profile of v3, /device:TPU:1, one launch (start us, length us, event | category | flops | bytes accessed | tf_op | source)
XLA Modules:
  0.0 250.6 jit_solution(18071262852867800434)
XLA Ops:
  9.2 3.8 %copy.65 = bf16[1,256,3584]{1,2,0:T(8,128)(2,1)} copy(bf16[1,256,3584]{2,1,0:T(8,128)(2,1)} %param.11) | data formatting | bytes 3670016 | tf_op args[4]
  13.0 4.0 %collective-permute-start = (bf16[3584,256]{1,0:T(8,128)(2,1)}, bf16[3584,256]{1,0:T(8,128)(2,1)}, u32[]{:S(2)}, u32[]{:S(2)}) collective-permute-start(bf16[3584,256]{1,0:T(8,128)(2,1)} %bitcast.4), channel_id=1, source_target_pairs={{0,1},{1,2},{2,3},{3,0},{4,5},{5,6},{6,7},{7,4},{8,9},{9,10},{10,1... | collective-permute-start | bytes 5505032 | tf_op jit(solution)/shard_map/ppermute | solution.py:36
  17.0 3.4 %collective-permute-start.1 = (bf16[3584,256]{1,0:T(8,128)(2,1)}, bf16[3584,256]{1,0:T(8,128)(2,1)}, u32[]{:S(2)}, u32[]{:S(2)}) collective-permute-start(bf16[3584,256]{1,0:T(8,128)(2,1)} %bitcast.4), channel_id=1, source_target_pairs={{0,3},{1,0},{2,1},{3,2},{4,7},{5,4},{6,5},{7,6},{8,11},{9,8},{10,9... | collective-permute-start | bytes 5505032 | tf_op jit(solution)/shard_map/ppermute | solution.py:36
  23.7 14.9 %all-to-all-start = ((f32[16,2,48]{2,1,0:T(2,128)}), f32[16,2,48]{2,1,0:T(2,128)S(1)}, u32[]{:S(2)}, u32[]{:S(2)}) async-start(f32[16,2,48]{2,1,0:T(2,128)} %copy.61), calls=%async_computation | async-start | bytes 32768 | tf_op jit(solution)/shard_map/all_to_all | solution.py:312
  40.4 3.5 %broadcast_in_dim.77 = bf16[4,3584,256]{2,1,0:T(8,128)(2,1)} broadcast(bf16[]{:T(256)} %constant.166.clone.1), dimensions={} | broadcast | bytes 7340034 | tf_op jit(solution)/shard_map/broadcast_in_dim | solution.py:47
  51.2 8.5 %all-to-all-start.2 = ((f32[32,1,24]{2,1,0:T(1,128)}), f32[32,1,24]{2,1,0:T(1,128)S(1)}, u32[]{:S(2)}, u32[]{:S(2)}) async-start(f32[32,1,24]{2,1,0:T(1,128)} %reshape.293), calls=%async_computation.2 | async-start | bytes 32768 | tf_op jit(solution)/shard_map/all_to_all | solution.py:321
  60.2 6.4 %all-to-all-done.2 = f32[32,1,24]{2,1,0:T(1,128)S(1)} async-done(((f32[32,1,24]{2,1,0:T(1,128)}), f32[32,1,24]{2,1,0:T(1,128)S(1)}, u32[]{:S(2)}, u32[]{:S(2)}) %all-to-all-start.2) | async-done | bytes 3104 | tf_op jit(solution)/shard_map/all_to_all | solution.py:321
  66.7 3.5 %all-to-all-start.1 = ((bf16[4,192,512]{2,1,0:T(8,128)(2,1)}), bf16[4,192,512]{2,1,0:T(8,128)(2,1)S(1)}, u32[]{:S(2)}, u32[]{:S(2)}) async-start(bf16[4,192,512]{2,1,0:T(8,128)(2,1)} %bitcast.13), calls=%async_computation.1 | async-start | bytes 1572864 | tf_op jit(solution)/shard_map/all_to_all | solution.py:338
  71.5 3.3 %collective-permute-start.2 = (bf16[1792,256]{1,0:T(8,128)(2,1)S(1)}, bf16[1792,256]{1,0:T(8,128)(2,1)S(1)}, u32[]{:S(2)}, u32[]{:S(2)}) collective-permute-start(bf16[1792,256]{1,0:T(8,128)(2,1)S(1)} %slice.28), channel_id=1, source_target_pairs={{0,1},{1,2},{2,3},{3,0},{4,5},{5,6},{6,7},{7,4},{8,9},{9,10},{10,1... | collective-permute-start | bytes 2752520 | tf_op jit(solution)/shard_map/ppermute | solution.py:36
  85.0 16.3 %collective-permute-done.2 = bf16[1792,256]{1,0:T(8,128)(2,1)S(1)} collective-permute-done((bf16[1792,256]{1,0:T(8,128)(2,1)S(1)}, bf16[1792,256]{1,0:T(8,128)(2,1)S(1)}, u32[]{:S(2)}, u32[]{:S(2)}) %collective-permute-start.2) | collective-permute-done | bytes 917536 | tf_op jit(solution)/shard_map/ppermute | solution.py:36
  103.3 8.2 %all-gather.2.cloned.1.call-done = bf16[2048,1792]{1,0:T(8,128)(2,1)} async-done(((bf16[128,1792]{1,0:T(8,128)(2,1)}), bf16[2048,1792]{1,0:T(8,128)(2,1)}) %all-gather.2.cloned.1.call-update) | async-done | bytes 7340048 | tf_op jit(solution)/shard_map/all_gather | solution.py:295
  111.6 4.7 %pick_tokens.1 = bf16[8,4,24,896]{3,2,1,0:T(8,128)(2,1)} custom-call(f32[4,192,1]{2,1,0:T(8,128)S(1)} %reshape.294.index_ref, bf16[4,512,1792]{2,1,0:T(8,128)(2,1)} %bitcast.40), custom_call_target="tpu_custom_call" | custom-call | tf_op jit(solution)/shard_map/pick_tokens/pallas_call | solution.py:83
  116.3 4.9 %all-to-all-start.3 = ((bf16[8,96,896]{2,1,0:T(8,128)(2,1)}), bf16[8,96,896]{2,1,0:T(8,128)(2,1)S(1)}, u32[]{:S(2)}, u32[]{:S(2)}) async-start(bf16[8,96,896]{2,1,0:T(8,128)(2,1)} %bitcast.17), calls=%async_computation.3 | async-start | bytes 2752512 | tf_op jit(solution)/shard_map/all_to_all | solution.py:346
  121.2 4.8 %pick_grads.1 = bf16[4,8,24,896]{3,2,1,0:T(8,128)(2,1)} custom-call(f32[4,192,1]{2,1,0:T(8,128)S(1)} %reshape.294.index_ref, bf16[4,512,1792]{2,1,0:T(8,128)(2,1)} %bitcast.41), custom_call_target="tpu_custom_call" | custom-call | tf_op jit(solution)/shard_map/pick_grads/pallas_call | solution.py:83
  126.0 13.8 %all-to-all-done.3 = bf16[8,96,896]{2,1,0:T(8,128)(2,1)S(1)} async-done(((bf16[8,96,896]{2,1,0:T(8,128)(2,1)}), bf16[8,96,896]{2,1,0:T(8,128)(2,1)S(1)}, u32[]{:S(2)}, u32[]{:S(2)}) %all-to-all-start.3) | async-done | bytes 1376288 | tf_op jit(solution)/shard_map/all_to_all | solution.py:346
  139.8 5.9 %all-to-all-start.4 = ((bf16[32,24,896]{2,1,0:T(8,128)(2,1)}), bf16[32,24,896]{2,1,0:T(8,128)(2,1)S(1)}, u32[]{:S(2)}, u32[]{:S(2)}) async-start(bf16[32,24,896]{2,1,0:T(8,128)(2,1)} %bitcast.19), calls=%async_computation.4 | async-start | bytes 2752512 | tf_op jit(solution)/shard_map/all_to_all | solution.py:354
  149.0 3.3 %collective-permute-start.4 = (bf16[576,384]{1,0:T(8,128)(2,1)}, bf16[576,384]{1,0:T(8,128)(2,1)S(1)}, u32[]{:S(2)}, u32[]{:S(2)}) collective-permute-start(bf16[576,384]{1,0:T(8,128)(2,1)} %get-tuple-element.21.low_a), channel_id=1, source_target_pairs={{0,1},{1,0},{2,3},{3,2},{4,5},{5,4},{6,7},{7,6},{8,9},{9,8},{10,11... | collective-permute-start | bytes 1327112 | tf_op jit(solution)/shard_map/ppermute | solution.py:61
  152.3 3.7 %collective-permute-start.5 = (bf16[576,384]{1,0:T(8,128)(2,1)}, bf16[576,384]{1,0:T(8,128)(2,1)S(1)}, u32[]{:S(2)}, u32[]{:S(2)}) collective-permute-start(bf16[576,384]{1,0:T(8,128)(2,1)} %get-tuple-element.22.high_a), channel_id=1, source_target_pairs={{0,3},{1,2},{2,1},{3,0},{4,7},{5,6},{6,5},{7,4},{8,11},{9,10},{10,... | collective-permute-start | bytes 1327112 | tf_op jit(solution)/shard_map/ppermute | solution.py:61
  156.8 15.4 %collective-permute-done.4.low_b = bf16[576,384]{1,0:T(8,128)(2,1)S(1)} collective-permute-done((bf16[576,384]{1,0:T(8,128)(2,1)}, bf16[576,384]{1,0:T(8,128)(2,1)S(1)}, u32[]{:S(2)}, u32[]{:S(2)}) %collective-permute-start.4) | collective-permute-done | bytes 442400 | tf_op jit(solution)/shard_map/ppermute | solution.py:61
  177.7 7.0 %hidden_step.1 = (bf16[192,1024]{1,0:T(8,128)(2,1)}, bf16[192,2176]{1,0:T(8,128)(2,1)}, bf16[192,2176]{1,0:T(8,128)(2,1)}, f32[192,1]{1,0:T(8,128)S(1)}) custom-call(bf16[4,192,896]{2,1,0:T(8,128)(2,1)S(1)} %bitcast.39, bf16[4,3584,256]{2,1,0:T(8,128)(2,1)} %bitcast_dynamic-update-slice_fusion.3.matrix_ref, ...), custom_call_target="tpu_custom_call" | custom-call | tf_op jit(solution)/shard_map/hidden_step/pallas_call | solution.py:180
  190.3 4.6 %collective-permute-start.8 = (bf16[192,1024]{1,0:T(8,128)(2,1)}, bf16[192,1024]{1,0:T(8,128)(2,1)S(1)}, u32[]{:S(2)}, u32[]{:S(2)}) collective-permute-start(bf16[192,1024]{1,0:T(8,128)(2,1)} %get-tuple-element.27), channel_id=1, source_target_pairs={{0,2},{1,3},{2,0},{3,1},{4,6},{5,7},{6,4},{7,5},{8,10},{9,11},{10,... | collective-permute-start | bytes 1179656 | tf_op jit(solution)/shard_map/ppermute | solution.py:36
  196.0 24.9 %all_to_all.43 = f32[32,1,24]{2,1,0:T(1,128)S(1)} all-to-all(f32[32,1,24]{2,1,0:T(1,128)S(1)} %bitcast.48), channel_id=1, replica_groups=mesh['x'=4,'z'=16,'c'=2,'y'=4] {'y','x','c'}, dimensions={0} | all-to-all | bytes 6144 | tf_op jit(solution)/shard_map/all_to_all | solution.py:363
  221.9 8.6 %all-to-all-start.6 = ((f32[16,8,128]{2,1,0:T(8,128)}), f32[16,8,128]{2,1,0:T(8,128)S(1)}, u32[]{:S(2)}, u32[]{:S(2)}) async-start(f32[16,8,128]{2,1,0:T(8,128)} %pad.4.clone), calls=%async_computation.6 | async-start | bytes 131072 | tf_op jit(solution)/shard_map/all_to_all | solution.py:368
  230.6 11.9 %last_step.1 = bf16[1,896,1024]{2,1,0:T(8,128)(2,1)} custom-call(s32[1]{0:T(128)} %bitcast.25.rank_ref, bf16[896,768]{1,0:T(8,128)(2,1)S(1)} %copy-done.1, bf16[192,2176]{1,0:T(8,128)(2,1)} %get-tuple-element.25.west_a, bf16[192,2176]{1,0:T(8,128)(2,1)S(1)} %collective-permute-done.6.west_b, bf16[192,2176]{1,0:T(8,128)(2,1)} %get-tuple-element.26.east_a, ...), custom_call_target="tpu_custom_call" | custom-call | tf_op jit(solution)/shard_map/last_step/pallas_call | solution.py:264
  (92 shorter events, 46.8 us)
Async XLA Ops:
  7.2 13.2 %copy-start.10 = (s32[128,8]{0,1:T(8,128)S(1)}, s32[128,8]{0,1:T(8,128)}, u32[]{:S(2)}) copy-start(s32[128,8]{0,1:T(8,128)} %param.9) | copy-start | bytes 12292
  7.2 13.4 %copy-start.11 = (bf16[128,8]{0,1:T(8,128)(2,1)S(1)}, bf16[128,8]{0,1:T(8,128)(2,1)}, u32[]{:S(2)}) copy-start(bf16[128,8]{0,1:T(8,128)(2,1)} %param.10) | copy-start | bytes 6148
  7.2 31.5 %copy-start.13 = (bf16[1,768,256]{2,1,0:T(8,128)(2,1)S(1)}, bf16[1,768,256]{2,1,0:T(8,128)(2,1)}, u32[]{:S(2)}) copy-start(bf16[1,768,256]{2,1,0:T(8,128)(2,1)} %param.12) | copy-start | bytes 1179652
  7.2 31.5 %copy-start.12 = (bf16[1,768,256]{2,1,0:T(8,128)(2,1)S(1)}, bf16[1,768,256]{2,1,0:T(8,128)(2,1)}, u32[]{:S(2)}) copy-start(bf16[1,768,256]{2,1,0:T(8,128)(2,1)} %param.13) | copy-start | bytes 1179652
  7.2 104.4 %all-gather.2.cloned.1.call-start = ((), (), s32[]{:S(2)}) async-start(), calls=%async_computation.7 | async-start | bytes 7798784 | tf_op jit(solution)/shard_map/all_gather | solution.py:295
  13.0 57.3 %collective-permute-start = (bf16[3584,256]{1,0:T(8,128)(2,1)}, bf16[3584,256]{1,0:T(8,128)(2,1)}, u32[]{:S(2)}, u32[]{:S(2)}) collective-permute-start(bf16[3584,256]{1,0:T(8,128)(2,1)} %bitcast.4), channel_id=1, source_target_pairs={{0,1},{1,2},{2,3},{3,0},{4,5},{5,6},{6,7},{7,4},{8,9},{9,10},{10,1... | collective-permute-start | bytes 5505032 | tf_op jit(solution)/shard_map/ppermute | solution.py:36
  17.0 57.8 %collective-permute-start.1 = (bf16[3584,256]{1,0:T(8,128)(2,1)}, bf16[3584,256]{1,0:T(8,128)(2,1)}, u32[]{:S(2)}, u32[]{:S(2)}) collective-permute-start(bf16[3584,256]{1,0:T(8,128)(2,1)} %bitcast.4), channel_id=1, source_target_pairs={{0,3},{1,0},{2,1},{3,2},{4,7},{5,4},{6,5},{7,6},{8,11},{9,8},{10,9... | collective-permute-start | bytes 5505032 | tf_op jit(solution)/shard_map/ppermute | solution.py:36
  23.7 26.4 %all-to-all-start = ((f32[16,2,48]{2,1,0:T(2,128)}), f32[16,2,48]{2,1,0:T(2,128)S(1)}, u32[]{:S(2)}, u32[]{:S(2)}) async-start(f32[16,2,48]{2,1,0:T(2,128)} %copy.61), calls=%async_computation | async-start | bytes 32768 | tf_op jit(solution)/shard_map/all_to_all | solution.py:312
  51.2 15.4 %all-to-all-start.2 = ((f32[32,1,24]{2,1,0:T(1,128)}), f32[32,1,24]{2,1,0:T(1,128)S(1)}, u32[]{:S(2)}, u32[]{:S(2)}) async-start(f32[32,1,24]{2,1,0:T(1,128)} %reshape.293), calls=%async_computation.2 | async-start | bytes 32768 | tf_op jit(solution)/shard_map/all_to_all | solution.py:321
  66.7 36.7 %all-to-all-start.1 = ((bf16[4,192,512]{2,1,0:T(8,128)(2,1)}), bf16[4,192,512]{2,1,0:T(8,128)(2,1)S(1)}, u32[]{:S(2)}, u32[]{:S(2)}) async-start(bf16[4,192,512]{2,1,0:T(8,128)(2,1)} %bitcast.13), calls=%async_computation.1 | async-start | bytes 1572864 | tf_op jit(solution)/shard_map/all_to_all | solution.py:338
  71.5 29.8 %collective-permute-start.2 = (bf16[1792,256]{1,0:T(8,128)(2,1)S(1)}, bf16[1792,256]{1,0:T(8,128)(2,1)S(1)}, u32[]{:S(2)}, u32[]{:S(2)}) collective-permute-start(bf16[1792,256]{1,0:T(8,128)(2,1)S(1)} %slice.28), channel_id=1, source_target_pairs={{0,1},{1,2},{2,3},{3,0},{4,5},{5,6},{6,7},{7,4},{8,9},{9,10},{10,1... | collective-permute-start | bytes 2752520 | tf_op jit(solution)/shard_map/ppermute | solution.py:36
  76.1 26.2 %collective-permute-start.3 = (bf16[1792,256]{1,0:T(8,128)(2,1)S(1)}, bf16[1792,256]{1,0:T(8,128)(2,1)S(1)}, u32[]{:S(2)}, u32[]{:S(2)}) collective-permute-start(bf16[1792,256]{1,0:T(8,128)(2,1)S(1)} %slice.29), channel_id=1, source_target_pairs={{0,3},{1,0},{2,1},{3,2},{4,7},{5,4},{6,5},{7,6},{8,11},{9,8},{10,9... | collective-permute-start | bytes 2752520 | tf_op jit(solution)/shard_map/ppermute | solution.py:36
  116.3 23.5 %all-to-all-start.3 = ((bf16[8,96,896]{2,1,0:T(8,128)(2,1)}), bf16[8,96,896]{2,1,0:T(8,128)(2,1)S(1)}, u32[]{:S(2)}, u32[]{:S(2)}) async-start(bf16[8,96,896]{2,1,0:T(8,128)(2,1)} %bitcast.17), calls=%async_computation.3 | async-start | bytes 2752512 | tf_op jit(solution)/shard_map/all_to_all | solution.py:346
  139.8 34.9 %all-to-all-start.4 = ((bf16[32,24,896]{2,1,0:T(8,128)(2,1)}), bf16[32,24,896]{2,1,0:T(8,128)(2,1)S(1)}, u32[]{:S(2)}, u32[]{:S(2)}) async-start(bf16[32,24,896]{2,1,0:T(8,128)(2,1)} %bitcast.19), calls=%async_computation.4 | async-start | bytes 2752512 | tf_op jit(solution)/shard_map/all_to_all | solution.py:354
  148.0 1.1 copy-start
  149.0 23.2 %collective-permute-start.4 = (bf16[576,384]{1,0:T(8,128)(2,1)}, bf16[576,384]{1,0:T(8,128)(2,1)S(1)}, u32[]{:S(2)}, u32[]{:S(2)}) collective-permute-start(bf16[576,384]{1,0:T(8,128)(2,1)} %get-tuple-element.21.low_a), channel_id=1, source_target_pairs={{0,1},{1,0},{2,3},{3,2},{4,5},{5,4},{6,7},{7,6},{8,9},{9,8},{10,11... | collective-permute-start | bytes 1327112 | tf_op jit(solution)/shard_map/ppermute | solution.py:61
  152.3 21.6 %collective-permute-start.5 = (bf16[576,384]{1,0:T(8,128)(2,1)}, bf16[576,384]{1,0:T(8,128)(2,1)S(1)}, u32[]{:S(2)}, u32[]{:S(2)}) collective-permute-start(bf16[576,384]{1,0:T(8,128)(2,1)} %get-tuple-element.22.high_a), channel_id=1, source_target_pairs={{0,3},{1,2},{2,1},{3,0},{4,7},{5,6},{6,5},{7,4},{8,11},{9,10},{10,... | collective-permute-start | bytes 1327112 | tf_op jit(solution)/shard_map/ppermute | solution.py:61
  174.7 1.0 copy-start.3
  177.7 52.9 %copy-start.1 = (bf16[896,768]{1,0:T(8,128)(2,1)S(1)}, bf16[896,768]{1,0:T(8,128)(2,1)}, u32[]{:S(2)}) copy-start(bf16[896,768]{1,0:T(8,128)(2,1)} %copy-done) | copy-start | bytes 4128772
  185.3 45.2 %collective-permute-start.6 = (bf16[192,2176]{1,0:T(8,128)(2,1)}, bf16[192,2176]{1,0:T(8,128)(2,1)S(1)}, u32[]{:S(2)}, u32[]{:S(2)}) collective-permute-start(bf16[192,2176]{1,0:T(8,128)(2,1)} %get-tuple-element.25.west_a), channel_id=1, source_target_pairs={{0,3},{1,2},{2,1},{3,0},{4,7},{5,6},{6,5},{7,4},{8,11},{9,10},{10,... | collective-permute-start | bytes 2506760 | tf_op jit(solution)/shard_map/ppermute | solution.py:61
  188.3 42.2 %collective-permute-start.7 = (bf16[192,2176]{1,0:T(8,128)(2,1)}, bf16[192,2176]{1,0:T(8,128)(2,1)S(1)}, u32[]{:S(2)}, u32[]{:S(2)}) collective-permute-start(bf16[192,2176]{1,0:T(8,128)(2,1)} %get-tuple-element.26.east_a), channel_id=1, source_target_pairs={{0,1},{1,0},{2,3},{3,2},{4,5},{5,4},{6,7},{7,6},{8,9},{9,8},{10,11... | collective-permute-start | bytes 2506760 | tf_op jit(solution)/shard_map/ppermute | solution.py:61
  190.3 40.2 %collective-permute-start.8 = (bf16[192,1024]{1,0:T(8,128)(2,1)}, bf16[192,1024]{1,0:T(8,128)(2,1)S(1)}, u32[]{:S(2)}, u32[]{:S(2)}) collective-permute-start(bf16[192,1024]{1,0:T(8,128)(2,1)} %get-tuple-element.27), channel_id=1, source_target_pairs={{0,2},{1,3},{2,0},{3,1},{4,6},{5,7},{6,4},{7,5},{8,10},{9,11},{10,... | collective-permute-start | bytes 1179656 | tf_op jit(solution)/shard_map/ppermute | solution.py:36
  221.9 20.5 %all-to-all-start.6 = ((f32[16,8,128]{2,1,0:T(8,128)}), f32[16,8,128]{2,1,0:T(8,128)S(1)}, u32[]{:S(2)}, u32[]{:S(2)}) async-start(f32[16,8,128]{2,1,0:T(8,128)} %pad.4.clone), calls=%async_computation.6 | async-start | bytes 131072 | tf_op jit(solution)/shard_map/all_to_all | solution.py:368
  230.5 12.0 %copy-start.9 = (s32[1024]{0:T(1024)S(1)}, s32[1024]{0:T(1024)}, u32[]{:S(2)}) copy-start(s32[1024]{0:T(1024)} %copy-done.8) | copy-start | bytes 12292
  (6 other events, 4.7 us)
Sparse Core Ops, SparseCore 0:
  10.1 101.4 all-gather.1

commit v4 on v3

--- a/solution.py
+++ b/solution.py
@@ -125,100 +125,72 @@
     )(recv)
 
 
-def hidden_kernel(
-    grads_ref, matrix_ref, saved_ref, weight_ref, low_a, low_b, high_a, high_b,
-    up_ref, west_ref, east_ref, dw_ref, rows_ref,
-):
-    parts, rows, feats = grads_ref.shape
-    width = matrix_ref.shape[2]
-    hidden_all = up_ref.shape[1]
-    half = low_a.shape[1]
+def hidden_kernel(grads_ref, matrix_ref, saved_ref, weight_ref, up_ref, dw_ref, hidden_ref):
+    blocks, depth, width = matrix_ref.shape
+    grads = jnp.concatenate([grads_ref[i] for i in range(grads_ref.shape[0])], axis=1)
+    matrix = jnp.concatenate([matrix_ref[j] for j in range(blocks)], axis=1)
+    share = dot(grads, matrix, ((1,), (0,)))
 
     @pl.when(pl.program_id(0) == 0)
     def _():
-        for part in range(parts):
-            rows_ref[:, part * feats : (part + 1) * feats] = grads_ref[part]
-        for one, two, out in ((low_a, low_b, west_ref), (high_a, high_b, east_ref)):
-            for i in range(3):
-                piece = one[i * rows : (i + 1) * rows].astype(f32)
-                piece = piece + two[i * rows : (i + 1) * rows].astype(f32)
-                first = hidden_all + i * half
-                out[:, first : first + half] = piece.astype(bf16)
-
-    hidden = dot(rows_ref[...], matrix_ref[0], ((1,), (0,)))
-    gate = saved_ref[0, :, :width].astype(f32)
-    up = saved_ref[0, :, width:].astype(f32)
-    act = gate / (1.0 + jnp.exp(-gate))
-    scaled = hidden * act
-    up_grad = (weight_ref[...] * scaled).astype(bf16)
-    place = pl.ds(pl.multiple_of(pl.program_id(0) * width, width), width)
-    up_ref[:, place] = up_grad
-    west_ref[:, place] = up_grad
-    east_ref[:, place] = up_grad
-    share = jnp.sum(scaled * up, axis=1, keepdims=True)
-
-    @pl.when(pl.program_id(0) == 0)
+        hidden_ref[...] = share
+
+    @pl.when(pl.program_id(0) == pl.num_programs(0) - 1)
     def _():
-        dw_ref[...] = share
-
-    @pl.when(pl.program_id(0) != 0)
-    def _():
-        dw_ref[...] += share
-
-
-def hidden_step(grads, matrix, saved, weight, sums):
+        dw = jnp.zeros((grads.shape[0], 1), f32)
+        for j in range(blocks):
+            lanes = slice(j * width, (j + 1) * width)
+            gate = saved_ref[j, :, :width].astype(f32)
+            up = saved_ref[j, :, width:].astype(f32)
+            act = gate / (1.0 + jnp.exp(-gate))
+            scaled = (hidden_ref[:, lanes] + share[:, lanes]) * act
+            up_ref[:, lanes] = (weight_ref[...] * scaled).astype(bf16)
+            dw = dw + jnp.sum(scaled * up, axis=1, keepdims=True)
+        dw_ref[...] = dw
+
+
+def hidden_step(grads, matrix, saved, weight):
     parts, rows, feats = grads.shape
     blocks, depth, width = matrix.shape
-    half = sums[0].shape[1]
-    packed = jax.ShapeDtypeStruct((rows, blocks * width + 3 * half), bf16)
     outs = [
         jax.ShapeDtypeStruct((rows, blocks * width), bf16),
-        packed,
-        packed,
         jax.ShapeDtypeStruct((rows, 1), f32),
     ]
     return pl.pallas_call(
         hidden_kernel,
-        grid=(blocks,),
+        grid=(2,),
         in_specs=[
-            pl.BlockSpec((parts, rows, feats), lambda j: (0, 0, 0)),
-            pl.BlockSpec((1, depth, width), lambda j: (j, 0, 0)),
-            pl.BlockSpec((1, rows, 2 * width), lambda j: (j, 0, 0)),
-            pl.BlockSpec((rows, 1), lambda j: (0, 0)),
-        ]
-        + [pl.BlockSpec(part.shape, lambda j: (0, 0)) for part in sums],
-        out_specs=[pl.BlockSpec(out.shape, lambda j: (0, 0)) for out in outs],
+            pl.BlockSpec((parts // 2, rows, feats), lambda k: (k, 0, 0)),
+            pl.BlockSpec((blocks, depth // 2, width), lambda k: (0, k, 0)),
+            pl.BlockSpec(saved.shape, lambda k: (0, 0, 0)),
+            pl.BlockSpec((rows, 1), lambda k: (0, 0)),
+        ],
+        out_specs=[pl.BlockSpec(out.shape, lambda k: (0, 0)) for out in outs],
         out_shape=outs,
-        scratch_shapes=[pltpu.VMEM((rows, depth), bf16)],
+        scratch_shapes=[pltpu.VMEM((rows, blocks * width), f32)],
         compiler_params=pltpu.CompilerParams(vmem_limit_bytes=VMEM),
         name="hidden_step",
-    )(grads, matrix, saved, weight, *sums)
+    )(grads, matrix, saved, weight)
 
 
 def last_kernel(
-    rank_ref, rows_t_ref, west_a, west_b, east_a, east_b, far_ref, out_ref,
-    up_ref, inner_ref, carried_ref, gram_ref, square_ref, poly_ref, start_ref,
+    rank_ref, rows_t_ref, low_a, low_b, high_a, high_b, own_ref, west_ref, east_ref, far_ref,
+    out_ref, up_ref, inner_ref, carried_ref, gram_ref, square_ref, poly_ref, start_ref,
 ):
     rank = rank_ref[0]
-    own = far_ref.shape[0]
+    own = own_ref.shape[0]
     slots, hidden = up_ref.shape
     feats = rows_t_ref.shape[0]
     half = slots // 2
     near = rank + 1 - 2 * lax.rem(rank, 2)
-    owners = ((rank, west_a), (3 - rank, west_b), (near, east_b), (3 - near, far_ref))
+    owners = ((rank, own_ref), (3 - rank, west_ref), (near, east_ref), (3 - near, far_ref))
     for owner, part in owners:
-        up_ref[pl.ds(pl.multiple_of(owner * own, own), own)] = part[:, :hidden]
-
-    def summed(one, two, i):
-        lanes = slice(hidden + i * half, hidden + (i + 1) * half)
-        return one[:, lanes].astype(f32) + two[:, lanes].astype(f32)
-
-    low = [summed(west_a, west_b, i) for i in range(3)]
-    high = [summed(east_a, east_b, i) for i in range(3)]
-    cross = jnp.concatenate([low[2], high[0]], axis=0)
-    for i in range(2):
-        inner_ref[i * own : (i + 1) * own, :half] = low[i].astype(bf16)
-        inner_ref[half + i * own : half + (i + 1) * own, half:] = high[1 + i].astype(bf16)
+        up_ref[pl.ds(pl.multiple_of(owner * own, own), own)] = part[...]
+    low = low_a[...].astype(f32) + low_b[...].astype(f32)
+    high = high_a[...].astype(f32) + high_b[...].astype(f32)
+    inner_ref[:half, :half] = low[:half].astype(bf16)
+    inner_ref[half:, half:] = high[half // 2 :].astype(bf16)
+    cross = jnp.concatenate([low[half:], high[: half // 2]], axis=0)
     inner_ref[:half, half:] = cross.astype(bf16)
     inner_ref[half:, :half] = cross.T.astype(bf16)
     norm = jnp.zeros((1, 1), f32)
@@ -257,13 +229,13 @@
         ).astype(bf16)
 
 
-def last_step(rank, rows_t, parts):
+def last_step(rank, rows_t, packs, ups):
     feats, slots = rows_t.shape
-    hidden = parts[-1].shape[1]
+    hidden = ups[0].shape[1]
     vmem = pl.BlockSpec(memory_space=pltpu.VMEM)
     return pl.pallas_call(
         last_kernel,
-        in_specs=[pl.BlockSpec(memory_space=pltpu.SMEM)] + [vmem] * 6,
+        in_specs=[pl.BlockSpec(memory_space=pltpu.SMEM)] + [vmem] * 9,
         out_specs=vmem,
         out_shape=jax.ShapeDtypeStruct((1, feats, hidden), bf16),
         scratch_shapes=[
@@ -277,7 +249,7 @@
         ],
         compiler_params=pltpu.CompilerParams(vmem_limit_bytes=VMEM),
         name="last_step",
-    )(rank, rows_t, *parts)
+    )(rank, rows_t, *packs, *ups)
 
 
 def on_device(tokens_in, out_grad, expert_ids, combine, down_weight, gate_saved, up_saved):
@@ -341,36 +313,41 @@
 
     column, matrix, saved, weight = lax.optimization_barrier((column, matrix, saved, weight))
     column = column.reshape(ny, zl * tok_rows, 2 * feats)
+    grad_send = pick_rows(index, column, near, 1, True, "pick_grads")
     token_send = pick_rows(index, column, near, 0, False, "pick_tokens")
-    grad_send = pick_rows(index, column, near, 1, True, "pick_grads")
+    beside, across = (lambda i: i ^ 1), (lambda i: ny - 1 - i)
+
+    grads = lax.all_to_all(
+        grad_send.reshape(ny * near, zl * CAP, feats), ("y", "x", "c"), 0, 0, tiled=True
+    ).reshape(ny, own_slots, feats)
+    token_send, grads = lax.optimization_barrier((token_send, grads))
+    up_own, slot_dw = hidden_step(grads, matrix, saved, weight)
+    ups = (up_own, swap(up_own, across), swap(up_own, beside), shift(up_own, 2))
+
     rows = lax.all_to_all(
         token_send.reshape(near, nz * CAP, feats), ("x", "c"), 0, 0, tiled=True
     ).reshape(near, ny, zl * CAP, feats)
+    rows, *ups = lax.optimization_barrier((rows, *ups))
     rows_t, low, high = inner_products(rows)
-    beside, across = (lambda i: i ^ 1), (lambda i: ny - 1 - i)
-    low_near, high_near = swap(low, beside), swap(high, across)
-
-    grad_send, _ = lax.optimization_barrier((grad_send, rows))
-    grads = lax.all_to_all(
-        grad_send.reshape(ny * near, zl * CAP, feats), ("y", "x", "c"), 0, 0, tiled=True
-    ).reshape(ny, own_slots, feats)
-    up_own, west, east, slot_dw = hidden_step(
-        grads, matrix, saved, weight, (low, low_near, high, high_near)
-    )
-    parts = (west, swap(west, across), east, swap(east, beside), shift(up_own, 2))
-
-    back = jnp.broadcast_to(slot_dw.reshape(1, near, zl * CAP), (ny, near, zl * CAP))
-    back = lax.all_to_all(
-        back.reshape(ny * near, zl * CAP), ("y", "x", "c"), 0, 0, tiled=True
-    )
-    back = back.reshape(ny, near, zl, CAP).transpose(0, 2, 1, 3).reshape(nz, near, CAP)
+    low = low + swap(low, beside)
+    high = high + swap(high, across)
+    packs = (low, swap(low, across), high, swap(high, beside))
+
+    back = slot_dw.reshape(near, zl, CAP).transpose(1, 0, 2)
     back = jnp.pad(back, ((0, 0), (0, 0), (0, 128 - CAP)))
-    back = lax.all_to_all(back, "z", 0, 0, tiled=True)
+    back = lax.dynamic_update_slice(
+        jnp.zeros((nz, near, 128), f32), back, (lax.axis_index("y") * zl, 0, 0)
+    )
+    back, rows_t = lax.optimization_barrier((back, rows_t))
+    back = lax.all_to_all(back, "z", 0, 0, tiled=True)[:, :, :CAP]
+    back = back.transpose(1, 0, 2).reshape(1, near, nz * CAP)
+    back = jnp.broadcast_to(back, (ny, near, nz * CAP)).reshape(ny * near, nz * CAP)
+    back = lax.all_to_all(back, ("y", "x", "c"), 0, 0, tiled=True)
 
     rank = lax.axis_index("y").reshape(1)
-    update = last_step(rank, rows_t, parts)
+    update = last_step(rank, rows_t, packs, ups)
     back, update = lax.optimization_barrier((back, update))
-    back = back[:, :, :CAP].reshape(-1)
+    back = jnp.sum(back.reshape(ny, near, nz, CAP), axis=0).transpose(1, 0, 2).reshape(-1)
     dcombine = jnp.sum(jnp.where(matches, back[:, None], 0.0), axis=0)
     dcombine = dcombine.reshape(tok_rows, top_count)
     return (update, dcombine)

time: 252 us -> 248 us (0.984)
  blocking collectives: 24.9 us -> 0 us
  starting transfers between devices: 76.8 us -> 95.2 us
  Pallas kernels: 30.6 us -> 25.9 us
  local copies, waits for them, and re-layouts: 32.8 us -> 37 us
    all_to_all x1 -> x0, blocking collectives: 24.9 us -> none  [on_device(): lax.all_to_all(back.reshape(ny * near, zl * CAP), ('y', 'x', 'c'), 0, 0,...]
    all_to_all x1, waiting for transfers between devices: 0.01 us -> 15.1 us  [on_device(): lax.all_to_all(grad_send.reshape(ny * near, zl * CAP, feats), ('y', 'x',...]
    all_to_all x1, waiting for transfers between devices: 13.8 us -> 0.01 us  [on_device(): lax.all_to_all(token_send.reshape(near, nz * CAP, feats), ('x', 'c'), 0,...]
    ppermute x4 -> x6, waiting for transfers between devices: 16.4 us -> 3.4 us  [swap(): return lax.ppermute(values, 'y', [(i, partner(i)) for i in range(size)])]
    all_to_all x1 -> x2, starting transfers between devices: 8.59 us -> 20 us  [the longest x1 11.4 us: on_device(): back = lax.all_to_all(back, ('y', 'x', 'c'), 0, 0, tiled=True)]
    ppermute x5, waiting for transfers between devices: 16.3 us -> 26 us  [shift(): lax.ppermute(values, 'y', [(i, (i + step) % size) for i in range(size)])]
    ppermute x4 -> x6, starting transfers between devices: 12 us -> 15.9 us  [swap(): return lax.ppermute(values, 'y', [(i, partner(i)) for i in range(size)])]
    unnamed x32 -> x36, local copies, waits for them, and re-layouts: 11.5 us -> 14.2 us
  transfers between devices with their start and end apart: 16 -> 19, of which waited for: 7 -> 8; matrix products, arithmetic and copies ran while one was open for 12% -> 13% of each run, Pallas kernels for 8% -> 8%
where the time goes in v4:
time: 248 us; the launch traced here: 246 us
  starting transfers between devices  95.2 us (38%)
  waiting for transfers between devices  65.5 us (26%)
  local copies, waits for them, and re-layouts  37 us (15%)
  Pallas kernels  25.9 us (10%)
  between operations  14.5 us (6%)
  other arithmetic  6.36 us (3%)
    ppermute x5, waiting for transfers between devices, shift(): lax.ppermute(values, 'y', [(i, (i + step) % size) for i in range(size)])  26 us
    ppermute x5, starting transfers between devices, shift(): lax.ppermute(values, 'y', [(i, (i + step) % size) for i in range(size)])  19.4 us
    ppermute x6, starting transfers between devices, swap(): return lax.ppermute(values, 'y', [(i, partner(i)) for i in range(size)])  15.9 us
    all_to_all x1, waiting for transfers between devices, on_device(): lax.all_to_all(grad_send.reshape(ny * near, zl * CAP, feats), ('y', 'x',...  15.1 us
    all_to_all x1, starting transfers between devices, on_device(): lax.all_to_all(jnp.stack([index_send.reshape(nz, near * CAP), weight_send...  14.9 us
    unnamed x36, local copies, waits for them, and re-layouts  14.2 us
    all_to_all x1, starting transfers between devices, on_device(): back = lax.all_to_all(back, ('y', 'x', 'c'), 0, 0, tiled=True)  11.4 us
    dynamic_update_slice x5, local copies, waits for them, and re-layouts, gather_weights(): whole = lax.dynamic_update_slice(whole, part[None], (place, row, 0))  10.7 us
  transfers between devices with their start and end apart: 19, of which 8 were waited for; matrix products, arithmetic and copies ran while one was open for 13% of the time, Pallas kernels for 8%

profile of v4, /device:TPU:1, one launch (start us, length us, event | category | flops | bytes accessed | tf_op | source)
XLA Modules:
  0.0 246.1 jit_solution(13205416640876320172)
XLA Ops:
  9.2 3.8 %copy.62 = bf16[1,256,3584]{1,2,0:T(8,128)(2,1)} copy(bf16[1,256,3584]{2,1,0:T(8,128)(2,1)} %param.11) | data formatting | bytes 3670016 | tf_op args[4]
  13.0 4.0 %collective-permute-start = (bf16[3584,256]{1,0:T(8,128)(2,1)}, bf16[3584,256]{1,0:T(8,128)(2,1)}, u32[]{:S(2)}, u32[]{:S(2)}) collective-permute-start(bf16[3584,256]{1,0:T(8,128)(2,1)} %bitcast.4), channel_id=1, source_target_pairs={{0,1},{1,2},{2,3},{3,0},{4,5},{5,6},{6,7},{7,4},{8,9},{9,10},{10,1... | collective-permute-start | bytes 5505032 | tf_op jit(solution)/shard_map/ppermute | solution.py:36
  17.0 3.4 %collective-permute-start.1 = (bf16[3584,256]{1,0:T(8,128)(2,1)}, bf16[3584,256]{1,0:T(8,128)(2,1)}, u32[]{:S(2)}, u32[]{:S(2)}) collective-permute-start(bf16[3584,256]{1,0:T(8,128)(2,1)} %bitcast.4), channel_id=1, source_target_pairs={{0,3},{1,0},{2,1},{3,2},{4,7},{5,4},{6,5},{7,6},{8,11},{9,8},{10,9... | collective-permute-start | bytes 5505032 | tf_op jit(solution)/shard_map/ppermute | solution.py:36
  23.1 14.9 %all-to-all-start = ((f32[16,2,48]{2,1,0:T(2,128)}), f32[16,2,48]{2,1,0:T(2,128)S(1)}, u32[]{:S(2)}, u32[]{:S(2)}) async-start(f32[16,2,48]{2,1,0:T(2,128)} %copy.58), calls=%async_computation | async-start | bytes 32768 | tf_op jit(solution)/shard_map/all_to_all | solution.py:284
  39.8 3.5 %broadcast_in_dim.81 = bf16[4,3584,256]{2,1,0:T(8,128)(2,1)} broadcast(bf16[]{:T(256)} %constant.167.clone.1), dimensions={} | broadcast | bytes 7340034 | tf_op jit(solution)/shard_map/broadcast_in_dim | solution.py:47
  50.7 8.5 %all-to-all-start.2 = ((f32[32,1,24]{2,1,0:T(1,128)}), f32[32,1,24]{2,1,0:T(1,128)S(1)}, u32[]{:S(2)}, u32[]{:S(2)}) async-start(f32[32,1,24]{2,1,0:T(1,128)} %reshape.292), calls=%async_computation.2 | async-start | bytes 32768 | tf_op jit(solution)/shard_map/all_to_all | solution.py:293
  59.7 6.4 %all-to-all-done.2 = f32[32,1,24]{2,1,0:T(1,128)S(1)} async-done(((f32[32,1,24]{2,1,0:T(1,128)}), f32[32,1,24]{2,1,0:T(1,128)S(1)}, u32[]{:S(2)}, u32[]{:S(2)}) %all-to-all-start.2) | async-done | bytes 3104 | tf_op jit(solution)/shard_map/all_to_all | solution.py:293
  66.1 3.5 %all-to-all-start.1 = ((bf16[4,192,512]{2,1,0:T(8,128)(2,1)}), bf16[4,192,512]{2,1,0:T(8,128)(2,1)S(1)}, u32[]{:S(2)}, u32[]{:S(2)}) async-start(bf16[4,192,512]{2,1,0:T(8,128)(2,1)} %bitcast.13), calls=%async_computation.1 | async-start | bytes 1572864 | tf_op jit(solution)/shard_map/all_to_all | solution.py:310
  84.5 16.3 %collective-permute-done.2 = bf16[1792,256]{1,0:T(8,128)(2,1)S(1)} collective-permute-done((bf16[1792,256]{1,0:T(8,128)(2,1)S(1)}, bf16[1792,256]{1,0:T(8,128)(2,1)S(1)}, u32[]{:S(2)}, u32[]{:S(2)}) %collective-permute-start.2) | collective-permute-done | bytes 917536 | tf_op jit(solution)/shard_map/ppermute | solution.py:36
  102.8 8.8 %all-gather.2.cloned.1.call-done = bf16[2048,1792]{1,0:T(8,128)(2,1)} async-done(((bf16[128,1792]{1,0:T(8,128)(2,1)}), bf16[2048,1792]{1,0:T(8,128)(2,1)}) %all-gather.2.cloned.1.call-update) | async-done | bytes 7340048 | tf_op jit(solution)/shard_map/all_gather | solution.py:267
  111.6 4.8 %pick_grads.1 = bf16[4,8,24,896]{3,2,1,0:T(8,128)(2,1)} custom-call(f32[4,192,1]{2,1,0:T(8,128)S(1)} %reshape.293.index_ref, bf16[4,512,1792]{2,1,0:T(8,128)(2,1)} %bitcast.53), custom_call_target="tpu_custom_call" | custom-call | tf_op jit(solution)/shard_map/pick_grads/pallas_call | solution.py:83
  116.3 7.5 %all-to-all-start.3 = ((bf16[32,24,896]{2,1,0:T(8,128)(2,1)}), bf16[32,24,896]{2,1,0:T(8,128)(2,1)S(1)}, u32[]{:S(2)}, u32[]{:S(2)}) async-start(bf16[32,24,896]{2,1,0:T(8,128)(2,1)} %bitcast.17), calls=%async_computation.3 | async-start | bytes 2752512 | tf_op jit(solution)/shard_map/all_to_all | solution.py:320
  123.9 4.7 %pick_tokens.1 = bf16[8,4,24,896]{3,2,1,0:T(8,128)(2,1)} custom-call(f32[4,192,1]{2,1,0:T(8,128)S(1)} %reshape.293.index_ref, bf16[4,512,1792]{2,1,0:T(8,128)(2,1)} %bitcast.54), custom_call_target="tpu_custom_call" | custom-call | tf_op jit(solution)/shard_map/pick_tokens/pallas_call | solution.py:83
  128.6 15.1 %all-to-all-done.3 = bf16[32,24,896]{2,1,0:T(8,128)(2,1)S(1)} async-done(((bf16[32,24,896]{2,1,0:T(8,128)(2,1)}), bf16[32,24,896]{2,1,0:T(8,128)(2,1)S(1)}, u32[]{:S(2)}, u32[]{:S(2)}) %all-to-all-start.3) | async-done | bytes 1376288 | tf_op jit(solution)/shard_map/all_to_all | solution.py:320
  143.8 5.4 %all-to-all-start.4 = ((bf16[8,96,896]{2,1,0:T(8,128)(2,1)}), bf16[8,96,896]{2,1,0:T(8,128)(2,1)S(1)}, u32[]{:S(2)}, u32[]{:S(2)}) async-start(bf16[8,96,896]{2,1,0:T(8,128)(2,1)} %bitcast.20), calls=%async_computation.4 | async-start | bytes 2752512 | tf_op jit(solution)/shard_map/all_to_all | solution.py:327
  150.8 4.6 %hidden_step.1 = (bf16[192,1024]{1,0:T(8,128)(2,1)S(1)}, f32[192,1]{1,0:T(8,128)S(1)}) custom-call(bf16[4,192,896]{2,1,0:T(8,128)(2,1)S(1)} %bitcast.51, bf16[4,3584,256]{2,1,0:T(8,128)(2,1)} %bitcast_dynamic-update-slice_fusion.3.matrix_ref, bf16[4,192,512]{2,1,0:T(8,128)(2,1)S(1)} %all-to-all-done.1.saved_ref, f32[192,1]{1,0:T(8,128)S(1)} %copy-done.2), custom_call_target="tpu_custom_call" | custom-call | tf_op jit(solution)/shard_map/hidden_step/pallas_call | solution.py:159
  160.1 5.5 %collective-permute-start.6 = (bf16[192,1024]{1,0:T(8,128)(2,1)S(1)}, bf16[192,1024]{1,0:T(8,128)(2,1)S(1)}, u32[]{:S(2)}, u32[]{:S(2)}) collective-permute-start(bf16[192,1024]{1,0:T(8,128)(2,1)S(1)} %get-tuple-element.36.own_ref), channel_id=1, source_target_pairs={{0,2},{1,3},{2,0},{3,1},{4,6},{5,7},{6,4},{7,5},{8,10},{9,11},{10,... | collective-permute-start | bytes 1179656 | tf_op jit(solution)/shard_map/ppermute | solution.py:36
  166.4 3.4 %collective-permute-done.4.west_ref = bf16[192,1024]{1,0:T(8,128)(2,1)S(1)} collective-permute-done((bf16[192,1024]{1,0:T(8,128)(2,1)S(1)}, bf16[192,1024]{1,0:T(8,128)(2,1)S(1)}, u32[]{:S(2)}, u32[]{:S(2)}) %collective-permute-start.4) | collective-permute-done | bytes 393248 | tf_op jit(solution)/shard_map/ppermute | solution.py:61
  171.4 9.7 %collective-permute-done.6.far_ref = bf16[192,1024]{1,0:T(8,128)(2,1)S(1)} collective-permute-done((bf16[192,1024]{1,0:T(8,128)(2,1)S(1)}, bf16[192,1024]{1,0:T(8,128)(2,1)S(1)}, u32[]{:S(2)}, u32[]{:S(2)}) %collective-permute-start.6) | collective-permute-done | bytes 393248 | tf_op jit(solution)/shard_map/ppermute | solution.py:36
  190.7 8.6 %all-to-all-start.5 = ((f32[16,8,128]{2,1,0:T(8,128)}), f32[16,8,128]{2,1,0:T(8,128)S(1)}, u32[]{:S(2)}, u32[]{:S(2)}) async-start(f32[16,8,128]{2,1,0:T(8,128)} %pad_dynamic-update-slice_fusion), calls=%async_computation.5 | async-start | bytes 131072 | tf_op jit(solution)/shard_map/all_to_all | solution.py:342
  199.4 3.4 %collective-permute-start.10 = (bf16[576,384]{1,0:T(8,128)(2,1)S(1)}, bf16[576,384]{1,0:T(8,128)(2,1)S(1)}, u32[]{:S(2)}, u32[]{:S(2)}) collective-permute-start(bf16[576,384]{1,0:T(8,128)(2,1)S(1)} %add.241.high_a), channel_id=1, source_target_pairs={{0,1},{1,0},{2,3},{3,2},{4,5},{5,4},{6,7},{7,6},{8,9},{9,8},{10,11... | collective-permute-start | bytes 1327112 | tf_op jit(solution)/shard_map/ppermute | solution.py:61
  203.9 4.5 %collective-permute-start.8 = (bf16[576,384]{1,0:T(8,128)(2,1)S(1)}, bf16[576,384]{1,0:T(8,128)(2,1)S(1)}, u32[]{:S(2)}, u32[]{:S(2)}) collective-permute-start(bf16[576,384]{1,0:T(8,128)(2,1)S(1)} %add.240.low_a), channel_id=1, source_target_pairs={{0,3},{1,2},{2,1},{3,0},{4,7},{5,6},{6,5},{7,4},{8,11},{9,10},{10,... | collective-permute-start | bytes 1327112 | tf_op jit(solution)/shard_map/ppermute | solution.py:61
  211.6 11.4 %all-to-all-start.6 = ((f32[32,1,96]{2,1,0:T(1,128)}), f32[32,1,96]{2,1,0:T(1,128)S(1)}, u32[]{:S(2)}, u32[]{:S(2)}) async-start(f32[32,1,96]{2,1,0:T(1,128)} %bitcast.24), calls=%async_computation.6 | async-start | bytes 32768 | tf_op jit(solution)/shard_map/all_to_all | solution.py:345
  227.0 10.4 %last_step.1 = bf16[1,896,1024]{2,1,0:T(8,128)(2,1)} custom-call(s32[1]{0:T(128)} %bitcast.26.rank_ref, bf16[896,768]{1,0:T(8,128)(2,1)S(1)} %copy-done.1, bf16[576,384]{1,0:T(8,128)(2,1)S(1)} %add.240.low_a, bf16[576,384]{1,0:T(8,128)(2,1)S(1)} %collective-permute-done.8.low_b, bf16[576,384]{1,0:T(8,128)(2,1)S(1)} %add.241.high_a, ...), custom_call_target="tpu_custom_call" | custom-call | tf_op jit(solution)/shard_map/last_step/pallas_call | solution.py:236
  (108 shorter events, 59.5 us)
Async XLA Ops:
  7.2 13.3 %copy-start.12 = (s32[128,8]{0,1:T(8,128)S(1)}, s32[128,8]{0,1:T(8,128)}, u32[]{:S(2)}) copy-start(s32[128,8]{0,1:T(8,128)} %param.9) | copy-start | bytes 12292
  7.2 13.4 %copy-start.13 = (bf16[128,8]{0,1:T(8,128)(2,1)S(1)}, bf16[128,8]{0,1:T(8,128)(2,1)}, u32[]{:S(2)}) copy-start(bf16[128,8]{0,1:T(8,128)(2,1)} %param.10) | copy-start | bytes 6148
  7.2 30.9 %copy-start.15 = (bf16[1,768,256]{2,1,0:T(8,128)(2,1)S(1)}, bf16[1,768,256]{2,1,0:T(8,128)(2,1)}, u32[]{:S(2)}) copy-start(bf16[1,768,256]{2,1,0:T(8,128)(2,1)} %param.12) | copy-start | bytes 1179652
  7.2 30.9 %copy-start.14 = (bf16[1,768,256]{2,1,0:T(8,128)(2,1)S(1)}, bf16[1,768,256]{2,1,0:T(8,128)(2,1)}, u32[]{:S(2)}) copy-start(bf16[1,768,256]{2,1,0:T(8,128)(2,1)} %param.13) | copy-start | bytes 1179652
  7.2 104.4 %all-gather.2.cloned.1.call-start = ((), (), s32[]{:S(2)}) async-start(), calls=%async_computation.7 | async-start | bytes 7798784 | tf_op jit(solution)/shard_map/all_gather | solution.py:267
  13.0 56.7 %collective-permute-start = (bf16[3584,256]{1,0:T(8,128)(2,1)}, bf16[3584,256]{1,0:T(8,128)(2,1)}, u32[]{:S(2)}, u32[]{:S(2)}) collective-permute-start(bf16[3584,256]{1,0:T(8,128)(2,1)} %bitcast.4), channel_id=1, source_target_pairs={{0,1},{1,2},{2,3},{3,0},{4,5},{5,6},{6,7},{7,4},{8,9},{9,10},{10,1... | collective-permute-start | bytes 5505032 | tf_op jit(solution)/shard_map/ppermute | solution.py:36
  17.0 57.2 %collective-permute-start.1 = (bf16[3584,256]{1,0:T(8,128)(2,1)}, bf16[3584,256]{1,0:T(8,128)(2,1)}, u32[]{:S(2)}, u32[]{:S(2)}) collective-permute-start(bf16[3584,256]{1,0:T(8,128)(2,1)} %bitcast.4), channel_id=1, source_target_pairs={{0,3},{1,0},{2,1},{3,2},{4,7},{5,4},{6,5},{7,6},{8,11},{9,8},{10,9... | collective-permute-start | bytes 5505032 | tf_op jit(solution)/shard_map/ppermute | solution.py:36
  23.1 26.4 %all-to-all-start = ((f32[16,2,48]{2,1,0:T(2,128)}), f32[16,2,48]{2,1,0:T(2,128)S(1)}, u32[]{:S(2)}, u32[]{:S(2)}) async-start(f32[16,2,48]{2,1,0:T(2,128)} %copy.58), calls=%async_computation | async-start | bytes 32768 | tf_op jit(solution)/shard_map/all_to_all | solution.py:284
  50.7 15.4 %all-to-all-start.2 = ((f32[32,1,24]{2,1,0:T(1,128)}), f32[32,1,24]{2,1,0:T(1,128)S(1)}, u32[]{:S(2)}, u32[]{:S(2)}) async-start(f32[32,1,24]{2,1,0:T(1,128)} %reshape.292), calls=%async_computation.2 | async-start | bytes 32768 | tf_op jit(solution)/shard_map/all_to_all | solution.py:293
  66.1 36.7 %all-to-all-start.1 = ((bf16[4,192,512]{2,1,0:T(8,128)(2,1)}), bf16[4,192,512]{2,1,0:T(8,128)(2,1)S(1)}, u32[]{:S(2)}, u32[]{:S(2)}) async-start(bf16[4,192,512]{2,1,0:T(8,128)(2,1)} %bitcast.13), calls=%async_computation.1 | async-start | bytes 1572864 | tf_op jit(solution)/shard_map/all_to_all | solution.py:310
  71.0 29.8 %collective-permute-start.2 = (bf16[1792,256]{1,0:T(8,128)(2,1)S(1)}, bf16[1792,256]{1,0:T(8,128)(2,1)S(1)}, u32[]{:S(2)}, u32[]{:S(2)}) collective-permute-start(bf16[1792,256]{1,0:T(8,128)(2,1)S(1)} %slice.28), channel_id=1, source_target_pairs={{0,1},{1,2},{2,3},{3,0},{4,5},{5,6},{6,7},{7,4},{8,9},{9,10},{10,1... | collective-permute-start | bytes 2752520 | tf_op jit(solution)/shard_map/ppermute | solution.py:36
  75.6 26.2 %collective-permute-start.3 = (bf16[1792,256]{1,0:T(8,128)(2,1)S(1)}, bf16[1792,256]{1,0:T(8,128)(2,1)S(1)}, u32[]{:S(2)}, u32[]{:S(2)}) collective-permute-start(bf16[1792,256]{1,0:T(8,128)(2,1)S(1)} %slice.29), channel_id=1, source_target_pairs={{0,3},{1,0},{2,1},{3,2},{4,7},{5,4},{6,5},{7,6},{8,11},{9,8},{10,9... | collective-permute-start | bytes 2752520 | tf_op jit(solution)/shard_map/ppermute | solution.py:36
  116.3 27.4 %all-to-all-start.3 = ((bf16[32,24,896]{2,1,0:T(8,128)(2,1)}), bf16[32,24,896]{2,1,0:T(8,128)(2,1)S(1)}, u32[]{:S(2)}, u32[]{:S(2)}) async-start(bf16[32,24,896]{2,1,0:T(8,128)(2,1)} %bitcast.17), calls=%async_computation.3 | async-start | bytes 2752512 | tf_op jit(solution)/shard_map/all_to_all | solution.py:320
  143.8 38.1 %all-to-all-start.4 = ((bf16[8,96,896]{2,1,0:T(8,128)(2,1)}), bf16[8,96,896]{2,1,0:T(8,128)(2,1)S(1)}, u32[]{:S(2)}, u32[]{:S(2)}) async-start(bf16[8,96,896]{2,1,0:T(8,128)(2,1)} %bitcast.20), calls=%async_computation.4 | async-start | bytes 2752512 | tf_op jit(solution)/shard_map/all_to_all | solution.py:327
  156.1 13.8 %collective-permute-start.4 = (bf16[192,1024]{1,0:T(8,128)(2,1)S(1)}, bf16[192,1024]{1,0:T(8,128)(2,1)S(1)}, u32[]{:S(2)}, u32[]{:S(2)}) collective-permute-start(bf16[192,1024]{1,0:T(8,128)(2,1)S(1)} %get-tuple-element.36.own_ref), channel_id=1, source_target_pairs={{0,3},{1,2},{2,1},{3,0},{4,7},{5,6},{6,5},{7,4},{8,11},{9,10},{10,... | collective-permute-start | bytes 1179656 | tf_op jit(solution)/shard_map/ppermute | solution.py:61
  158.0 12.6 %collective-permute-start.5 = (bf16[192,1024]{1,0:T(8,128)(2,1)S(1)}, bf16[192,1024]{1,0:T(8,128)(2,1)S(1)}, u32[]{:S(2)}, u32[]{:S(2)}) collective-permute-start(bf16[192,1024]{1,0:T(8,128)(2,1)S(1)} %get-tuple-element.36.own_ref), channel_id=1, source_target_pairs={{0,1},{1,0},{2,3},{3,2},{4,5},{5,4},{6,7},{7,6},{8,9},{9,8},{10,11... | collective-permute-start | bytes 1179656 | tf_op jit(solution)/shard_map/ppermute | solution.py:61
  160.1 20.9 %collective-permute-start.6 = (bf16[192,1024]{1,0:T(8,128)(2,1)S(1)}, bf16[192,1024]{1,0:T(8,128)(2,1)S(1)}, u32[]{:S(2)}, u32[]{:S(2)}) collective-permute-start(bf16[192,1024]{1,0:T(8,128)(2,1)S(1)} %get-tuple-element.36.own_ref), channel_id=1, source_target_pairs={{0,2},{1,3},{2,0},{3,1},{4,6},{5,7},{6,4},{7,5},{8,10},{9,11},{10,... | collective-permute-start | bytes 1179656 | tf_op jit(solution)/shard_map/ppermute | solution.py:36
  184.3 38.7 %copy-start.1 = (bf16[896,768]{1,0:T(8,128)(2,1)S(1)}, bf16[896,768]{1,0:T(8,128)(2,1)}, u32[]{:S(2)}) copy-start(bf16[896,768]{1,0:T(8,128)(2,1)} %copy-done) | copy-start | bytes 4128772
  184.3 15.0 %collective-permute-start.9 = (bf16[576,384]{1,0:T(8,128)(2,1)S(1)}, bf16[576,384]{1,0:T(8,128)(2,1)S(1)}, u32[]{:S(2)}, u32[]{:S(2)}) collective-permute-start(bf16[576,384]{1,0:T(8,128)(2,1)S(1)} %get-tuple-element.35), channel_id=1, source_target_pairs={{0,3},{1,2},{2,1},{3,0},{4,7},{5,6},{6,5},{7,4},{8,11},{9,10},{10,... | collective-permute-start | bytes 1327112 | tf_op jit(solution)/shard_map/ppermute | solution.py:61
  186.4 16.4 %collective-permute-start.7 = (bf16[576,384]{1,0:T(8,128)(2,1)S(1)}, bf16[576,384]{1,0:T(8,128)(2,1)}, u32[]{:S(2)}, u32[]{:S(2)}) collective-permute-start(bf16[576,384]{1,0:T(8,128)(2,1)S(1)} %get-tuple-element.34), channel_id=1, source_target_pairs={{0,1},{1,0},{2,3},{3,2},{4,5},{5,4},{6,7},{7,6},{8,9},{9,8},{10,11... | collective-permute-start | bytes 1327112 | tf_op jit(solution)/shard_map/ppermute | solution.py:61
  190.7 20.2 %all-to-all-start.5 = ((f32[16,8,128]{2,1,0:T(8,128)}), f32[16,8,128]{2,1,0:T(8,128)S(1)}, u32[]{:S(2)}, u32[]{:S(2)}) async-start(f32[16,8,128]{2,1,0:T(8,128)} %pad_dynamic-update-slice_fusion), calls=%async_computation.5 | async-start | bytes 131072 | tf_op jit(solution)/shard_map/all_to_all | solution.py:342
  199.4 23.6 %collective-permute-start.10 = (bf16[576,384]{1,0:T(8,128)(2,1)S(1)}, bf16[576,384]{1,0:T(8,128)(2,1)S(1)}, u32[]{:S(2)}, u32[]{:S(2)}) collective-permute-start(bf16[576,384]{1,0:T(8,128)(2,1)S(1)} %add.241.high_a), channel_id=1, source_target_pairs={{0,1},{1,0},{2,3},{3,2},{4,5},{5,4},{6,7},{7,6},{8,9},{9,8},{10,11... | collective-permute-start | bytes 1327112 | tf_op jit(solution)/shard_map/ppermute | solution.py:61
  203.9 19.1 %collective-permute-start.8 = (bf16[576,384]{1,0:T(8,128)(2,1)S(1)}, bf16[576,384]{1,0:T(8,128)(2,1)S(1)}, u32[]{:S(2)}, u32[]{:S(2)}) collective-permute-start(bf16[576,384]{1,0:T(8,128)(2,1)S(1)} %add.240.low_a), channel_id=1, source_target_pairs={{0,3},{1,2},{2,1},{3,0},{4,7},{5,6},{6,5},{7,4},{8,11},{9,10},{10,... | collective-permute-start | bytes 1327112 | tf_op jit(solution)/shard_map/ppermute | solution.py:61
  211.6 25.9 %all-to-all-start.6 = ((f32[32,1,96]{2,1,0:T(1,128)}), f32[32,1,96]{2,1,0:T(1,128)S(1)}, u32[]{:S(2)}, u32[]{:S(2)}) async-start(f32[32,1,96]{2,1,0:T(1,128)} %bitcast.24), calls=%async_computation.6 | async-start | bytes 32768 | tf_op jit(solution)/shard_map/all_to_all | solution.py:345
  (11 other events, 9.7 us)
Sparse Core Ops, SparseCore 0:
  10.1 101.4 all-gather.1

commit v5 on v4

--- a/solution.py
+++ b/solution.py
@@ -17,7 +17,7 @@
 poly_fifth = 17.300387312530933
 
 f32, bf16 = jnp.float32, jnp.bfloat16
-VMEM = 48 * 1024 * 1024
+MIB = 1024 * 1024
 
 
 def dot(a, b, contract):
@@ -89,43 +89,48 @@
         ],
         out_specs=pl.BlockSpec(block, place),
         out_shape=jax.ShapeDtypeStruct(shape, bf16),
-        compiler_params=pltpu.CompilerParams(vmem_limit_bytes=VMEM),
+        compiler_params=pltpu.CompilerParams(vmem_limit_bytes=48 * MIB),
         name=name,
     )(index, column)
 
 
-def inner_kernel(recv_ref, rows_t_ref, low_ref, high_ref, rows_ref):
+def inner_kernel(recv_ref, west_ref, east_ref, rows_t_ref, low_ref, high_ref, rows_ref):
     near, quarters, piece, feats = recv_ref.shape
-    own = near * piece
+    own, hidden = west_ref.shape
     for q in range(quarters):
         rows_ref[q * own : (q + 1) * own] = (
             recv_ref[:, q].astype(f32).reshape(own, feats).astype(bf16)
         )
-    half = quarters * own // 2
+    half = 2 * own
     top, end = rows_ref[:half], rows_ref[half:]
-    low_ref[:half] = dot(top, top, ((1,), (1,))).astype(bf16)
+    first = dot(top, top, ((1,), (1,))).astype(bf16)
     cross = dot(top, end, ((1,), (1,))).astype(bf16)
-    low_ref[half:] = cross[: half // 2]
-    high_ref[: half // 2] = cross[half // 2 :]
-    high_ref[half // 2 :] = dot(end, end, ((1,), (1,))).astype(bf16)
+    last = dot(end, end, ((1,), (1,))).astype(bf16)
+    low_ref[:, :half] = first[:own]
+    low_ref[:, half : 2 * half] = first[own:]
+    low_ref[:, 2 * half : 3 * half] = cross[:own]
+    high_ref[:, :half] = cross[own:]
+    high_ref[:, half : 2 * half] = last[:own]
+    high_ref[:, 2 * half : 3 * half] = last[own:]
+    low_ref[:, 3 * half :] = west_ref[:, : hidden // 2]
+    high_ref[:, 3 * half :] = east_ref[:, hidden // 2 :]
     rows_t_ref[...] = rows_ref[...].T
 
 
-def inner_products(recv):
+def inner_products(recv, west, east):
     near, quarters, piece, feats = recv.shape
-    slots = near * quarters * piece
-    half = slots // 2
-    pack = jax.ShapeDtypeStruct((half + half // 2, half), bf16)
+    own, hidden = west.shape
+    pack = jax.ShapeDtypeStruct((own, 6 * own + hidden // 2), bf16)
     return pl.pallas_call(
         inner_kernel,
-        out_shape=[jax.ShapeDtypeStruct((feats, slots), bf16), pack, pack],
-        scratch_shapes=[pltpu.VMEM((slots, feats), bf16)],
-        compiler_params=pltpu.CompilerParams(vmem_limit_bytes=VMEM),
+        out_shape=[pltpu.HBM((feats, quarters * own), bf16), pack, pack],
+        scratch_shapes=[pltpu.VMEM((quarters * own, feats), bf16)],
+        compiler_params=pltpu.CompilerParams(vmem_limit_bytes=20 * MIB),
         name="inner_products",
-    )(recv)
-
-
-def hidden_kernel(grads_ref, matrix_ref, saved_ref, weight_ref, up_ref, dw_ref, hidden_ref):
+    )(recv, west, east)
+
+
+def hidden_kernel(grads_ref, matrix_ref, out_act_ref, dw_act_ref, up_ref, dw_ref, hidden_ref):
     blocks, depth, width = matrix_ref.shape
     grads = jnp.concatenate([grads_ref[i] for i in range(grads_ref.shape[0])], axis=1)
     matrix = jnp.concatenate([matrix_ref[j] for j in range(blocks)], axis=1)
@@ -140,20 +145,17 @@
         dw = jnp.zeros((grads.shape[0], 1), f32)
         for j in range(blocks):
             lanes = slice(j * width, (j + 1) * width)
-            gate = saved_ref[j, :, :width].astype(f32)
-            up = saved_ref[j, :, width:].astype(f32)
-            act = gate / (1.0 + jnp.exp(-gate))
-            scaled = (hidden_ref[:, lanes] + share[:, lanes]) * act
-            up_ref[:, lanes] = (weight_ref[...] * scaled).astype(bf16)
-            dw = dw + jnp.sum(scaled * up, axis=1, keepdims=True)
+            hidden = hidden_ref[:, lanes] + share[:, lanes]
+            up_ref[:, lanes] = (hidden * out_act_ref[j]).astype(bf16)
+            dw = dw + jnp.sum(hidden * dw_act_ref[j], axis=1, keepdims=True)
         dw_ref[...] = dw
 
 
-def hidden_step(grads, matrix, saved, weight):
+def hidden_step(grads, matrix, out_act, dw_act):
     parts, rows, feats = grads.shape
     blocks, depth, width = matrix.shape
     outs = [
-        jax.ShapeDtypeStruct((rows, blocks * width), bf16),
+        pltpu.HBM((rows, blocks * width), bf16),
         jax.ShapeDtypeStruct((rows, 1), f32),
     ]
     return pl.pallas_call(
@@ -162,37 +164,54 @@
         in_specs=[
             pl.BlockSpec((parts // 2, rows, feats), lambda k: (k, 0, 0)),
             pl.BlockSpec((blocks, depth // 2, width), lambda k: (0, k, 0)),
-            pl.BlockSpec(saved.shape, lambda k: (0, 0, 0)),
-            pl.BlockSpec((rows, 1), lambda k: (0, 0)),
+            pl.BlockSpec(out_act.shape, lambda k: (0, 0, 0)),
+            pl.BlockSpec(dw_act.shape, lambda k: (0, 0, 0)),
         ],
         out_specs=[pl.BlockSpec(out.shape, lambda k: (0, 0)) for out in outs],
         out_shape=outs,
         scratch_shapes=[pltpu.VMEM((rows, blocks * width), f32)],
-        compiler_params=pltpu.CompilerParams(vmem_limit_bytes=VMEM),
+        compiler_params=pltpu.CompilerParams(vmem_limit_bytes=28 * MIB),
         name="hidden_step",
-    )(grads, matrix, saved, weight)
+    )(grads, matrix, out_act, dw_act)
 
 
 def last_kernel(
-    rank_ref, rows_t_ref, low_a, low_b, high_a, high_b, own_ref, west_ref, east_ref, far_ref,
-    out_ref, up_ref, inner_ref, carried_ref, gram_ref, square_ref, poly_ref, start_ref,
+    rank_ref, rows_t_hbm, own_hbm, low_a, low_b, high_a, high_b, west_ref, east_ref,
+    far_low, far_high, out_ref,
+    up_ref, inner_ref, carried_ref, gram_ref, square_ref, poly_ref, start_ref, rows_t_ref,
+    own_sem, rows_sem,
 ):
     rank = rank_ref[0]
-    own = own_ref.shape[0]
-    slots, hidden = up_ref.shape
-    feats = rows_t_ref.shape[0]
+    own, hidden = west_ref.shape
+    feats, slots = rows_t_ref.shape
     half = slots // 2
     near = rank + 1 - 2 * lax.rem(rank, 2)
-    owners = ((rank, own_ref), (3 - rank, west_ref), (near, east_ref), (3 - near, far_ref))
-    for owner, part in owners:
-        up_ref[pl.ds(pl.multiple_of(owner * own, own), own)] = part[...]
-    low = low_a[...].astype(f32) + low_b[...].astype(f32)
-    high = high_a[...].astype(f32) + high_b[...].astype(f32)
-    inner_ref[:half, :half] = low[:half].astype(bf16)
-    inner_ref[half:, half:] = high[half // 2 :].astype(bf16)
-    cross = jnp.concatenate([low[half:], high[: half // 2]], axis=0)
+
+    def owned(owner):
+        return pl.ds(pl.multiple_of(owner * own, own), own)
+
+    own_copy = pltpu.make_async_copy(own_hbm, up_ref.at[owned(rank)], own_sem)
+    rows_copy = pltpu.make_async_copy(rows_t_hbm, rows_t_ref, rows_sem)
+    own_copy.start()
+    rows_copy.start()
+    for owner, part in ((3 - rank, west_ref), (near, east_ref)):
+        up_ref[owned(owner)] = part[...]
+    up_ref[owned(3 - near), : hidden // 2] = far_low[:, 3 * half :]
+    up_ref[owned(3 - near), hidden // 2 :] = far_high[:, 3 * half :]
+
+    def summed(one, two, i):
+        lanes = slice(i * half, (i + 1) * half)
+        return one[:, lanes].astype(f32) + two[:, lanes].astype(f32)
+
+    low = [summed(low_a, low_b, i) for i in range(3)]
+    high = [summed(high_a, high_b, i) for i in range(3)]
+    cross = jnp.concatenate([low[2], high[0]], axis=0)
+    for i in range(2):
+        inner_ref[i * own : (i + 1) * own, :half] = low[i].astype(bf16)
+        inner_ref[half + i * own : half + (i + 1) * own, half:] = high[1 + i].astype(bf16)
     inner_ref[:half, half:] = cross.astype(bf16)
     inner_ref[half:, :half] = cross.T.astype(bf16)
+    own_copy.wait()
     norm = jnp.zeros((1, 1), f32)
     step = slots // 3
     for i in range(0, slots, step):
@@ -210,6 +229,7 @@
         quartic = quartic + total(square * square)
         square_ref[i : i + step] = square
     rows = feats // 4
+    rows_copy.wait()
     for i in range(0, feats, rows):
         gradient = dot(rows_t_ref[i : i + rows], up_ref[...], ((1,), (0,)))
         start_ref[i : i + rows] = (gradient * scale).astype(bf16)
@@ -229,14 +249,14 @@
         ).astype(bf16)
 
 
-def last_step(rank, rows_t, packs, ups):
+def last_step(rank, rows_t, own, packs, ups):
     feats, slots = rows_t.shape
-    hidden = ups[0].shape[1]
-    vmem = pl.BlockSpec(memory_space=pltpu.VMEM)
+    hidden = own.shape[1]
     return pl.pallas_call(
         last_kernel,
-        in_specs=[pl.BlockSpec(memory_space=pltpu.SMEM)] + [vmem] * 9,
-        out_specs=vmem,
+        in_specs=[pl.BlockSpec(memory_space=pltpu.SMEM)]
+        + [pl.BlockSpec(memory_space=pltpu.HBM)] * 2
+        + [pl.BlockSpec()] * 8,
         out_shape=jax.ShapeDtypeStruct((1, feats, hidden), bf16),
         scratch_shapes=[
             pltpu.VMEM((slots, hidden), bf16),
@@ -246,10 +266,13 @@
             pltpu.VMEM((hidden, hidden), f32),
             pltpu.VMEM((hidden, hidden), bf16),
             pltpu.VMEM((feats, hidden), bf16),
+            pltpu.VMEM((feats, slots), bf16),
+            pltpu.SemaphoreType.DMA,
+            pltpu.SemaphoreType.DMA,
         ],
-        compiler_params=pltpu.CompilerParams(vmem_limit_bytes=VMEM),
+        compiler_params=pltpu.CompilerParams(vmem_limit_bytes=56 * MIB),
         name="last_step",
-    )(rank, rows_t, *packs, *ups)
+    )(rank, rows_t, own, *packs, *ups)
 
 
 def on_device(tokens_in, out_grad, expert_ids, combine, down_weight, gate_saved, up_saved):
@@ -311,7 +334,10 @@
         saved.reshape(ny, own_slots, 2 * hidden_part), "y", 0, 0, tiled=True
     )
 
-    column, matrix, saved, weight = lax.optimization_barrier((column, matrix, saved, weight))
+    gate, up = saved[:, :, :hidden_part].astype(f32), saved[:, :, hidden_part:].astype(f32)
+    act = jax.nn.silu(gate)
+    out_act, dw_act = act * weight[None], act * up
+    column, matrix, out_act, dw_act = lax.optimization_barrier((column, matrix, out_act, dw_act))
     column = column.reshape(ny, zl * tok_rows, 2 * feats)
     grad_send = pick_rows(index, column, near, 1, True, "pick_grads")
     token_send = pick_rows(index, column, near, 0, False, "pick_tokens")
@@ -321,17 +347,18 @@
         grad_send.reshape(ny * near, zl * CAP, feats), ("y", "x", "c"), 0, 0, tiled=True
     ).reshape(ny, own_slots, feats)
     token_send, grads = lax.optimization_barrier((token_send, grads))
-    up_own, slot_dw = hidden_step(grads, matrix, saved, weight)
-    ups = (up_own, swap(up_own, across), swap(up_own, beside), shift(up_own, 2))
+    up_own, slot_dw = hidden_step(grads, matrix, out_act, dw_act)
+    west, east = swap(up_own, across), swap(up_own, beside)
 
     rows = lax.all_to_all(
         token_send.reshape(near, nz * CAP, feats), ("x", "c"), 0, 0, tiled=True
     ).reshape(near, ny, zl * CAP, feats)
-    rows, *ups = lax.optimization_barrier((rows, *ups))
-    rows_t, low, high = inner_products(rows)
-    low = low + swap(low, beside)
-    high = high + swap(high, across)
+    rows_t, low, high = inner_products(rows, west, east)
+    size = 6 * own_slots
+    low_near, high_near = swap(low, beside), swap(high, across)
+    low, high = low[:, :size] + low_near[:, :size], high[:, :size] + high_near[:, :size]
     packs = (low, swap(low, across), high, swap(high, beside))
+    ups = (west, east, low_near, high_near)
 
     back = slot_dw.reshape(near, zl, CAP).transpose(1, 0, 2)
     back = jnp.pad(back, ((0, 0), (0, 0), (0, 128 - CAP)))
@@ -345,7 +372,7 @@
     back = lax.all_to_all(back, ("y", "x", "c"), 0, 0, tiled=True)
 
     rank = lax.axis_index("y").reshape(1)
-    update = last_step(rank, rows_t, packs, ups)
+    update = last_step(rank, rows_t, up_own, packs, ups)
     back, update = lax.optimization_barrier((back, update))
     back = jnp.sum(back.reshape(ny, near, nz, CAP), axis=0).transpose(1, 0, 2).reshape(-1)
     dcombine = jnp.sum(jnp.where(matches, back[:, None], 0.0), axis=0)

time: 248 us -> 240 us (0.968)
  local copies, waits for them, and re-layouts: 37 us -> 29.1 us
  Pallas kernels: 25.9 us -> 30.7 us
  starting transfers between devices: 95.2 us -> 90.8 us
    ppermute x5 -> x4, waiting for transfers between devices: 26 us -> 11.3 us  [shift(): lax.ppermute(values, 'y', [(i, (i + step) % size) for i in range(size)])]
    all_to_all x1, waiting for transfers between devices: 3.29 us -> 11.4 us  [on_device(): lax.all_to_all(jnp.stack([index_send.reshape(nz, near * CAP), weight_send...]
    all_gather x1, waiting for transfers between devices: 8.78 us -> 1.14 us  [on_device(): lax.all_gather(jnp.concatenate([tokens_in, out_grad], axis=1), 'z', axis=...]
    unnamed x36 -> x28, local copies, waits for them, and re-layouts: 14.2 us -> 7.1 us
    ppermute x6, waiting for transfers between devices: 3.4 us -> 10.4 us  [swap(): return lax.ppermute(values, 'y', [(i, partner(i)) for i in range(size)])]
    ppermute x5 -> x4, starting transfers between devices: 19.4 us -> 13.9 us  [shift(): lax.ppermute(values, 'y', [(i, (i + step) % size) for i in range(size)])]
    all_to_all x1, waiting for transfers between devices: 0.01 us -> 4.6 us  [on_device(): lax.all_to_all(saved.reshape(ny, own_slots, 2 * hidden_part), 'y', 0, 0,...]
    all_to_all x1, starting transfers between devices: 8.59 us -> 12.1 us  [on_device(): back = lax.all_to_all(back, 'z', 0, 0, tiled=True)[:, :, :CAP]]
  transfers between devices with their start and end apart: 19 -> 18, of which waited for: 8 -> 10; matrix products, arithmetic and copies ran while one was open for 13% -> 14% of each run, Pallas kernels for 8% -> 10%
where the time goes in v5:
time: 240 us; the launch traced here: 238 us
  starting transfers between devices  90.8 us (38%)
  waiting for transfers between devices  63.1 us (26%)
  Pallas kernels  30.7 us (13%)
  local copies, waits for them, and re-layouts  29.1 us (12%)
  between operations  14.5 us (6%)
  other arithmetic  8.45 us (4%)
    ppermute x6, starting transfers between devices, swap(): return lax.ppermute(values, 'y', [(i, partner(i)) for i in range(size)])  15.8 us
    all_to_all x1, waiting for transfers between devices, on_device(): lax.all_to_all(grad_send.reshape(ny * near, zl * CAP, feats), ('y', 'x',...  15.1 us
    all_to_all x1, starting transfers between devices, on_device(): lax.all_to_all(jnp.stack([index_send.reshape(nz, near * CAP), weight_send...  14.9 us
    ppermute x4, starting transfers between devices, shift(): lax.ppermute(values, 'y', [(i, (i + step) % size) for i in range(size)])  13.9 us
    pallas_call x1, Pallas kernels, last_step(): pl.pallas_call(last_kernel, in_specs=[pl.BlockSpec(memory_space=pltpu.SME...  13.6 us
    all_to_all x1, starting transfers between devices, on_device(): back = lax.all_to_all(back, 'z', 0, 0, tiled=True)[:, :, :CAP]  12.1 us
    all_to_all x1, waiting for transfers between devices, on_device(): lax.all_to_all(jnp.stack([index_send.reshape(nz, near * CAP), weight_send...  11.4 us
    ppermute x4, waiting for transfers between devices, shift(): lax.ppermute(values, 'y', [(i, (i + step) % size) for i in range(size)])  11.3 us
  transfers between devices with their start and end apart: 18, of which 10 were waited for; matrix products, arithmetic and copies ran while one was open for 14% of the time, Pallas kernels for 10%

profile of v5, /device:TPU:1, one launch (start us, length us, event | category | flops | bytes accessed | tf_op | source)
XLA Modules:
  0.0 238.4 jit_solution(2758963369624635267)
XLA Ops:
  9.2 3.8 %copy.57 = bf16[1,256,3584]{1,2,0:T(8,128)(2,1)} copy(bf16[1,256,3584]{2,1,0:T(8,128)(2,1)} %param.11) | data formatting | bytes 3670016 | tf_op args[4]
  13.0 4.0 %collective-permute-start = (bf16[3584,256]{1,0:T(8,128)(2,1)}, bf16[3584,256]{1,0:T(8,128)(2,1)}, u32[]{:S(2)}, u32[]{:S(2)}) collective-permute-start(bf16[3584,256]{1,0:T(8,128)(2,1)} %bitcast.4), channel_id=1, source_target_pairs={{0,1},{1,2},{2,3},{3,0},{4,5},{5,6},{6,7},{7,4},{8,9},{9,10},{10,1... | collective-permute-start | bytes 5505032 | tf_op jit(solution)/shard_map/ppermute | solution.py:36
  23.1 14.9 %all-to-all-start = ((f32[16,2,48]{2,1,0:T(2,128)}), f32[16,2,48]{2,1,0:T(2,128)S(1)}, u32[]{:S(2)}, u32[]{:S(2)}) async-start(f32[16,2,48]{2,1,0:T(2,128)} %copy.53), calls=%async_computation | async-start | bytes 32768 | tf_op jit(solution)/shard_map/all_to_all | solution.py:307
  38.1 11.4 %all-to-all-done = f32[16,2,48]{2,1,0:T(2,128)S(1)} async-done(((f32[16,2,48]{2,1,0:T(2,128)}), f32[16,2,48]{2,1,0:T(2,128)S(1)}, u32[]{:S(2)}, u32[]{:S(2)}) %all-to-all-start) | async-done | bytes 6176 | tf_op jit(solution)/shard_map/all_to_all | solution.py:307
  50.5 8.6 %all-to-all-start.2 = ((f32[32,1,24]{2,1,0:T(1,128)}), f32[32,1,24]{2,1,0:T(1,128)S(1)}, u32[]{:S(2)}, u32[]{:S(2)}) async-start(f32[32,1,24]{2,1,0:T(1,128)} %reshape.293), calls=%async_computation.2 | async-start | bytes 32768 | tf_op jit(solution)/shard_map/all_to_all | solution.py:316
  60.9 5.2 %all-to-all-done.2 = f32[32,1,24]{2,1,0:T(1,128)S(1)} async-done(((f32[32,1,24]{2,1,0:T(1,128)}), f32[32,1,24]{2,1,0:T(1,128)S(1)}, u32[]{:S(2)}, u32[]{:S(2)}) %all-to-all-start.2) | async-done | bytes 3104 | tf_op jit(solution)/shard_map/all_to_all | solution.py:316
  66.1 3.5 %all-to-all-start.1 = ((bf16[4,192,512]{2,1,0:T(8,128)(2,1)}), bf16[4,192,512]{2,1,0:T(8,128)(2,1)S(1)}, u32[]{:S(2)}, u32[]{:S(2)}) async-start(bf16[4,192,512]{2,1,0:T(8,128)(2,1)} %bitcast.13), calls=%async_computation.1 | async-start | bytes 1572864 | tf_op jit(solution)/shard_map/all_to_all | solution.py:333
  69.6 3.5 %broadcast_in_dim.81 = bf16[4,3584,256]{2,1,0:T(8,128)(2,1)} broadcast(bf16[]{:T(256)} %constant.169.clone.1), dimensions={} | broadcast | bytes 7340034 | tf_op jit(solution)/shard_map/broadcast_in_dim | solution.py:47
  76.7 4.6 %all-to-all-done.1 = bf16[4,192,512]{2,1,0:T(8,128)(2,1)S(1)} async-done(((bf16[4,192,512]{2,1,0:T(8,128)(2,1)}), bf16[4,192,512]{2,1,0:T(8,128)(2,1)S(1)}, u32[]{:S(2)}, u32[]{:S(2)}) %all-to-all-start.1) | async-done | bytes 786464 | tf_op jit(solution)/shard_map/all_to_all | solution.py:333
  87.2 4.2 %collective-permute-start.3 = (bf16[1792,256]{1,0:T(8,128)(2,1)S(1)}, bf16[1792,256]{1,0:T(8,128)(2,1)S(1)}, u32[]{:S(2)}, u32[]{:S(2)}) collective-permute-start(bf16[1792,256]{1,0:T(8,128)(2,1)S(1)} %slice.53), channel_id=1, source_target_pairs={{0,3},{1,0},{2,1},{3,2},{4,7},{5,4},{6,5},{7,6},{8,11},{9,8},{10,9... | collective-permute-start | bytes 2752520 | tf_op jit(solution)/shard_map/ppermute | solution.py:36
  97.2 10.0 %collective-permute-done.2 = bf16[1792,256]{1,0:T(8,128)(2,1)S(1)} collective-permute-done((bf16[1792,256]{1,0:T(8,128)(2,1)S(1)}, bf16[1792,256]{1,0:T(8,128)(2,1)S(1)}, u32[]{:S(2)}, u32[]{:S(2)}) %collective-permute-start.2) | collective-permute-done | bytes 917536 | tf_op jit(solution)/shard_map/ppermute | solution.py:36
  111.6 4.7 %pick_grads.1 = bf16[4,8,24,896]{3,2,1,0:T(8,128)(2,1)} custom-call(f32[4,192,1]{2,1,0:T(8,128)S(1)} %reshape.294.index_ref, bf16[4,512,1792]{2,1,0:T(8,128)(2,1)} %bitcast.53), custom_call_target="tpu_custom_call" | custom-call | tf_op jit(solution)/shard_map/pick_grads/pallas_call | solution.py:83
  116.3 7.5 %all-to-all-start.3 = ((bf16[32,24,896]{2,1,0:T(8,128)(2,1)}), bf16[32,24,896]{2,1,0:T(8,128)(2,1)S(1)}, u32[]{:S(2)}, u32[]{:S(2)}) async-start(bf16[32,24,896]{2,1,0:T(8,128)(2,1)} %bitcast.17), calls=%async_computation.3 | async-start | bytes 2752512 | tf_op jit(solution)/shard_map/all_to_all | solution.py:346
  123.9 4.7 %pick_tokens.1 = bf16[8,4,24,896]{3,2,1,0:T(8,128)(2,1)} custom-call(f32[4,192,1]{2,1,0:T(8,128)S(1)} %reshape.294.index_ref, bf16[4,512,1792]{2,1,0:T(8,128)(2,1)} %bitcast.54), custom_call_target="tpu_custom_call" | custom-call | tf_op jit(solution)/shard_map/pick_tokens/pallas_call | solution.py:83
  128.6 15.1 %all-to-all-done.3 = bf16[32,24,896]{2,1,0:T(8,128)(2,1)S(1)} async-done(((bf16[32,24,896]{2,1,0:T(8,128)(2,1)}), bf16[32,24,896]{2,1,0:T(8,128)(2,1)S(1)}, u32[]{:S(2)}, u32[]{:S(2)}) %all-to-all-start.3) | async-done | bytes 1376288 | tf_op jit(solution)/shard_map/all_to_all | solution.py:346
  143.7 5.4 %all-to-all-start.4 = ((bf16[8,96,896]{2,1,0:T(8,128)(2,1)}), bf16[8,96,896]{2,1,0:T(8,128)(2,1)S(1)}, u32[]{:S(2)}, u32[]{:S(2)}) async-start(bf16[8,96,896]{2,1,0:T(8,128)(2,1)} %bitcast.20), calls=%async_computation.4 | async-start | bytes 2752512 | tf_op jit(solution)/shard_map/all_to_all | solution.py:353
  150.3 5.0 %hidden_step.1 = (bf16[192,1024]{1,0:T(8,128)(2,1)}, f32[192,1]{1,0:T(8,128)S(1)}) custom-call(bf16[4,192,896]{2,1,0:T(8,128)(2,1)S(1)} %bitcast.51, bf16[4,3584,256]{2,1,0:T(8,128)(2,1)} %bitcast_dynamic-update-slice_fusion.3.matrix_ref, f32[4,192,256]{2,1,0:T(8,128)S(1)} %copy-done, f32[4,192,256]{2,1,0:T(8,128)S(1)} %get-tuple-element.21.dw_act_ref), custom_call_target="tpu_custom_call" | custom-call | tf_op jit(solution)/shard_map/hidden_step/pallas_call | solution.py:161
  160.0 9.9 %collective-permute-done.4.west_ref = bf16[192,1024]{1,0:T(8,128)(2,1)S(1)} collective-permute-done((bf16[192,1024]{1,0:T(8,128)(2,1)}, bf16[192,1024]{1,0:T(8,128)(2,1)S(1)}, u32[]{:S(2)}, u32[]{:S(2)}) %collective-permute-start.4) | collective-permute-done | bytes 393248 | tf_op jit(solution)/shard_map/ppermute | solution.py:61
  173.0 4.5 %collective-permute-start.8 = (bf16[192,1664]{1,0:T(8,128)(2,1)}, bf16[192,1664]{1,0:T(8,128)(2,1)S(1)}, u32[]{:S(2)}, u32[]{:S(2)}) collective-permute-start(bf16[192,1664]{1,0:T(8,128)(2,1)} %get-tuple-element.29), channel_id=1, source_target_pairs={{0,3},{1,2},{2,1},{3,0},{4,7},{5,6},{6,5},{7,4},{8,11},{9,10},{10,... | collective-permute-start | bytes 1916936 | tf_op jit(solution)/shard_map/ppermute | solution.py:61
  181.8 12.1 %all-to-all-start.5 = ((f32[16,8,128]{2,1,0:T(8,128)}), f32[16,8,128]{2,1,0:T(8,128)S(1)}, u32[]{:S(2)}, u32[]{:S(2)}) async-start(f32[16,8,128]{2,1,0:T(8,128)} %pad_dynamic-update-slice_fusion), calls=%async_computation.5 | async-start | bytes 131072 | tf_op jit(solution)/shard_map/all_to_all | solution.py:369
  195.2 3.4 %collective-permute-start.9 = (bf16[192,1152]{1,0:T(8,128)(2,1)S(1)}, bf16[192,1152]{1,0:T(8,128)(2,1)}, u32[]{:S(2)}, u32[]{:S(2)}) collective-permute-start(bf16[192,1152]{1,0:T(8,128)(2,1)S(1)} %slice_add_fusion.high_a), channel_id=1, source_target_pairs={{0,1},{1,0},{2,3},{3,2},{4,5},{5,4},{6,7},{7,6},{8,9},{9,8},{10,11... | collective-permute-start | bytes 1327112 | tf_op jit(solution)/shard_map/ppermute | solution.py:61
  201.5 4.0 %all-to-all-done.5 = f32[16,8,128]{2,1,0:T(8,128)S(1)} async-done(((f32[16,8,128]{2,1,0:T(8,128)}), f32[16,8,128]{2,1,0:T(8,128)S(1)}, u32[]{:S(2)}, u32[]{:S(2)}) %all-to-all-start.5) | async-done | bytes 65568 | tf_op jit(solution)/shard_map/all_to_all | solution.py:369
  206.2 9.1 %all-to-all-start.6 = ((f32[32,1,96]{2,1,0:T(1,128)}), f32[32,1,96]{2,1,0:T(1,128)S(1)}, u32[]{:S(2)}, u32[]{:S(2)}) async-start(f32[32,1,96]{2,1,0:T(1,128)} %bitcast.24), calls=%async_computation.6 | async-start | bytes 32768 | tf_op jit(solution)/shard_map/all_to_all | solution.py:372
  216.1 13.6 %last_step.1 = bf16[1,896,1024]{2,1,0:T(8,128)(2,1)} custom-call(s32[1]{0:T(128)} %bitcast.26.rank_ref, bf16[896,768]{1,0:T(8,128)(2,1)} %get-tuple-element.27.rows_t_hbm, bf16[192,1024]{1,0:T(8,128)(2,1)} %get-tuple-element.24.own_hbm, bf16[192,1152]{1,0:T(8,128)(2,1)} %slice_add_fusion.1.low_a, bf16[192,1152]{1,0:T(8,128)(2,1)} %copy-done.7, ...), custom_call_target="tpu_custom_call" | custom-call | tf_op jit(solution)/shard_map/last_step/pallas_call | solution.py:255
  (98 shorter events, 51.0 us)
Async XLA Ops:
  7.2 52.0 %copy-start.11 = (bf16[1,768,256]{2,1,0:T(8,128)(2,1)S(1)}, bf16[1,768,256]{2,1,0:T(8,128)(2,1)}, u32[]{:S(2)}) copy-start(bf16[1,768,256]{2,1,0:T(8,128)(2,1)} %param.12) | copy-start | bytes 1179652
  7.2 52.0 %copy-start.10 = (bf16[1,768,256]{2,1,0:T(8,128)(2,1)S(1)}, bf16[1,768,256]{2,1,0:T(8,128)(2,1)}, u32[]{:S(2)}) copy-start(bf16[1,768,256]{2,1,0:T(8,128)(2,1)} %param.13) | copy-start | bytes 1179652
  7.2 104.4 %all-gather.2.cloned.1.call-start = ((), (), s32[]{:S(2)}) async-start(), calls=%async_computation.7 | async-start | bytes 7798784 | tf_op jit(solution)/shard_map/all_gather | solution.py:290
  13.0 69.4 %collective-permute-start = (bf16[3584,256]{1,0:T(8,128)(2,1)}, bf16[3584,256]{1,0:T(8,128)(2,1)}, u32[]{:S(2)}, u32[]{:S(2)}) collective-permute-start(bf16[3584,256]{1,0:T(8,128)(2,1)} %bitcast.4), channel_id=1, source_target_pairs={{0,1},{1,2},{2,3},{3,0},{4,5},{5,6},{6,7},{7,4},{8,9},{9,10},{10,1... | collective-permute-start | bytes 5505032 | tf_op jit(solution)/shard_map/ppermute | solution.py:36
  17.0 68.9 %collective-permute-start.1 = (bf16[3584,256]{1,0:T(8,128)(2,1)}, bf16[3584,256]{1,0:T(8,128)(2,1)}, u32[]{:S(2)}, u32[]{:S(2)}) collective-permute-start(bf16[3584,256]{1,0:T(8,128)(2,1)} %bitcast.4), channel_id=1, source_target_pairs={{0,3},{1,0},{2,1},{3,2},{4,7},{5,4},{6,5},{7,6},{8,11},{9,8},{10,9... | collective-permute-start | bytes 5505032 | tf_op jit(solution)/shard_map/ppermute | solution.py:36
  23.1 26.3 %all-to-all-start = ((f32[16,2,48]{2,1,0:T(2,128)}), f32[16,2,48]{2,1,0:T(2,128)S(1)}, u32[]{:S(2)}, u32[]{:S(2)}) async-start(f32[16,2,48]{2,1,0:T(2,128)} %copy.53), calls=%async_computation | async-start | bytes 32768 | tf_op jit(solution)/shard_map/all_to_all | solution.py:307
  50.5 15.5 %all-to-all-start.2 = ((f32[32,1,24]{2,1,0:T(1,128)}), f32[32,1,24]{2,1,0:T(1,128)S(1)}, u32[]{:S(2)}, u32[]{:S(2)}) async-start(f32[32,1,24]{2,1,0:T(1,128)} %reshape.293), calls=%async_computation.2 | async-start | bytes 32768 | tf_op jit(solution)/shard_map/all_to_all | solution.py:316
  66.1 15.2 %all-to-all-start.1 = ((bf16[4,192,512]{2,1,0:T(8,128)(2,1)}), bf16[4,192,512]{2,1,0:T(8,128)(2,1)S(1)}, u32[]{:S(2)}, u32[]{:S(2)}) async-start(bf16[4,192,512]{2,1,0:T(8,128)(2,1)} %bitcast.13), calls=%async_computation.1 | async-start | bytes 1572864 | tf_op jit(solution)/shard_map/all_to_all | solution.py:333
  83.7 23.5 %collective-permute-start.2 = (bf16[1792,256]{1,0:T(8,128)(2,1)S(1)}, bf16[1792,256]{1,0:T(8,128)(2,1)S(1)}, u32[]{:S(2)}, u32[]{:S(2)}) collective-permute-start(bf16[1792,256]{1,0:T(8,128)(2,1)S(1)} %slice.52), channel_id=1, source_target_pairs={{0,1},{1,2},{2,3},{3,0},{4,5},{5,6},{6,7},{7,4},{8,9},{9,10},{10,1... | collective-permute-start | bytes 2752520 | tf_op jit(solution)/shard_map/ppermute | solution.py:36
  87.2 22.2 %collective-permute-start.3 = (bf16[1792,256]{1,0:T(8,128)(2,1)S(1)}, bf16[1792,256]{1,0:T(8,128)(2,1)S(1)}, u32[]{:S(2)}, u32[]{:S(2)}) collective-permute-start(bf16[1792,256]{1,0:T(8,128)(2,1)S(1)} %slice.53), channel_id=1, source_target_pairs={{0,3},{1,0},{2,1},{3,2},{4,7},{5,4},{6,5},{7,6},{8,11},{9,8},{10,9... | collective-permute-start | bytes 2752520 | tf_op jit(solution)/shard_map/ppermute | solution.py:36
  116.3 27.4 %all-to-all-start.3 = ((bf16[32,24,896]{2,1,0:T(8,128)(2,1)}), bf16[32,24,896]{2,1,0:T(8,128)(2,1)S(1)}, u32[]{:S(2)}, u32[]{:S(2)}) async-start(bf16[32,24,896]{2,1,0:T(8,128)(2,1)} %bitcast.17), calls=%async_computation.3 | async-start | bytes 2752512 | tf_op jit(solution)/shard_map/all_to_all | solution.py:346
  143.7 26.7 %all-to-all-start.4 = ((bf16[8,96,896]{2,1,0:T(8,128)(2,1)}), bf16[8,96,896]{2,1,0:T(8,128)(2,1)S(1)}, u32[]{:S(2)}, u32[]{:S(2)}) async-start(bf16[8,96,896]{2,1,0:T(8,128)(2,1)} %bitcast.20), calls=%async_computation.4 | async-start | bytes 2752512 | tf_op jit(solution)/shard_map/all_to_all | solution.py:353
  155.9 14.0 %collective-permute-start.4 = (bf16[192,1024]{1,0:T(8,128)(2,1)}, bf16[192,1024]{1,0:T(8,128)(2,1)S(1)}, u32[]{:S(2)}, u32[]{:S(2)}) collective-permute-start(bf16[192,1024]{1,0:T(8,128)(2,1)} %get-tuple-element.24.own_hbm), channel_id=1, source_target_pairs={{0,3},{1,2},{2,1},{3,0},{4,7},{5,6},{6,5},{7,4},{8,11},{9,10},{10,... | collective-permute-start | bytes 1179656 | tf_op jit(solution)/shard_map/ppermute | solution.py:61
  157.9 12.5 %collective-permute-start.5 = (bf16[192,1024]{1,0:T(8,128)(2,1)}, bf16[192,1024]{1,0:T(8,128)(2,1)S(1)}, u32[]{:S(2)}, u32[]{:S(2)}) collective-permute-start(bf16[192,1024]{1,0:T(8,128)(2,1)} %get-tuple-element.24.own_hbm), channel_id=1, source_target_pairs={{0,1},{1,0},{2,3},{3,2},{4,5},{5,4},{6,7},{7,6},{8,9},{9,8},{10,11... | collective-permute-start | bytes 1179656 | tf_op jit(solution)/shard_map/ppermute | solution.py:61
  169.9 45.4 %copy-start.1 = (bf16[192,1024]{1,0:T(8,128)(2,1)}, bf16[192,1024]{1,0:T(8,128)(2,1)S(1)}, u32[]{:S(2)}) copy-start(bf16[192,1024]{1,0:T(8,128)(2,1)S(1)} %collective-permute-done.4.west_ref) | copy-start | bytes 1179652
  170.4 44.9 %copy-start.2 = (bf16[192,1024]{1,0:T(8,128)(2,1)}, bf16[192,1024]{1,0:T(8,128)(2,1)S(1)}, u32[]{:S(2)}) copy-start(bf16[192,1024]{1,0:T(8,128)(2,1)S(1)} %collective-permute-done.5.east_ref) | copy-start | bytes 1179652
  173.0 20.9 %collective-permute-start.8 = (bf16[192,1664]{1,0:T(8,128)(2,1)}, bf16[192,1664]{1,0:T(8,128)(2,1)S(1)}, u32[]{:S(2)}, u32[]{:S(2)}) collective-permute-start(bf16[192,1664]{1,0:T(8,128)(2,1)} %get-tuple-element.29), channel_id=1, source_target_pairs={{0,3},{1,2},{2,1},{3,0},{4,7},{5,6},{6,5},{7,4},{8,11},{9,10},{10,... | collective-permute-start | bytes 1916936 | tf_op jit(solution)/shard_map/ppermute | solution.py:61
  177.5 21.1 %collective-permute-start.6 = (bf16[192,1664]{1,0:T(8,128)(2,1)S(1)}, bf16[192,1664]{1,0:T(8,128)(2,1)S(1)}, u32[]{:S(2)}, u32[]{:S(2)}) collective-permute-start(bf16[192,1664]{1,0:T(8,128)(2,1)S(1)} %get-tuple-element.28), channel_id=1, source_target_pairs={{0,1},{1,0},{2,3},{3,2},{4,5},{5,4},{6,7},{7,6},{8,9},{9,8},{10,11... | collective-permute-start | bytes 1916936 | tf_op jit(solution)/shard_map/ppermute | solution.py:61
  181.8 23.7 %all-to-all-start.5 = ((f32[16,8,128]{2,1,0:T(8,128)}), f32[16,8,128]{2,1,0:T(8,128)S(1)}, u32[]{:S(2)}, u32[]{:S(2)}) async-start(f32[16,8,128]{2,1,0:T(8,128)} %pad_dynamic-update-slice_fusion), calls=%async_computation.5 | async-start | bytes 131072 | tf_op jit(solution)/shard_map/all_to_all | solution.py:369
  193.9 21.4 %copy-start.4 = (bf16[192,1664]{1,0:T(8,128)(2,1)}, bf16[192,1664]{1,0:T(8,128)(2,1)S(1)}, u32[]{:S(2)}) copy-start(bf16[192,1664]{1,0:T(8,128)(2,1)S(1)} %collective-permute-done.8.far_high) | copy-start | bytes 1916932
  195.2 20.1 %copy-start.6 = (bf16[192,1152]{1,0:T(8,128)(2,1)}, bf16[192,1152]{1,0:T(8,128)(2,1)S(1)}, u32[]{:S(2)}) copy-start(bf16[192,1152]{1,0:T(8,128)(2,1)S(1)} %slice_add_fusion.high_a) | copy-start | bytes 1327108
  195.2 20.0 %collective-permute-start.9 = (bf16[192,1152]{1,0:T(8,128)(2,1)S(1)}, bf16[192,1152]{1,0:T(8,128)(2,1)}, u32[]{:S(2)}, u32[]{:S(2)}) collective-permute-start(bf16[192,1152]{1,0:T(8,128)(2,1)S(1)} %slice_add_fusion.high_a), channel_id=1, source_target_pairs={{0,1},{1,0},{2,3},{3,2},{4,5},{5,4},{6,7},{7,6},{8,9},{9,8},{10,11... | collective-permute-start | bytes 1327112 | tf_op jit(solution)/shard_map/ppermute | solution.py:61
  199.5 15.8 %collective-permute-start.7 = (bf16[192,1152]{1,0:T(8,128)(2,1)}, bf16[192,1152]{1,0:T(8,128)(2,1)S(1)}, u32[]{:S(2)}, u32[]{:S(2)}) collective-permute-start(bf16[192,1152]{1,0:T(8,128)(2,1)} %slice_add_fusion.1.low_a), channel_id=1, source_target_pairs={{0,3},{1,2},{2,1},{3,0},{4,7},{5,6},{6,5},{7,4},{8,11},{9,10},{10,... | collective-permute-start | bytes 1327112 | tf_op jit(solution)/shard_map/ppermute | solution.py:61
  206.2 23.5 %all-to-all-start.6 = ((f32[32,1,96]{2,1,0:T(1,128)}), f32[32,1,96]{2,1,0:T(1,128)S(1)}, u32[]{:S(2)}, u32[]{:S(2)}) async-start(f32[32,1,96]{2,1,0:T(1,128)} %bitcast.24), calls=%async_computation.6 | async-start | bytes 32768 | tf_op jit(solution)/shard_map/all_to_all | solution.py:372
  (6 other events, 46.0 us)
Sparse Core Ops, SparseCore 0:
  10.1 101.4 all-gather.1

commit v6 on v5

--- a/solution.py
+++ b/solution.py
@@ -1,3 +1,4 @@
+import functools
 import math
 
 import jax
@@ -36,12 +37,13 @@
     return lax.ppermute(values, "y", [(i, (i + step) % size) for i in range(size)])
 
 
-def gather_weights(own):
+def gather_weights(own, behind):
     size, rank = lax.axis_size("y"), lax.axis_index("y")
     own = own.T
     half = own.shape[0] // 2
     before = shift(own, 1)
     after = shift(own, -1)
+    before, after, behind = lax.optimization_barrier((before, after, behind))
     far_low = shift(before[:half], 1)
     far_high = shift(after[half:], -1)
     whole = jnp.zeros((size,) + own.shape, own.dtype)
@@ -49,7 +51,7 @@
     for part, step, row in parts:
         place = lax.rem(rank + size + step, size)
         whole = lax.dynamic_update_slice(whole, part[None], (place, row, 0))
-    return whole
+    return whole, behind
 
 
 def total(values):
@@ -61,13 +63,19 @@
     return lax.ppermute(values, "y", [(i, partner(i)) for i in range(size)])
 
 
-def pick_kernel(index_ref, column_ref, out_ref):
-    rows, count = index_ref.shape[1], column_ref.shape[1]
-    feats = out_ref.shape[-1]
+def pick_kernel(by_quarter, index_ref, column_ref, out_ref):
+    quarters, rows, _ = index_ref.shape
+    count = column_ref.shape[1]
+    piece, feats = out_ref.shape[2:]
     columns = lax.broadcasted_iota(jnp.int32, (rows, count), 1).astype(f32) + 1.0
-    chosen = jnp.where(index_ref[0] == columns, 1.0, 0.0).astype(bf16)
-    picked = dot(chosen, column_ref[0], ((1,), (0,)))
-    out_ref[...] = picked.reshape(out_ref.shape).astype(bf16)
+    for q in range(quarters):
+        chosen = jnp.where(index_ref[q] == columns, 1.0, 0.0).astype(bf16)
+        picked = dot(chosen, column_ref[q], ((1,), (0,)))
+        picked = picked.reshape(rows // piece, piece, feats).astype(bf16)
+        if by_quarter:
+            out_ref[q] = picked
+        else:
+            out_ref[:, q] = picked
 
 
 def pick_rows(index, column, near, part, by_quarter, name):
@@ -75,17 +83,17 @@
     feats = column.shape[2] // 2
     piece = rows // near
     if by_quarter:
-        block, place = (1, near, piece, feats), (lambda q: (q, 0, 0, 0))
+        block, place = (2, near, piece, feats), (lambda q: (q, 0, 0, 0))
         shape = (quarters, near, piece, feats)
     else:
-        block, place = (near, 1, piece, feats), (lambda q: (0, q, 0, 0))
+        block, place = (near, 2, piece, feats), (lambda q: (0, q, 0, 0))
         shape = (near, quarters, piece, feats)
     return pl.pallas_call(
-        pick_kernel,
-        grid=(quarters,),
+        functools.partial(pick_kernel, by_quarter),
+        grid=(quarters // 2,),
         in_specs=[
-            pl.BlockSpec((1, rows, 1), lambda q: (q, 0, 0)),
-            pl.BlockSpec((1, column.shape[1], feats), lambda q: (q, 0, part)),
+            pl.BlockSpec((2, rows, 1), lambda q: (q, 0, 0)),
+            pl.BlockSpec((2, column.shape[1], feats), lambda q: (q, 0, part)),
         ],
         out_specs=pl.BlockSpec(block, place),
         out_shape=jax.ShapeDtypeStruct(shape, bf16),
@@ -156,7 +164,7 @@
     blocks, depth, width = matrix.shape
     outs = [
         pltpu.HBM((rows, blocks * width), bf16),
-        jax.ShapeDtypeStruct((rows, 1), f32),
+        pltpu.HBM((rows, 1), f32),
     ]
     return pl.pallas_call(
         hidden_kernel,
@@ -170,48 +178,65 @@
         out_specs=[pl.BlockSpec(out.shape, lambda k: (0, 0)) for out in outs],
         out_shape=outs,
         scratch_shapes=[pltpu.VMEM((rows, blocks * width), f32)],
-        compiler_params=pltpu.CompilerParams(vmem_limit_bytes=28 * MIB),
+        compiler_params=pltpu.CompilerParams(vmem_limit_bytes=46 * MIB),
         name="hidden_step",
     )(grads, matrix, out_act, dw_act)
 
 
 def last_kernel(
-    rank_ref, rows_t_hbm, own_hbm, low_a, low_b, high_a, high_b, west_ref, east_ref,
+    rank_ref, rows_t_hbm, own_hbm, low_a, low_b, high_a, high_b, west_hbm, east_hbm,
     far_low, far_high, out_ref,
     up_ref, inner_ref, carried_ref, gram_ref, square_ref, poly_ref, start_ref, rows_t_ref,
-    own_sem, rows_sem,
+    packs_ref, sems,
 ):
     rank = rank_ref[0]
-    own, hidden = west_ref.shape
-    feats, slots = rows_t_ref.shape
+    own = west_hbm.shape[0]
+    slots, hidden = up_ref.shape
+    feats = rows_t_ref.shape[0]
     half = slots // 2
     near = rank + 1 - 2 * lax.rem(rank, 2)
 
     def owned(owner):
         return pl.ds(pl.multiple_of(owner * own, own), own)
 
-    own_copy = pltpu.make_async_copy(own_hbm, up_ref.at[owned(rank)], own_sem)
-    rows_copy = pltpu.make_async_copy(rows_t_hbm, rows_t_ref, rows_sem)
-    own_copy.start()
-    rows_copy.start()
-    for owner, part in ((3 - rank, west_ref), (near, east_ref)):
-        up_ref[owned(owner)] = part[...]
-    up_ref[owned(3 - near), : hidden // 2] = far_low[:, 3 * half :]
-    up_ref[owned(3 - near), hidden // 2 :] = far_high[:, 3 * half :]
-
-    def summed(one, two, i):
+    far = owned(3 - near)
+    first, second = pl.ds(0, hidden // 2), pl.ds(hidden // 2, hidden // 2)
+    riding = pl.ds(3 * half, hidden // 2)
+    moves = [
+        (low_a, packs_ref.at[0]),
+        (low_b, packs_ref.at[1]),
+        (high_a, packs_ref.at[2]),
+        (high_b, packs_ref.at[3]),
+        (own_hbm, up_ref.at[owned(rank)]),
+        (west_hbm, up_ref.at[owned(3 - rank)]),
+        (east_hbm, up_ref.at[owned(near)]),
+        (far_low.at[:, riding], up_ref.at[far, first]),
+        (far_high.at[:, riding], up_ref.at[far, second]),
+        (rows_t_hbm, rows_t_ref),
+    ]
+    copies = [
+        pltpu.make_async_copy(source, place, sems.at[i])
+        for i, (source, place) in enumerate(moves)
+    ]
+    for copy in copies:
+        copy.start()
+    for copy in copies[:4]:
+        copy.wait()
+
+    def summed(one, i):
         lanes = slice(i * half, (i + 1) * half)
-        return one[:, lanes].astype(f32) + two[:, lanes].astype(f32)
-
-    low = [summed(low_a, low_b, i) for i in range(3)]
-    high = [summed(high_a, high_b, i) for i in range(3)]
+        return packs_ref[one, :, lanes].astype(f32) + packs_ref[one + 1, :, lanes].astype(f32)
+
+    low = [summed(0, i) for i in range(3)]
+    high = [summed(2, i) for i in range(3)]
     cross = jnp.concatenate([low[2], high[0]], axis=0)
     for i in range(2):
         inner_ref[i * own : (i + 1) * own, :half] = low[i].astype(bf16)
         inner_ref[half + i * own : half + (i + 1) * own, half:] = high[1 + i].astype(bf16)
     inner_ref[:half, half:] = cross.astype(bf16)
     inner_ref[half:, :half] = cross.T.astype(bf16)
-    own_copy.wait()
+    for copy in copies[4:9]:
+        copy.wait()
     norm = jnp.zeros((1, 1), f32)
     step = slots // 3
     for i in range(0, slots, step):
@@ -229,7 +254,7 @@
         quartic = quartic + total(square * square)
         square_ref[i : i + step] = square
     rows = feats // 4
-    rows_copy.wait()
+    copies[9].wait()
     for i in range(0, feats, rows):
         gradient = dot(rows_t_ref[i : i + rows], up_ref[...], ((1,), (0,)))
         start_ref[i : i + rows] = (gradient * scale).astype(bf16)
@@ -255,8 +280,7 @@
     return pl.pallas_call(
         last_kernel,
         in_specs=[pl.BlockSpec(memory_space=pltpu.SMEM)]
-        + [pl.BlockSpec(memory_space=pltpu.HBM)] * 2
-        + [pl.BlockSpec()] * 8,
+        + [pl.BlockSpec(memory_space=pltpu.HBM)] * 10,
         out_shape=jax.ShapeDtypeStruct((1, feats, hidden), bf16),
         scratch_shapes=[
             pltpu.VMEM((slots, hidden), bf16),
@@ -267,8 +291,8 @@
             pltpu.VMEM((hidden, hidden), bf16),
             pltpu.VMEM((feats, hidden), bf16),
             pltpu.VMEM((feats, slots), bf16),
-            pltpu.SemaphoreType.DMA,
-            pltpu.SemaphoreType.DMA,
+            pltpu.VMEM((4,) + packs[0].shape, bf16),
+            pltpu.SemaphoreType.DMA((10,)),
         ],
         compiler_params=pltpu.CompilerParams(vmem_limit_bytes=56 * MIB),
         name="last_step",
@@ -290,7 +314,6 @@
     column = lax.all_gather(
         jnp.concatenate([tokens_in, out_grad], axis=1), "z", axis=0, tiled=True
     )
-    matrix = gather_weights(down_weight[0])
 
     flat_ids = expert_ids.reshape(-1)
     position = block_positions(flat_ids)
@@ -312,11 +335,10 @@
     start = (jnp.arange(nz, dtype=jnp.int32) % zl * tok_rows).astype(f32)[:, None, None]
     index = jnp.where(routes[:, 0] > 0.0, routes[:, 0] + start, 0.0)
     index = index.reshape(ny, zl, near, CAP).transpose(0, 2, 1, 3).reshape(ny, own_slots, 1)
-    weight_order = routes[:, 1].reshape(ny, zl, near, CAP).transpose(0, 2, 1, 3)
-    weight = lax.all_to_all(
-        weight_order.reshape(ny * near, zl * CAP), ("y", "x", "c"), 0, 0, tiled=True
-    )
-    weight = weight.reshape(ny, own_slots)[0][:, None]
+    weight = routes[:, 1].reshape(ny, zl, near, CAP).transpose(0, 2, 1, 3)
+    weight = lax.dynamic_index_in_dim(weight, lax.axis_index("y"), 0, keepdims=False)
+    weight = lax.all_to_all(weight.reshape(near, zl * CAP), ("x", "c"), 0, 0, tiled=True)
+    weight = weight.reshape(own_slots)[:, None]
 
     row = jnp.arange(slots, dtype=jnp.int32)
     rest = row // CAP
@@ -330,6 +352,7 @@
     order = (source[:, None] == row[None, :]).astype(bf16)
     saved = jnp.concatenate([gate_saved[0], up_saved[0]], axis=1)
     saved = dot(order, saved, ((1,), (0,))).astype(bf16)
+    matrix, saved = gather_weights(down_weight[0], saved)
     saved = lax.all_to_all(
         saved.reshape(ny, own_slots, 2 * hidden_part), "y", 0, 0, tiled=True
     )

time: 240 us -> 233 us (0.971)
  starting transfers between devices: 90.8 us -> 86.6 us
  Pallas kernels: 30.7 us -> 27.5 us
  local copies, waits for them, and re-layouts: 29.1 us -> 32.2 us
  waiting for transfers between devices: 63.1 us -> 60.6 us
    all_to_all x1, waiting for transfers between devices: 4.6 us -> 16.2 us  [on_device(): lax.all_to_all(saved.reshape(ny, own_slots, 2 * hidden_part), 'y', 0, 0,...]
    ppermute x4, waiting for transfers between devices: 11.3 us -> 0.01 us  [shift(): lax.ppermute(values, 'y', [(i, (i + step) % size) for i in range(size)])]
    all_to_all x1, waiting for transfers between devices: 11.4 us -> 3.29 us  [on_device(): lax.all_to_all(jnp.stack([index_send.reshape(nz, near * CAP), weight_send...]
    all_gather x1, waiting for transfers between devices: 1.14 us -> 7.4 us  [on_device(): lax.all_gather(jnp.concatenate([tokens_in, out_grad], axis=1), 'z', axis=...]
    all_to_all x1, starting transfers between devices: 12.1 us -> 8.6 us  [on_device(): back = lax.all_to_all(back, 'z', 0, 0, tiled=True)[:, :, :CAP]]
    unnamed x28 -> x26, local copies, waits for them, and re-layouts: 7.1 us -> 6.47 us
  transfers between devices with their start and end apart: 18 -> 18, of which waited for: 10 -> 9; matrix products, arithmetic and copies ran while one was open for 14% -> 16% of each run, Pallas kernels for 10% -> 9%
where the time goes in v6:
time: 233 us; the launch traced here: 232 us
  starting transfers between devices  86.6 us (37%)
  waiting for transfers between devices  60.6 us (26%)
  local copies, waits for them, and re-layouts  32.2 us (14%)
  Pallas kernels  27.5 us (12%)
  between operations  14.5 us (6%)
  other arithmetic  9.11 us (4%)
    ppermute x6, starting transfers between devices, swap(): return lax.ppermute(values, 'y', [(i, partner(i)) for i in range(size)])  16.8 us
    all_to_all x1, waiting for transfers between devices, on_device(): lax.all_to_all(grad_send.reshape(ny * near, zl * CAP, feats), ('y', 'x',...  16.2 us
    all_to_all x1, waiting for transfers between devices, on_device(): lax.all_to_all(saved.reshape(ny, own_slots, 2 * hidden_part), 'y', 0, 0,...  16.2 us
    all_to_all x1, starting transfers between devices, on_device(): lax.all_to_all(jnp.stack([index_send.reshape(nz, near * CAP), weight_send...  14.9 us
    ppermute x4, starting transfers between devices, shift(): lax.ppermute(values, 'y', [(i, (i + step) % size) for i in range(size)])  13.9 us
    dynamic_update_slice x5, local copies, waits for them, and re-layouts, gather_weights(): whole = lax.dynamic_update_slice(whole, part[None], (place, row, 0))  13 us
    pallas_call x1, Pallas kernels, last_step(): pl.pallas_call(last_kernel, in_specs=[pl.BlockSpec(memory_space=pltpu.SME...  12.6 us
    ppermute x6, waiting for transfers between devices, swap(): return lax.ppermute(values, 'y', [(i, partner(i)) for i in range(size)])  11.1 us
  transfers between devices with their start and end apart: 18, of which 9 were waited for; matrix products, arithmetic and copies ran while one was open for 16% of the time, Pallas kernels for 9%

profile of v6, /device:TPU:1, one launch (start us, length us, event | category | flops | bytes accessed | tf_op | source)
XLA Modules:
  0.0 232.1 jit_solution(9765165654193187570)
XLA Ops:
  9.2 3.8 %copy.56 = bf16[1,256,3584]{1,2,0:T(8,128)(2,1)} copy(bf16[1,256,3584]{2,1,0:T(8,128)(2,1)} %param.11) | data formatting | bytes 3670016 | tf_op args[4]
  13.0 4.0 %collective-permute-start = (bf16[3584,256]{1,0:T(8,128)(2,1)}, bf16[3584,256]{1,0:T(8,128)(2,1)}, u32[]{:S(2)}, u32[]{:S(2)}) collective-permute-start(bf16[3584,256]{1,0:T(8,128)(2,1)} %bitcast.4), channel_id=1, source_target_pairs={{0,1},{1,2},{2,3},{3,0},{4,5},{5,6},{6,7},{7,4},{8,9},{9,10},{10,1... | collective-permute-start | bytes 5505032 | tf_op jit(solution)/shard_map/ppermute | solution.py:37
  17.0 3.4 %collective-permute-start.1 = (bf16[3584,256]{1,0:T(8,128)(2,1)}, bf16[3584,256]{1,0:T(8,128)(2,1)}, u32[]{:S(2)}, u32[]{:S(2)}) collective-permute-start(bf16[3584,256]{1,0:T(8,128)(2,1)} %bitcast.4), channel_id=1, source_target_pairs={{0,3},{1,0},{2,1},{3,2},{4,7},{5,4},{6,5},{7,6},{8,11},{9,8},{10,9... | collective-permute-start | bytes 5505032 | tf_op jit(solution)/shard_map/ppermute | solution.py:37
  23.1 14.9 %all-to-all-start = ((f32[16,2,48]{2,1,0:T(2,128)}), f32[16,2,48]{2,1,0:T(2,128)S(1)}, u32[]{:S(2)}, u32[]{:S(2)}) async-start(f32[16,2,48]{2,1,0:T(2,128)} %copy.52), calls=%async_computation | async-start | bytes 32768 | tf_op jit(solution)/shard_map/all_to_all | solution.py:330
  39.8 3.5 %broadcast_in_dim.81 = bf16[4,3584,256]{2,1,0:T(8,128)(2,1)} broadcast(bf16[]{:T(256)} %constant.173.clone.1), dimensions={} | broadcast | bytes 7340034 | tf_op jit(solution)/shard_map/broadcast_in_dim | solution.py:49
  46.2 3.3 %all-to-all-done = f32[16,2,48]{2,1,0:T(2,128)S(1)} async-done(((f32[16,2,48]{2,1,0:T(2,128)}), f32[16,2,48]{2,1,0:T(2,128)S(1)}, u32[]{:S(2)}, u32[]{:S(2)}) %all-to-all-start) | async-done | bytes 6176 | tf_op jit(solution)/shard_map/all_to_all | solution.py:330
  50.5 6.9 %all-to-all-start.2 = ((f32[8,1,24]{2,1,0:T(1,128)}), f32[8,1,24]{2,1,0:T(1,128)S(1)}, u32[]{:S(2)}, u32[]{:S(2)}) async-start(f32[8,1,24]{2,1,0:T(1,128)} %bitcast.16), calls=%async_computation.2 | async-start | bytes 8192 | tf_op jit(solution)/shard_map/all_to_all | solution.py:340
  58.0 4.1 %all-to-all-done.2 = f32[8,1,24]{2,1,0:T(1,128)S(1)} async-done(((f32[8,1,24]{2,1,0:T(1,128)}), f32[8,1,24]{2,1,0:T(1,128)S(1)}, u32[]{:S(2)}, u32[]{:S(2)}) %all-to-all-start.2) | async-done | bytes 800 | tf_op jit(solution)/shard_map/all_to_all | solution.py:340
  68.7 4.5 %collective-permute-start.3 = (bf16[1792,256]{1,0:T(8,128)(2,1)S(1)}, bf16[1792,256]{1,0:T(8,128)(2,1)}, u32[]{:S(2)}, u32[]{:S(2)}) collective-permute-start(bf16[1792,256]{1,0:T(8,128)(2,1)S(1)} %slice.36), channel_id=1, source_target_pairs={{0,3},{1,0},{2,1},{3,2},{4,7},{5,4},{6,5},{7,6},{8,11},{9,8},{10,9... | collective-permute-start | bytes 2752520 | tf_op jit(solution)/shard_map/ppermute | solution.py:37
  73.2 3.5 %all-to-all-start.1 = ((bf16[4,192,512]{2,1,0:T(8,128)(2,1)}), bf16[4,192,512]{2,1,0:T(8,128)(2,1)S(1)}, u32[]{:S(2)}, u32[]{:S(2)}) async-start(bf16[4,192,512]{2,1,0:T(8,128)(2,1)} %bitcast.13), calls=%async_computation.1 | async-start | bytes 1572864 | tf_op jit(solution)/shard_map/all_to_all | solution.py:356
  82.5 16.2 %all-to-all-done.1 = bf16[4,192,512]{2,1,0:T(8,128)(2,1)S(1)} async-done(((bf16[4,192,512]{2,1,0:T(8,128)(2,1)}), bf16[4,192,512]{2,1,0:T(8,128)(2,1)S(1)}, u32[]{:S(2)}, u32[]{:S(2)}) %all-to-all-start.1) | async-done | bytes 786464 | tf_op jit(solution)/shard_map/all_to_all | solution.py:356
  104.2 7.4 %all-gather.2.cloned.1.call-done = bf16[2048,1792]{1,0:T(8,128)(2,1)} async-done(((bf16[128,1792]{1,0:T(8,128)(2,1)}), bf16[2048,1792]{1,0:T(8,128)(2,1)}) %all-gather.2.cloned.1.call-update) | async-done | bytes 7340048 | tf_op jit(solution)/shard_map/all_gather | solution.py:314
  111.6 3.7 %pick_grads.1 = bf16[4,8,24,896]{3,2,1,0:T(8,128)(2,1)} custom-call(f32[4,192,1]{2,1,0:T(8,128)S(1)} %reshape.290.index_ref, bf16[4,512,1792]{2,1,0:T(8,128)(2,1)} %bitcast.53), custom_call_target="tpu_custom_call" | custom-call | tf_op jit(solution)/shard_map/pick_grads/pallas_call | solution.py:91
  115.2 7.5 %all-to-all-start.3 = ((bf16[32,24,896]{2,1,0:T(8,128)(2,1)}), bf16[32,24,896]{2,1,0:T(8,128)(2,1)S(1)}, u32[]{:S(2)}, u32[]{:S(2)}) async-start(bf16[32,24,896]{2,1,0:T(8,128)(2,1)} %bitcast.18), calls=%async_computation.3 | async-start | bytes 2752512 | tf_op jit(solution)/shard_map/all_to_all | solution.py:369
  122.8 3.6 %pick_tokens.1 = bf16[8,4,24,896]{3,2,1,0:T(8,128)(2,1)} custom-call(f32[4,192,1]{2,1,0:T(8,128)S(1)} %reshape.290.index_ref, bf16[4,512,1792]{2,1,0:T(8,128)(2,1)} %bitcast.54), custom_call_target="tpu_custom_call" | custom-call | tf_op jit(solution)/shard_map/pick_tokens/pallas_call | solution.py:91
  126.4 16.2 %all-to-all-done.3 = bf16[32,24,896]{2,1,0:T(8,128)(2,1)S(1)} async-done(((bf16[32,24,896]{2,1,0:T(8,128)(2,1)}), bf16[32,24,896]{2,1,0:T(8,128)(2,1)S(1)}, u32[]{:S(2)}, u32[]{:S(2)}) %all-to-all-start.3) | async-done | bytes 1376288 | tf_op jit(solution)/shard_map/all_to_all | solution.py:369
  142.7 5.4 %all-to-all-start.4 = ((bf16[8,96,896]{2,1,0:T(8,128)(2,1)}), bf16[8,96,896]{2,1,0:T(8,128)(2,1)S(1)}, u32[]{:S(2)}, u32[]{:S(2)}) async-start(bf16[8,96,896]{2,1,0:T(8,128)(2,1)} %bitcast.21), calls=%async_computation.4 | async-start | bytes 2752512 | tf_op jit(solution)/shard_map/all_to_all | solution.py:376
  149.2 5.1 %hidden_step.1 = (bf16[192,1024]{1,0:T(8,128)(2,1)}, f32[192,1]{1,0:T(8,128)}) custom-call(bf16[4,192,896]{2,1,0:T(8,128)(2,1)S(1)} %bitcast.51, bf16[4,3584,256]{2,1,0:T(8,128)(2,1)} %bitcast_dynamic-update-slice_fusion.3.matrix_ref, f32[4,192,256]{2,1,0:T(8,128)S(1)} %copy-done, f32[4,192,256]{2,1,0:T(8,128)S(1)} %get-tuple-element.27.dw_act_ref), custom_call_target="tpu_custom_call" | custom-call | tf_op jit(solution)/shard_map/hidden_step/pallas_call | solution.py:169
  158.3 9.9 %collective-permute-done.4.west_ref.west_hbm = bf16[192,1024]{1,0:T(8,128)(2,1)S(1)} collective-permute-done((bf16[192,1024]{1,0:T(8,128)(2,1)}, bf16[192,1024]{1,0:T(8,128)(2,1)S(1)}, u32[]{:S(2)}, u32[]{:S(2)}) %collective-permute-start.4) | collective-permute-done | bytes 393248 | tf_op jit(solution)/shard_map/ppermute | solution.py:63
  171.3 4.5 %collective-permute-start.8 = (bf16[192,1664]{1,0:T(8,128)(2,1)}, bf16[192,1664]{1,0:T(8,128)(2,1)S(1)}, u32[]{:S(2)}, u32[]{:S(2)}) collective-permute-start(bf16[192,1664]{1,0:T(8,128)(2,1)} %get-tuple-element.35), channel_id=1, source_target_pairs={{0,3},{1,2},{2,1},{3,0},{4,7},{5,6},{6,5},{7,4},{8,11},{9,10},{10,... | collective-permute-start | bytes 1916936 | tf_op jit(solution)/shard_map/ppermute | solution.py:63
  180.1 8.6 %all-to-all-start.5 = ((f32[16,8,128]{2,1,0:T(8,128)}), f32[16,8,128]{2,1,0:T(8,128)S(1)}, u32[]{:S(2)}, u32[]{:S(2)}) async-start(f32[16,8,128]{2,1,0:T(8,128)} %pad_dynamic-update-slice_fusion), calls=%async_computation.5 | async-start | bytes 131072 | tf_op jit(solution)/shard_map/all_to_all | solution.py:392
  194.3 3.6 %collective-permute-start.7 = (bf16[192,1152]{1,0:T(8,128)(2,1)}, bf16[192,1152]{1,0:T(8,128)(2,1)S(1)}, u32[]{:S(2)}, u32[]{:S(2)}) collective-permute-start(bf16[192,1152]{1,0:T(8,128)(2,1)} %slice_add_fusion.1.low_a), channel_id=1, source_target_pairs={{0,3},{1,2},{2,1},{3,0},{4,7},{5,6},{6,5},{7,4},{8,11},{9,10},{10,... | collective-permute-start | bytes 1327112 | tf_op jit(solution)/shard_map/ppermute | solution.py:63
  201.0 9.1 %all-to-all-start.6 = ((f32[32,1,96]{2,1,0:T(1,128)}), f32[32,1,96]{2,1,0:T(1,128)S(1)}, u32[]{:S(2)}, u32[]{:S(2)}) async-start(f32[32,1,96]{2,1,0:T(1,128)} %bitcast.25), calls=%async_computation.6 | async-start | bytes 32768 | tf_op jit(solution)/shard_map/all_to_all | solution.py:395
  210.9 12.6 %last_step.1 = bf16[1,896,1024]{2,1,0:T(8,128)(2,1)} custom-call(s32[1]{0:T(128)} %bitcast.27.rank_ref, bf16[896,768]{1,0:T(8,128)(2,1)} %get-tuple-element.33.rows_t_hbm, bf16[192,1024]{1,0:T(8,128)(2,1)} %get-tuple-element.30.own_hbm, bf16[192,1152]{1,0:T(8,128)(2,1)} %slice_add_fusion.1.low_a, bf16[192,1152]{1,0:T(8,128)(2,1)} %copy-done.6, ...), custom_call_target="tpu_custom_call" | custom-call | tf_op jit(solution)/shard_map/last_step/pallas_call | solution.py:280
  (98 shorter events, 52.4 us)
Async XLA Ops:
  7.2 30.9 %copy-start.10 = (bf16[1,768,256]{2,1,0:T(8,128)(2,1)S(1)}, bf16[1,768,256]{2,1,0:T(8,128)(2,1)}, u32[]{:S(2)}) copy-start(bf16[1,768,256]{2,1,0:T(8,128)(2,1)} %param.12) | copy-start | bytes 1179652
  7.2 30.9 %copy-start.9 = (bf16[1,768,256]{2,1,0:T(8,128)(2,1)S(1)}, bf16[1,768,256]{2,1,0:T(8,128)(2,1)}, u32[]{:S(2)}) copy-start(bf16[1,768,256]{2,1,0:T(8,128)(2,1)} %param.13) | copy-start | bytes 1179652
  7.2 104.4 %all-gather.2.cloned.1.call-start = ((), (), s32[]{:S(2)}) async-start(), calls=%async_computation.7 | async-start | bytes 7798784 | tf_op jit(solution)/shard_map/all_gather | solution.py:314
  13.0 50.3 %collective-permute-start = (bf16[3584,256]{1,0:T(8,128)(2,1)}, bf16[3584,256]{1,0:T(8,128)(2,1)}, u32[]{:S(2)}, u32[]{:S(2)}) collective-permute-start(bf16[3584,256]{1,0:T(8,128)(2,1)} %bitcast.4), channel_id=1, source_target_pairs={{0,1},{1,2},{2,3},{3,0},{4,5},{5,6},{6,7},{7,4},{8,9},{9,10},{10,1... | collective-permute-start | bytes 5505032 | tf_op jit(solution)/shard_map/ppermute | solution.py:37
  17.0 46.3 %collective-permute-start.1 = (bf16[3584,256]{1,0:T(8,128)(2,1)}, bf16[3584,256]{1,0:T(8,128)(2,1)}, u32[]{:S(2)}, u32[]{:S(2)}) collective-permute-start(bf16[3584,256]{1,0:T(8,128)(2,1)} %bitcast.4), channel_id=1, source_target_pairs={{0,3},{1,0},{2,1},{3,2},{4,7},{5,4},{6,5},{7,6},{8,11},{9,8},{10,9... | collective-permute-start | bytes 5505032 | tf_op jit(solution)/shard_map/ppermute | solution.py:37
  23.1 26.4 %all-to-all-start = ((f32[16,2,48]{2,1,0:T(2,128)}), f32[16,2,48]{2,1,0:T(2,128)S(1)}, u32[]{:S(2)}, u32[]{:S(2)}) async-start(f32[16,2,48]{2,1,0:T(2,128)} %copy.52), calls=%async_computation | async-start | bytes 32768 | tf_op jit(solution)/shard_map/all_to_all | solution.py:330
  50.5 11.5 %all-to-all-start.2 = ((f32[8,1,24]{2,1,0:T(1,128)}), f32[8,1,24]{2,1,0:T(1,128)S(1)}, u32[]{:S(2)}, u32[]{:S(2)}) async-start(f32[8,1,24]{2,1,0:T(1,128)} %bitcast.16), calls=%async_computation.2 | async-start | bytes 8192 | tf_op jit(solution)/shard_map/all_to_all | solution.py:340
  65.5 34.3 %collective-permute-start.2 = (bf16[1792,256]{1,0:T(8,128)(2,1)}, bf16[1792,256]{1,0:T(8,128)(2,1)}, u32[]{:S(2)}, u32[]{:S(2)}) collective-permute-start(bf16[1792,256]{1,0:T(8,128)(2,1)} %slice.35), channel_id=1, source_target_pairs={{0,1},{1,2},{2,3},{3,0},{4,5},{5,6},{6,7},{7,4},{8,9},{9,10},{10,1... | collective-permute-start | bytes 2752520 | tf_op jit(solution)/shard_map/ppermute | solution.py:37
  68.7 33.2 %collective-permute-start.3 = (bf16[1792,256]{1,0:T(8,128)(2,1)S(1)}, bf16[1792,256]{1,0:T(8,128)(2,1)}, u32[]{:S(2)}, u32[]{:S(2)}) collective-permute-start(bf16[1792,256]{1,0:T(8,128)(2,1)S(1)} %slice.36), channel_id=1, source_target_pairs={{0,3},{1,0},{2,1},{3,2},{4,7},{5,4},{6,5},{7,6},{8,11},{9,8},{10,9... | collective-permute-start | bytes 2752520 | tf_op jit(solution)/shard_map/ppermute | solution.py:37
  73.2 25.4 %all-to-all-start.1 = ((bf16[4,192,512]{2,1,0:T(8,128)(2,1)}), bf16[4,192,512]{2,1,0:T(8,128)(2,1)S(1)}, u32[]{:S(2)}, u32[]{:S(2)}) async-start(bf16[4,192,512]{2,1,0:T(8,128)(2,1)} %bitcast.13), calls=%async_computation.1 | async-start | bytes 1572864 | tf_op jit(solution)/shard_map/all_to_all | solution.py:356
  115.2 27.4 %all-to-all-start.3 = ((bf16[32,24,896]{2,1,0:T(8,128)(2,1)}), bf16[32,24,896]{2,1,0:T(8,128)(2,1)S(1)}, u32[]{:S(2)}, u32[]{:S(2)}) async-start(bf16[32,24,896]{2,1,0:T(8,128)(2,1)} %bitcast.18), calls=%async_computation.3 | async-start | bytes 2752512 | tf_op jit(solution)/shard_map/all_to_all | solution.py:369
  142.7 26.1 %all-to-all-start.4 = ((bf16[8,96,896]{2,1,0:T(8,128)(2,1)}), bf16[8,96,896]{2,1,0:T(8,128)(2,1)S(1)}, u32[]{:S(2)}, u32[]{:S(2)}) async-start(bf16[8,96,896]{2,1,0:T(8,128)(2,1)} %bitcast.21), calls=%async_computation.4 | async-start | bytes 2752512 | tf_op jit(solution)/shard_map/all_to_all | solution.py:376
  154.3 14.0 %collective-permute-start.4 = (bf16[192,1024]{1,0:T(8,128)(2,1)}, bf16[192,1024]{1,0:T(8,128)(2,1)S(1)}, u32[]{:S(2)}, u32[]{:S(2)}) collective-permute-start(bf16[192,1024]{1,0:T(8,128)(2,1)} %get-tuple-element.30.own_hbm), channel_id=1, source_target_pairs={{0,3},{1,2},{2,1},{3,0},{4,7},{5,6},{6,5},{7,4},{8,11},{9,10},{10,... | collective-permute-start | bytes 1179656 | tf_op jit(solution)/shard_map/ppermute | solution.py:63
  156.2 12.5 %collective-permute-start.5 = (bf16[192,1024]{1,0:T(8,128)(2,1)}, bf16[192,1024]{1,0:T(8,128)(2,1)S(1)}, u32[]{:S(2)}, u32[]{:S(2)}) collective-permute-start(bf16[192,1024]{1,0:T(8,128)(2,1)} %get-tuple-element.30.own_hbm), channel_id=1, source_target_pairs={{0,1},{1,0},{2,3},{3,2},{4,5},{5,4},{6,7},{7,6},{8,9},{9,8},{10,11... | collective-permute-start | bytes 1179656 | tf_op jit(solution)/shard_map/ppermute | solution.py:63
  168.3 41.8 %copy-start.1 = (bf16[192,1024]{1,0:T(8,128)(2,1)}, bf16[192,1024]{1,0:T(8,128)(2,1)S(1)}, u32[]{:S(2)}) copy-start(bf16[192,1024]{1,0:T(8,128)(2,1)S(1)} %collective-permute-done.4.west_ref.west_hbm) | copy-start | bytes 1179652
  168.7 41.4 %copy-start.2 = (bf16[192,1024]{1,0:T(8,128)(2,1)}, bf16[192,1024]{1,0:T(8,128)(2,1)S(1)}, u32[]{:S(2)}) copy-start(bf16[192,1024]{1,0:T(8,128)(2,1)S(1)} %collective-permute-done.5.east_ref.east_hbm) | copy-start | bytes 1179652
  171.3 18.1 %collective-permute-start.8 = (bf16[192,1664]{1,0:T(8,128)(2,1)}, bf16[192,1664]{1,0:T(8,128)(2,1)S(1)}, u32[]{:S(2)}, u32[]{:S(2)}) collective-permute-start(bf16[192,1664]{1,0:T(8,128)(2,1)} %get-tuple-element.35), channel_id=1, source_target_pairs={{0,3},{1,2},{2,1},{3,0},{4,7},{5,6},{6,5},{7,4},{8,11},{9,10},{10,... | collective-permute-start | bytes 1916936 | tf_op jit(solution)/shard_map/ppermute | solution.py:63
  175.8 17.6 %collective-permute-start.6 = (bf16[192,1664]{1,0:T(8,128)(2,1)S(1)}, bf16[192,1664]{1,0:T(8,128)(2,1)S(1)}, u32[]{:S(2)}, u32[]{:S(2)}) collective-permute-start(bf16[192,1664]{1,0:T(8,128)(2,1)S(1)} %get-tuple-element.34), channel_id=1, source_target_pairs={{0,1},{1,0},{2,3},{3,2},{4,5},{5,4},{6,7},{7,6},{8,9},{9,8},{10,11... | collective-permute-start | bytes 1916936 | tf_op jit(solution)/shard_map/ppermute | solution.py:63
  180.1 20.2 %all-to-all-start.5 = ((f32[16,8,128]{2,1,0:T(8,128)}), f32[16,8,128]{2,1,0:T(8,128)S(1)}, u32[]{:S(2)}, u32[]{:S(2)}) async-start(f32[16,8,128]{2,1,0:T(8,128)} %pad_dynamic-update-slice_fusion), calls=%async_computation.5 | async-start | bytes 131072 | tf_op jit(solution)/shard_map/all_to_all | solution.py:392
  189.4 20.7 %copy-start.3 = (bf16[192,1664]{1,0:T(8,128)(2,1)}, bf16[192,1664]{1,0:T(8,128)(2,1)S(1)}, u32[]{:S(2)}) copy-start(bf16[192,1664]{1,0:T(8,128)(2,1)S(1)} %collective-permute-done.8.far_high) | copy-start | bytes 1916932
  190.7 19.5 %copy-start.5 = (bf16[192,1152]{1,0:T(8,128)(2,1)}, bf16[192,1152]{1,0:T(8,128)(2,1)S(1)}, u32[]{:S(2)}) copy-start(bf16[192,1152]{1,0:T(8,128)(2,1)S(1)} %slice_add_fusion.high_a) | copy-start | bytes 1327108
  190.7 19.4 %collective-permute-start.9 = (bf16[192,1152]{1,0:T(8,128)(2,1)S(1)}, bf16[192,1152]{1,0:T(8,128)(2,1)}, u32[]{:S(2)}, u32[]{:S(2)}) collective-permute-start(bf16[192,1152]{1,0:T(8,128)(2,1)S(1)} %slice_add_fusion.high_a), channel_id=1, source_target_pairs={{0,1},{1,0},{2,3},{3,2},{4,5},{5,4},{6,7},{7,6},{8,9},{9,8},{10,11... | collective-permute-start | bytes 1327112 | tf_op jit(solution)/shard_map/ppermute | solution.py:63
  194.3 15.8 %collective-permute-start.7 = (bf16[192,1152]{1,0:T(8,128)(2,1)}, bf16[192,1152]{1,0:T(8,128)(2,1)S(1)}, u32[]{:S(2)}, u32[]{:S(2)}) collective-permute-start(bf16[192,1152]{1,0:T(8,128)(2,1)} %slice_add_fusion.1.low_a), channel_id=1, source_target_pairs={{0,3},{1,2},{2,1},{3,0},{4,7},{5,6},{6,5},{7,4},{8,11},{9,10},{10,... | collective-permute-start | bytes 1327112 | tf_op jit(solution)/shard_map/ppermute | solution.py:63
  201.0 22.4 %all-to-all-start.6 = ((f32[32,1,96]{2,1,0:T(1,128)}), f32[32,1,96]{2,1,0:T(1,128)S(1)}, u32[]{:S(2)}, u32[]{:S(2)}) async-start(f32[32,1,96]{2,1,0:T(1,128)} %bitcast.25), calls=%async_computation.6 | async-start | bytes 32768 | tf_op jit(solution)/shard_map/all_to_all | solution.py:395
  (5 other events, 45.3 us)
Sparse Core Ops, SparseCore 0:
  10.1 101.4 all-gather.1

commit v7 on v6

--- a/solution.py
+++ b/solution.py
@@ -102,6 +102,17 @@
     )(index, column)
 
 
+TRIANGLE = ((0, 3, 4), (1, 2, 5))
+
+
+def triangle(which):
+    first, places = 0, []
+    for i in TRIANGLE[which]:
+        places.append((i, first))
+        first += 6 - i
+    return places, first
+
+
 def inner_kernel(recv_ref, west_ref, east_ref, rows_t_ref, low_ref, high_ref, rows_ref):
     near, quarters, piece, feats = recv_ref.shape
     own, hidden = west_ref.shape
@@ -109,29 +120,33 @@
         rows_ref[q * own : (q + 1) * own] = (
             recv_ref[:, q].astype(f32).reshape(own, feats).astype(bf16)
         )
-    half = 2 * own
-    top, end = rows_ref[:half], rows_ref[half:]
-    first = dot(top, top, ((1,), (1,))).astype(bf16)
-    cross = dot(top, end, ((1,), (1,))).astype(bf16)
-    last = dot(end, end, ((1,), (1,))).astype(bf16)
-    low_ref[:, :half] = first[:own]
-    low_ref[:, half : 2 * half] = first[own:]
-    low_ref[:, 2 * half : 3 * half] = cross[:own]
-    high_ref[:, :half] = cross[own:]
-    high_ref[:, half : 2 * half] = last[:own]
-    high_ref[:, 2 * half : 3 * half] = last[own:]
-    low_ref[:, 3 * half :] = west_ref[:, : hidden // 2]
-    high_ref[:, 3 * half :] = east_ref[:, hidden // 2 :]
+    side = quarters * own // 6
+    lanes = hidden // 2
+    for which, out, riding in ((0, low_ref, west_ref), (1, high_ref, east_ref)):
+        places, blocks = triangle(which)
+        for i, first in places:
+            part = dot(rows_ref[i * side : (i + 1) * side], rows_ref[i * side :], ((1,), (1,)))
+            out[:, first * side : (first + 6 - i) * side] = part.astype(bf16)
+        end, base = blocks * side, which * lanes
+        out[:, end : end + lanes] = riding[:side, base : base + lanes]
+        end += lanes
+        for j in range(2):
+            spread = riding[side:, base + j * lanes // 2 : base + (j + 1) * lanes // 2]
+            out[j * side // 2 : (j + 1) * side // 2, end : end + lanes // 2] = spread
     rows_t_ref[...] = rows_ref[...].T
 
 
 def inner_products(recv, west, east):
     near, quarters, piece, feats = recv.shape
     own, hidden = west.shape
-    pack = jax.ShapeDtypeStruct((own, 6 * own + hidden // 2), bf16)
+    side = quarters * own // 6
+    packs = [
+        jax.ShapeDtypeStruct((side, triangle(i)[1] * side + 3 * hidden // 4), bf16)
+        for i in range(2)
+    ]
     return pl.pallas_call(
         inner_kernel,
-        out_shape=[pltpu.HBM((feats, quarters * own), bf16), pack, pack],
+        out_shape=[pltpu.HBM((feats, quarters * own), bf16), *packs],
         scratch_shapes=[pltpu.VMEM((quarters * own, feats), bf16)],
         compiler_params=pltpu.CompilerParams(vmem_limit_bytes=20 * MIB),
         name="inner_products",
@@ -187,33 +202,38 @@
     rank_ref, rows_t_hbm, own_hbm, low_a, low_b, high_a, high_b, west_hbm, east_hbm,
     far_low, far_high, out_ref,
     up_ref, inner_ref, carried_ref, gram_ref, square_ref, poly_ref, start_ref, rows_t_ref,
-    packs_ref, sems,
+    low_ref, high_ref, sems, up_t_ref,
 ):
     rank = rank_ref[0]
     own = west_hbm.shape[0]
     slots, hidden = up_ref.shape
     feats = rows_t_ref.shape[0]
-    half = slots // 2
+    side, lanes = slots // 6, hidden // 2
     near = rank + 1 - 2 * lax.rem(rank, 2)
 
-    def owned(owner):
-        return pl.ds(pl.multiple_of(owner * own, own), own)
-
-    far = owned(3 - near)
-    first, second = pl.ds(0, hidden // 2), pl.ds(hidden // 2, hidden // 2)
-    riding = pl.ds(3 * half, hidden // 2)
+    def owned(owner, first=0, rows=own):
+        return pl.ds(pl.multiple_of(owner * own + first, 16), rows)
+
     moves = [
-        (low_a, packs_ref.at[0]),
-        (low_b, packs_ref.at[1]),
-        (high_a, packs_ref.at[2]),
-        (high_b, packs_ref.at[3]),
+        (low_a, low_ref.at[0]),
+        (low_b, low_ref.at[1]),
+        (high_a, high_ref.at[0]),
+        (high_b, high_ref.at[1]),
         (own_hbm, up_ref.at[owned(rank)]),
         (west_hbm, up_ref.at[owned(3 - rank)]),
         (east_hbm, up_ref.at[owned(near)]),
-        (far_low.at[:, riding], up_ref.at[far, first]),
-        (far_high.at[:, riding], up_ref.at[far, second]),
-        (rows_t_hbm, rows_t_ref),
     ]
+    for which, source in ((0, far_low), (1, far_high)):
+        end, base = triangle(which)[1] * side, which * lanes
+        place = up_ref.at[owned(3 - near, 0, side), pl.ds(base, lanes)]
+        moves.append((source.at[:, pl.ds(end, lanes)], place))
+        end += lanes
+        for j in range(2):
+            rows = pl.ds(j * side // 2, side // 2)
+            place = pl.ds(base + j * lanes // 2, lanes // 2)
+            place = up_ref.at[owned(3 - near, side, side // 2), place]
+            moves.append((source.at[rows, pl.ds(end, lanes // 2)], place))
+    moves.append((rows_t_hbm, rows_t_ref))
     copies = [
         pltpu.make_async_copy(source, place, sems.at[i])
         for i, (source, place) in enumerate(moves)
@@ -222,23 +242,19 @@
         copy.start()
     for copy in copies[:4]:
         copy.wait()
-
-    def summed(one, i):
-        lanes = slice(i * half, (i + 1) * half)
-        return packs_ref[one, :, lanes].astype(f32) + packs_ref[one + 1, :, lanes].astype(f32)
-
-    low = [summed(0, i) for i in range(3)]
-    high = [summed(2, i) for i in range(3)]
-    cross = jnp.concatenate([low[2], high[0]], axis=0)
-    for i in range(2):
-        inner_ref[i * own : (i + 1) * own, :half] = low[i].astype(bf16)
-        inner_ref[half + i * own : half + (i + 1) * own, half:] = high[1 + i].astype(bf16)
-    inner_ref[:half, half:] = cross.astype(bf16)
-    inner_ref[half:, :half] = cross.T.astype(bf16)
-    for copy in copies[4:9]:
+    for which, packs in ((0, low_ref), (1, high_ref)):
+        for i, first in triangle(which)[0]:
+            at = slice(first * side, (first + 6 - i) * side)
+            part = (packs[0, :, at].astype(f32) + packs[1, :, at].astype(f32)).astype(bf16)
+            inner_ref[i * side : (i + 1) * side, i * side :] = part
+            for j in range(i + 1, 6):
+                block = part[:, (j - i) * side : (j - i + 1) * side].T
+                inner_ref[j * side : (j + 1) * side, i * side : (i + 1) * side] = block
+    for copy in copies[4:13]:
         copy.wait()
+    up_t_ref[...] = up_ref[...].T
     norm = jnp.zeros((1, 1), f32)
-    step = slots // 3
+    step = slots // 2
     for i in range(0, slots, step):
         carried = dot(inner_ref[i : i + step], up_ref[...], ((1,), (0,)))
         norm = norm + total(carried * up_ref[i : i + step].astype(f32))
@@ -246,15 +262,18 @@
     scale = 1.0 / (1.01 * jnp.sqrt(jnp.maximum(norm, 0.0)) + 1e-07)
     step = hidden // 4
     for i in range(0, hidden, step):
-        gram = dot(up_ref[:, i : i + step], carried_ref[...], ((0,), (0,)))
-        gram_ref[i : i + step] = (gram * scale * scale).astype(bf16)
+        gram = dot(up_t_ref[i : i + step], carried_ref[:, i:], ((1,), (0,)))
+        gram = (gram * scale * scale).astype(bf16)
+        gram_ref[i : i + step, i:] = gram
+        for j in range(i + step, hidden, step):
+            gram_ref[j : j + step, i : i + step] = gram[:, j - i : j - i + step].T
     quartic = jnp.zeros((1, 1), f32)
     for i in range(0, hidden, step):
-        square = dot(gram_ref[i : i + step], gram_ref[...], ((1,), (0,)))
-        quartic = quartic + total(square * square)
-        square_ref[i : i + step] = square
-    rows = feats // 4
-    copies[9].wait()
+        square = dot(gram_ref[i : i + step], gram_ref[:, i:], ((1,), (0,)))
+        quartic = quartic + 2.0 * total(square * square) - total(square[:, :step] * square[:, :step])
+        square_ref[i : i + step, i:] = square
+    rows = feats // 2
+    copies[13].wait()
     for i in range(0, feats, rows):
         gradient = dot(rows_t_ref[i : i + rows], up_ref[...], ((1,), (0,)))
         start_ref[i : i + rows] = (gradient * scale).astype(bf16)
@@ -262,10 +281,13 @@
     first_scale = poly_third / bound
     second_scale = poly_fifth / (bound * bound)
     for i in range(0, hidden, step):
-        poly_ref[i : i + step] = (
-            first_scale * gram_ref[i : i + step].astype(f32)
-            + second_scale * square_ref[i : i + step]
+        poly = (
+            first_scale * gram_ref[i : i + step, i:].astype(f32)
+            + second_scale * square_ref[i : i + step, i:]
         ).astype(bf16)
+        poly_ref[i : i + step, i:] = poly
+        for j in range(i + step, hidden, step):
+            poly_ref[j : j + step, i : i + step] = poly[:, j - i : j - i + step].T
     for i in range(0, feats, rows):
         start = start_ref[i : i + rows]
         mixed = dot(start, poly_ref[...], ((1,), (0,)))
@@ -291,8 +313,10 @@
             pltpu.VMEM((hidden, hidden), bf16),
             pltpu.VMEM((feats, hidden), bf16),
             pltpu.VMEM((feats, slots), bf16),
-            pltpu.VMEM((4,) + packs[0].shape, bf16),
-            pltpu.SemaphoreType.DMA((10,)),
+            pltpu.VMEM((2,) + packs[0].shape, bf16),
+            pltpu.VMEM((2,) + packs[2].shape, bf16),
+            pltpu.SemaphoreType.DMA((14,)),
+            pltpu.VMEM((hidden, slots), bf16),
         ],
         compiler_params=pltpu.CompilerParams(vmem_limit_bytes=56 * MIB),
         name="last_step",
@@ -377,9 +401,10 @@
         token_send.reshape(near, nz * CAP, feats), ("x", "c"), 0, 0, tiled=True
     ).reshape(near, ny, zl * CAP, feats)
     rows_t, low, high = inner_products(rows, west, east)
-    size = 6 * own_slots
     low_near, high_near = swap(low, beside), swap(high, across)
-    low, high = low[:, :size] + low_near[:, :size], high[:, :size] + high_near[:, :size]
+    low_size, high_size = (triangle(i)[1] * (slots // 6) for i in range(2))
+    low = low[:, :low_size] + low_near[:, :low_size]
+    high = high[:, :high_size] + high_near[:, :high_size]
     packs = (low, swap(low, across), high, swap(high, beside))
     ups = (west, east, low_near, high_near)
 

time: 233 us -> 231 us (level)
  waiting for transfers between devices: 60.6 us -> 63.6 us
  starting transfers between devices: 86.6 us -> 84.2 us
    all_to_all x1, waiting for transfers between devices: 2.32 us -> 6.08 us  [on_device(): back = lax.all_to_all(back, 'z', 0, 0, tiled=True)[:, :, :CAP]]
    unnamed x26 -> x28, local copies, waits for them, and re-layouts: 6.47 us -> 6.51 us
  transfers between devices with their start and end apart: 18 -> 18, of which waited for: 9 -> 8; matrix products, arithmetic and copies ran while one was open for 16% -> 15% of each run, Pallas kernels for 9% -> 8%
where the time goes in v7:
time: 231 us; the launch traced here: 230 us
  starting transfers between devices  84.2 us (36%)
  waiting for transfers between devices  63.6 us (28%)
  local copies, waits for them, and re-layouts  32.2 us (14%)
  Pallas kernels  25.6 us (11%)
  between operations  14.5 us (6%)
  other arithmetic  7.96 us (3%)
    all_to_all x1, waiting for transfers between devices, on_device(): lax.all_to_all(grad_send.reshape(ny * near, zl * CAP, feats), ('y', 'x',...  16.2 us
    all_to_all x1, waiting for transfers between devices, on_device(): lax.all_to_all(saved.reshape(ny, own_slots, 2 * hidden_part), 'y', 0, 0,...  16.1 us
    ppermute x6, starting transfers between devices, swap(): return lax.ppermute(values, 'y', [(i, partner(i)) for i in range(size)])  15.1 us
    all_to_all x1, starting transfers between devices, on_device(): lax.all_to_all(jnp.stack([index_send.reshape(nz, near * CAP), weight_send...  14.9 us
    ppermute x4, starting transfers between devices, shift(): lax.ppermute(values, 'y', [(i, (i + step) % size) for i in range(size)])  13.9 us
    dynamic_update_slice x5, local copies, waits for them, and re-layouts, gather_weights(): whole = lax.dynamic_update_slice(whole, part[None], (place, row, 0))  13 us
    pallas_call x1, Pallas kernels, last_step(): pl.pallas_call(last_kernel, in_specs=[pl.BlockSpec(memory_space=pltpu.SME...  10.7 us
    ppermute x6, waiting for transfers between devices, swap(): return lax.ppermute(values, 'y', [(i, partner(i)) for i in range(size)])  10.4 us
  transfers between devices with their start and end apart: 18, of which 8 were waited for; matrix products, arithmetic and copies ran while one was open for 15% of the time, Pallas kernels for 8%

profile of v7, /device:TPU:1, one launch (start us, length us, event | category | flops | bytes accessed | tf_op | source)
XLA Modules:
  0.0 229.7 jit_solution(17636333741903747817)
XLA Ops:
  9.2 3.8 %copy.56 = bf16[1,256,3584]{1,2,0:T(8,128)(2,1)} copy(bf16[1,256,3584]{2,1,0:T(8,128)(2,1)} %param.11) | data formatting | bytes 3670016 | tf_op args[4]
  13.0 4.0 %collective-permute-start = (bf16[3584,256]{1,0:T(8,128)(2,1)}, bf16[3584,256]{1,0:T(8,128)(2,1)}, u32[]{:S(2)}, u32[]{:S(2)}) collective-permute-start(bf16[3584,256]{1,0:T(8,128)(2,1)} %bitcast.4), channel_id=1, source_target_pairs={{0,1},{1,2},{2,3},{3,0},{4,5},{5,6},{6,7},{7,4},{8,9},{9,10},{10,1... | collective-permute-start | bytes 5505032 | tf_op jit(solution)/shard_map/ppermute | solution.py:37
  17.0 3.4 %collective-permute-start.1 = (bf16[3584,256]{1,0:T(8,128)(2,1)}, bf16[3584,256]{1,0:T(8,128)(2,1)}, u32[]{:S(2)}, u32[]{:S(2)}) collective-permute-start(bf16[3584,256]{1,0:T(8,128)(2,1)} %bitcast.4), channel_id=1, source_target_pairs={{0,3},{1,0},{2,1},{3,2},{4,7},{5,4},{6,5},{7,6},{8,11},{9,8},{10,9... | collective-permute-start | bytes 5505032 | tf_op jit(solution)/shard_map/ppermute | solution.py:37
  23.1 14.9 %all-to-all-start = ((f32[16,2,48]{2,1,0:T(2,128)}), f32[16,2,48]{2,1,0:T(2,128)S(1)}, u32[]{:S(2)}, u32[]{:S(2)}) async-start(f32[16,2,48]{2,1,0:T(2,128)} %copy.52), calls=%async_computation | async-start | bytes 32768 | tf_op jit(solution)/shard_map/all_to_all | solution.py:354
  39.8 3.5 %broadcast_in_dim.81 = bf16[4,3584,256]{2,1,0:T(8,128)(2,1)} broadcast(bf16[]{:T(256)} %constant.173.clone.1), dimensions={} | broadcast | bytes 7340034 | tf_op jit(solution)/shard_map/broadcast_in_dim | solution.py:49
  46.2 3.2 %all-to-all-done = f32[16,2,48]{2,1,0:T(2,128)S(1)} async-done(((f32[16,2,48]{2,1,0:T(2,128)}), f32[16,2,48]{2,1,0:T(2,128)S(1)}, u32[]{:S(2)}, u32[]{:S(2)}) %all-to-all-start) | async-done | bytes 6176 | tf_op jit(solution)/shard_map/all_to_all | solution.py:354
  50.4 7.0 %all-to-all-start.2 = ((f32[8,1,24]{2,1,0:T(1,128)}), f32[8,1,24]{2,1,0:T(1,128)S(1)}, u32[]{:S(2)}, u32[]{:S(2)}) async-start(f32[8,1,24]{2,1,0:T(1,128)} %bitcast.16), calls=%async_computation.2 | async-start | bytes 8192 | tf_op jit(solution)/shard_map/all_to_all | solution.py:364
  58.0 4.1 %all-to-all-done.2 = f32[8,1,24]{2,1,0:T(1,128)S(1)} async-done(((f32[8,1,24]{2,1,0:T(1,128)}), f32[8,1,24]{2,1,0:T(1,128)S(1)}, u32[]{:S(2)}, u32[]{:S(2)}) %all-to-all-start.2) | async-done | bytes 800 | tf_op jit(solution)/shard_map/all_to_all | solution.py:364
  68.7 4.5 %collective-permute-start.3 = (bf16[1792,256]{1,0:T(8,128)(2,1)S(1)}, bf16[1792,256]{1,0:T(8,128)(2,1)}, u32[]{:S(2)}, u32[]{:S(2)}) collective-permute-start(bf16[1792,256]{1,0:T(8,128)(2,1)S(1)} %slice.36), channel_id=1, source_target_pairs={{0,3},{1,0},{2,1},{3,2},{4,7},{5,4},{6,5},{7,6},{8,11},{9,8},{10,9... | collective-permute-start | bytes 2752520 | tf_op jit(solution)/shard_map/ppermute | solution.py:37
  73.2 3.5 %all-to-all-start.1 = ((bf16[4,192,512]{2,1,0:T(8,128)(2,1)}), bf16[4,192,512]{2,1,0:T(8,128)(2,1)S(1)}, u32[]{:S(2)}, u32[]{:S(2)}) async-start(bf16[4,192,512]{2,1,0:T(8,128)(2,1)} %bitcast.13), calls=%async_computation.1 | async-start | bytes 1572864 | tf_op jit(solution)/shard_map/all_to_all | solution.py:380
  82.5 16.1 %all-to-all-done.1 = bf16[4,192,512]{2,1,0:T(8,128)(2,1)S(1)} async-done(((bf16[4,192,512]{2,1,0:T(8,128)(2,1)}), bf16[4,192,512]{2,1,0:T(8,128)(2,1)S(1)}, u32[]{:S(2)}, u32[]{:S(2)}) %all-to-all-start.1) | async-done | bytes 786464 | tf_op jit(solution)/shard_map/all_to_all | solution.py:380
  104.1 7.5 %all-gather.2.cloned.1.call-done = bf16[2048,1792]{1,0:T(8,128)(2,1)} async-done(((bf16[128,1792]{1,0:T(8,128)(2,1)}), bf16[2048,1792]{1,0:T(8,128)(2,1)}) %all-gather.2.cloned.1.call-update) | async-done | bytes 7340048 | tf_op jit(solution)/shard_map/all_gather | solution.py:338
  111.6 3.7 %pick_grads.1 = bf16[4,8,24,896]{3,2,1,0:T(8,128)(2,1)} custom-call(f32[4,192,1]{2,1,0:T(8,128)S(1)} %reshape.290.index_ref, bf16[4,512,1792]{2,1,0:T(8,128)(2,1)} %bitcast.53), custom_call_target="tpu_custom_call" | custom-call | tf_op jit(solution)/shard_map/pick_grads/pallas_call | solution.py:91
  115.2 7.5 %all-to-all-start.3 = ((bf16[32,24,896]{2,1,0:T(8,128)(2,1)}), bf16[32,24,896]{2,1,0:T(8,128)(2,1)S(1)}, u32[]{:S(2)}, u32[]{:S(2)}) async-start(bf16[32,24,896]{2,1,0:T(8,128)(2,1)} %bitcast.18), calls=%async_computation.3 | async-start | bytes 2752512 | tf_op jit(solution)/shard_map/all_to_all | solution.py:393
  122.8 3.7 %pick_tokens.1 = bf16[8,4,24,896]{3,2,1,0:T(8,128)(2,1)} custom-call(f32[4,192,1]{2,1,0:T(8,128)S(1)} %reshape.290.index_ref, bf16[4,512,1792]{2,1,0:T(8,128)(2,1)} %bitcast.54), custom_call_target="tpu_custom_call" | custom-call | tf_op jit(solution)/shard_map/pick_tokens/pallas_call | solution.py:91
  126.4 16.2 %all-to-all-done.3 = bf16[32,24,896]{2,1,0:T(8,128)(2,1)S(1)} async-done(((bf16[32,24,896]{2,1,0:T(8,128)(2,1)}), bf16[32,24,896]{2,1,0:T(8,128)(2,1)S(1)}, u32[]{:S(2)}, u32[]{:S(2)}) %all-to-all-start.3) | async-done | bytes 1376288 | tf_op jit(solution)/shard_map/all_to_all | solution.py:393
  142.7 5.4 %all-to-all-start.4 = ((bf16[8,96,896]{2,1,0:T(8,128)(2,1)}), bf16[8,96,896]{2,1,0:T(8,128)(2,1)S(1)}, u32[]{:S(2)}, u32[]{:S(2)}) async-start(bf16[8,96,896]{2,1,0:T(8,128)(2,1)} %bitcast.21), calls=%async_computation.4 | async-start | bytes 2752512 | tf_op jit(solution)/shard_map/all_to_all | solution.py:400
  149.2 5.0 %hidden_step.1 = (bf16[192,1024]{1,0:T(8,128)(2,1)}, f32[192,1]{1,0:T(8,128)}) custom-call(bf16[4,192,896]{2,1,0:T(8,128)(2,1)S(1)} %bitcast.51, bf16[4,3584,256]{2,1,0:T(8,128)(2,1)} %bitcast_dynamic-update-slice_fusion.3.matrix_ref, f32[4,192,256]{2,1,0:T(8,128)S(1)} %copy-done, f32[4,192,256]{2,1,0:T(8,128)S(1)} %get-tuple-element.27.dw_act_ref), custom_call_target="tpu_custom_call" | custom-call | tf_op jit(solution)/shard_map/hidden_step/pallas_call | solution.py:184
  158.3 9.9 %collective-permute-done.4.west_ref.west_hbm = bf16[192,1024]{1,0:T(8,128)(2,1)S(1)} collective-permute-done((bf16[192,1024]{1,0:T(8,128)(2,1)}, bf16[192,1024]{1,0:T(8,128)(2,1)S(1)}, u32[]{:S(2)}, u32[]{:S(2)}) %collective-permute-start.4) | collective-permute-done | bytes 393248 | tf_op jit(solution)/shard_map/ppermute | solution.py:63
  174.4 4.7 %collective-permute-start.8 = (bf16[128,2048]{1,0:T(8,128)(2,1)S(1)}, bf16[128,2048]{1,0:T(8,128)(2,1)}, u32[]{:S(2)}, u32[]{:S(2)}) collective-permute-start(bf16[128,2048]{1,0:T(8,128)(2,1)S(1)} %get-tuple-element.35), channel_id=1, source_target_pairs={{0,3},{1,2},{2,1},{3,0},{4,7},{5,6},{6,5},{7,4},{8,11},{9,10},{10,... | collective-permute-start | bytes 1572872 | tf_op jit(solution)/shard_map/ppermute | solution.py:63
  180.4 8.6 %all-to-all-start.5 = ((f32[16,8,128]{2,1,0:T(8,128)}), f32[16,8,128]{2,1,0:T(8,128)S(1)}, u32[]{:S(2)}, u32[]{:S(2)}) async-start(f32[16,8,128]{2,1,0:T(8,128)} %pad_dynamic-update-slice_fusion), calls=%async_computation.5 | async-start | bytes 131072 | tf_op jit(solution)/shard_map/all_to_all | solution.py:417
  194.5 6.1 %all-to-all-done.5 = f32[16,8,128]{2,1,0:T(8,128)S(1)} async-done(((f32[16,8,128]{2,1,0:T(8,128)}), f32[16,8,128]{2,1,0:T(8,128)S(1)}, u32[]{:S(2)}, u32[]{:S(2)}) %all-to-all-start.5) | async-done | bytes 65568 | tf_op jit(solution)/shard_map/all_to_all | solution.py:417
  201.3 8.2 %all-to-all-start.6 = ((f32[32,1,96]{2,1,0:T(1,128)}), f32[32,1,96]{2,1,0:T(1,128)S(1)}, u32[]{:S(2)}, u32[]{:S(2)}) async-start(f32[32,1,96]{2,1,0:T(1,128)} %bitcast.25), calls=%async_computation.6 | async-start | bytes 32768 | tf_op jit(solution)/shard_map/all_to_all | solution.py:420
  210.3 10.7 %last_step.1 = bf16[1,896,1024]{2,1,0:T(8,128)(2,1)} custom-call(s32[1]{0:T(128)} %bitcast.27.rank_ref, bf16[896,768]{1,0:T(8,128)(2,1)} %get-tuple-element.33.rows_t_hbm, bf16[192,1024]{1,0:T(8,128)(2,1)} %get-tuple-element.30.own_hbm, bf16[128,1408]{1,0:T(8,128)(2,1)} %copy-done.4, bf16[128,1408]{1,0:T(8,128)(2,1)} %copy-done.6, ...), custom_call_target="tpu_custom_call" | custom-call | tf_op jit(solution)/shard_map/last_step/pallas_call | solution.py:302
  (100 shorter events, 50.1 us)
Async XLA Ops:
  7.2 30.9 %copy-start.11 = (bf16[1,768,256]{2,1,0:T(8,128)(2,1)S(1)}, bf16[1,768,256]{2,1,0:T(8,128)(2,1)}, u32[]{:S(2)}) copy-start(bf16[1,768,256]{2,1,0:T(8,128)(2,1)} %param.12) | copy-start | bytes 1179652
  7.2 30.9 %copy-start.10 = (bf16[1,768,256]{2,1,0:T(8,128)(2,1)S(1)}, bf16[1,768,256]{2,1,0:T(8,128)(2,1)}, u32[]{:S(2)}) copy-start(bf16[1,768,256]{2,1,0:T(8,128)(2,1)} %param.13) | copy-start | bytes 1179652
  7.2 104.4 %all-gather.2.cloned.1.call-start = ((), (), s32[]{:S(2)}) async-start(), calls=%async_computation.7 | async-start | bytes 7798784 | tf_op jit(solution)/shard_map/all_gather | solution.py:338
  13.0 50.3 %collective-permute-start = (bf16[3584,256]{1,0:T(8,128)(2,1)}, bf16[3584,256]{1,0:T(8,128)(2,1)}, u32[]{:S(2)}, u32[]{:S(2)}) collective-permute-start(bf16[3584,256]{1,0:T(8,128)(2,1)} %bitcast.4), channel_id=1, source_target_pairs={{0,1},{1,2},{2,3},{3,0},{4,5},{5,6},{6,7},{7,4},{8,9},{9,10},{10,1... | collective-permute-start | bytes 5505032 | tf_op jit(solution)/shard_map/ppermute | solution.py:37
  17.0 46.3 %collective-permute-start.1 = (bf16[3584,256]{1,0:T(8,128)(2,1)}, bf16[3584,256]{1,0:T(8,128)(2,1)}, u32[]{:S(2)}, u32[]{:S(2)}) collective-permute-start(bf16[3584,256]{1,0:T(8,128)(2,1)} %bitcast.4), channel_id=1, source_target_pairs={{0,3},{1,0},{2,1},{3,2},{4,7},{5,4},{6,5},{7,6},{8,11},{9,8},{10,9... | collective-permute-start | bytes 5505032 | tf_op jit(solution)/shard_map/ppermute | solution.py:37
  23.1 26.3 %all-to-all-start = ((f32[16,2,48]{2,1,0:T(2,128)}), f32[16,2,48]{2,1,0:T(2,128)S(1)}, u32[]{:S(2)}, u32[]{:S(2)}) async-start(f32[16,2,48]{2,1,0:T(2,128)} %copy.52), calls=%async_computation | async-start | bytes 32768 | tf_op jit(solution)/shard_map/all_to_all | solution.py:354
  50.4 11.6 %all-to-all-start.2 = ((f32[8,1,24]{2,1,0:T(1,128)}), f32[8,1,24]{2,1,0:T(1,128)S(1)}, u32[]{:S(2)}, u32[]{:S(2)}) async-start(f32[8,1,24]{2,1,0:T(1,128)} %bitcast.16), calls=%async_computation.2 | async-start | bytes 8192 | tf_op jit(solution)/shard_map/all_to_all | solution.py:364
  65.5 34.2 %collective-permute-start.2 = (bf16[1792,256]{1,0:T(8,128)(2,1)}, bf16[1792,256]{1,0:T(8,128)(2,1)}, u32[]{:S(2)}, u32[]{:S(2)}) collective-permute-start(bf16[1792,256]{1,0:T(8,128)(2,1)} %slice.35), channel_id=1, source_target_pairs={{0,1},{1,2},{2,3},{3,0},{4,5},{5,6},{6,7},{7,4},{8,9},{9,10},{10,1... | collective-permute-start | bytes 2752520 | tf_op jit(solution)/shard_map/ppermute | solution.py:37
  68.7 33.1 %collective-permute-start.3 = (bf16[1792,256]{1,0:T(8,128)(2,1)S(1)}, bf16[1792,256]{1,0:T(8,128)(2,1)}, u32[]{:S(2)}, u32[]{:S(2)}) collective-permute-start(bf16[1792,256]{1,0:T(8,128)(2,1)S(1)} %slice.36), channel_id=1, source_target_pairs={{0,3},{1,0},{2,1},{3,2},{4,7},{5,4},{6,5},{7,6},{8,11},{9,8},{10,9... | collective-permute-start | bytes 2752520 | tf_op jit(solution)/shard_map/ppermute | solution.py:37
  73.2 25.3 %all-to-all-start.1 = ((bf16[4,192,512]{2,1,0:T(8,128)(2,1)}), bf16[4,192,512]{2,1,0:T(8,128)(2,1)S(1)}, u32[]{:S(2)}, u32[]{:S(2)}) async-start(bf16[4,192,512]{2,1,0:T(8,128)(2,1)} %bitcast.13), calls=%async_computation.1 | async-start | bytes 1572864 | tf_op jit(solution)/shard_map/all_to_all | solution.py:380
  115.2 27.4 %all-to-all-start.3 = ((bf16[32,24,896]{2,1,0:T(8,128)(2,1)}), bf16[32,24,896]{2,1,0:T(8,128)(2,1)S(1)}, u32[]{:S(2)}, u32[]{:S(2)}) async-start(bf16[32,24,896]{2,1,0:T(8,128)(2,1)} %bitcast.18), calls=%async_computation.3 | async-start | bytes 2752512 | tf_op jit(solution)/shard_map/all_to_all | solution.py:393
  142.7 26.0 %all-to-all-start.4 = ((bf16[8,96,896]{2,1,0:T(8,128)(2,1)}), bf16[8,96,896]{2,1,0:T(8,128)(2,1)S(1)}, u32[]{:S(2)}, u32[]{:S(2)}) async-start(bf16[8,96,896]{2,1,0:T(8,128)(2,1)} %bitcast.21), calls=%async_computation.4 | async-start | bytes 2752512 | tf_op jit(solution)/shard_map/all_to_all | solution.py:400
  154.3 14.0 %collective-permute-start.4 = (bf16[192,1024]{1,0:T(8,128)(2,1)}, bf16[192,1024]{1,0:T(8,128)(2,1)S(1)}, u32[]{:S(2)}, u32[]{:S(2)}) collective-permute-start(bf16[192,1024]{1,0:T(8,128)(2,1)} %get-tuple-element.30.own_hbm), channel_id=1, source_target_pairs={{0,3},{1,2},{2,1},{3,0},{4,7},{5,6},{6,5},{7,4},{8,11},{9,10},{10,... | collective-permute-start | bytes 1179656 | tf_op jit(solution)/shard_map/ppermute | solution.py:63
  156.2 12.5 %collective-permute-start.5 = (bf16[192,1024]{1,0:T(8,128)(2,1)}, bf16[192,1024]{1,0:T(8,128)(2,1)S(1)}, u32[]{:S(2)}, u32[]{:S(2)}) collective-permute-start(bf16[192,1024]{1,0:T(8,128)(2,1)} %get-tuple-element.30.own_hbm), channel_id=1, source_target_pairs={{0,1},{1,0},{2,3},{3,2},{4,5},{5,4},{6,7},{7,6},{8,9},{9,8},{10,11... | collective-permute-start | bytes 1179656 | tf_op jit(solution)/shard_map/ppermute | solution.py:63
  168.2 41.2 %copy-start.1 = (bf16[192,1024]{1,0:T(8,128)(2,1)}, bf16[192,1024]{1,0:T(8,128)(2,1)S(1)}, u32[]{:S(2)}) copy-start(bf16[192,1024]{1,0:T(8,128)(2,1)S(1)} %collective-permute-done.4.west_ref.west_hbm) | copy-start | bytes 1179652
  168.7 40.8 %copy-start.2 = (bf16[192,1024]{1,0:T(8,128)(2,1)}, bf16[192,1024]{1,0:T(8,128)(2,1)S(1)}, u32[]{:S(2)}) copy-start(bf16[192,1024]{1,0:T(8,128)(2,1)S(1)} %collective-permute-done.5.east_ref.east_hbm) | copy-start | bytes 1179652
  171.3 17.7 %collective-permute-start.6 = (bf16[128,2176]{1,0:T(8,128)(2,1)S(1)}, bf16[128,2176]{1,0:T(8,128)(2,1)S(1)}, u32[]{:S(2)}, u32[]{:S(2)}) collective-permute-start(bf16[128,2176]{1,0:T(8,128)(2,1)S(1)} %get-tuple-element.34), channel_id=1, source_target_pairs={{0,1},{1,0},{2,3},{3,2},{4,5},{5,4},{6,7},{7,6},{8,9},{9,8},{10,11... | collective-permute-start | bytes 1671176 | tf_op jit(solution)/shard_map/ppermute | solution.py:63
  174.4 16.6 %collective-permute-start.8 = (bf16[128,2048]{1,0:T(8,128)(2,1)S(1)}, bf16[128,2048]{1,0:T(8,128)(2,1)}, u32[]{:S(2)}, u32[]{:S(2)}) collective-permute-start(bf16[128,2048]{1,0:T(8,128)(2,1)S(1)} %get-tuple-element.35), channel_id=1, source_target_pairs={{0,3},{1,2},{2,1},{3,0},{4,7},{5,6},{6,5},{7,4},{8,11},{9,10},{10,... | collective-permute-start | bytes 1572872 | tf_op jit(solution)/shard_map/ppermute | solution.py:63
  180.4 20.2 %all-to-all-start.5 = ((f32[16,8,128]{2,1,0:T(8,128)}), f32[16,8,128]{2,1,0:T(8,128)S(1)}, u32[]{:S(2)}, u32[]{:S(2)}) async-start(f32[16,8,128]{2,1,0:T(8,128)} %pad_dynamic-update-slice_fusion), calls=%async_computation.5 | async-start | bytes 131072 | tf_op jit(solution)/shard_map/all_to_all | solution.py:417
  189.0 20.5 %copy-start.3 = (bf16[128,2176]{1,0:T(8,128)(2,1)}, bf16[128,2176]{1,0:T(8,128)(2,1)S(1)}, u32[]{:S(2)}) copy-start(bf16[128,2176]{1,0:T(8,128)(2,1)S(1)} %collective-permute-done.6.far_low) | copy-start | bytes 1671172
  189.1 20.4 %copy-start.4 = (bf16[128,1408]{1,0:T(8,128)(2,1)}, bf16[128,1408]{1,0:T(8,128)(2,1)S(1)}, u32[]{:S(2)}) copy-start(bf16[128,1408]{1,0:T(8,128)(2,1)S(1)} %slice_add_fusion.low_a) | copy-start | bytes 1081348
  189.1 20.4 %collective-permute-start.7 = (bf16[128,1408]{1,0:T(8,128)(2,1)S(1)}, bf16[128,1408]{1,0:T(8,128)(2,1)S(1)}, u32[]{:S(2)}, u32[]{:S(2)}) collective-permute-start(bf16[128,1408]{1,0:T(8,128)(2,1)S(1)} %slice_add_fusion.low_a), channel_id=1, source_target_pairs={{0,3},{1,2},{2,1},{3,0},{4,7},{5,6},{6,5},{7,4},{8,11},{9,10},{10,... | collective-permute-start | bytes 1081352 | tf_op jit(solution)/shard_map/ppermute | solution.py:63
  192.0 17.4 %collective-permute-start.9 = (bf16[128,1280]{1,0:T(8,128)(2,1)S(1)}, bf16[128,1280]{1,0:T(8,128)(2,1)S(1)}, u32[]{:S(2)}, u32[]{:S(2)}) collective-permute-start(bf16[128,1280]{1,0:T(8,128)(2,1)S(1)} %slice_add_fusion.1.high_a), channel_id=1, source_target_pairs={{0,1},{1,0},{2,3},{3,2},{4,5},{5,4},{6,7},{7,6},{8,9},{9,8},{10,11... | collective-permute-start | bytes 983048 | tf_op jit(solution)/shard_map/ppermute | solution.py:63
  201.3 19.7 %all-to-all-start.6 = ((f32[32,1,96]{2,1,0:T(1,128)}), f32[32,1,96]{2,1,0:T(1,128)S(1)}, u32[]{:S(2)}, u32[]{:S(2)}) async-start(f32[32,1,96]{2,1,0:T(1,128)} %bitcast.25), calls=%async_computation.6 | async-start | bytes 32768 | tf_op jit(solution)/shard_map/all_to_all | solution.py:420
  (6 other events, 46.8 us)
Sparse Core Ops, SparseCore 0:
  10.1 101.4 all-gather.1

commit v8 on v7

--- a/solution.py
+++ b/solution.py
@@ -193,7 +193,7 @@
         out_specs=[pl.BlockSpec(out.shape, lambda k: (0, 0)) for out in outs],
         out_shape=outs,
         scratch_shapes=[pltpu.VMEM((rows, blocks * width), f32)],
-        compiler_params=pltpu.CompilerParams(vmem_limit_bytes=46 * MIB),
+        compiler_params=pltpu.CompilerParams(vmem_limit_bytes=53 * MIB),
         name="hidden_step",
     )(grads, matrix, out_act, dw_act)
 
@@ -396,10 +396,16 @@
     token_send, grads = lax.optimization_barrier((token_send, grads))
     up_own, slot_dw = hidden_step(grads, matrix, out_act, dw_act)
     west, east = swap(up_own, across), swap(up_own, beside)
+    back = slot_dw.reshape(near, zl, CAP).transpose(1, 0, 2)
+    back = jnp.pad(back, ((0, 0), (0, 0), (0, 128 - CAP)))
+    back = lax.dynamic_update_slice(
+        jnp.zeros((nz, near, 128), f32), back, (lax.axis_index("y") * zl, 0, 0)
+    )
 
     rows = lax.all_to_all(
         token_send.reshape(near, nz * CAP, feats), ("x", "c"), 0, 0, tiled=True
     ).reshape(near, ny, zl * CAP, feats)
+    west, east, back = lax.optimization_barrier((west, east, back))
     rows_t, low, high = inner_products(rows, west, east)
     low_near, high_near = swap(low, beside), swap(high, across)
     low_size, high_size = (triangle(i)[1] * (slots // 6) for i in range(2))
@@ -408,11 +414,6 @@
     packs = (low, swap(low, across), high, swap(high, beside))
     ups = (west, east, low_near, high_near)
 
-    back = slot_dw.reshape(near, zl, CAP).transpose(1, 0, 2)
-    back = jnp.pad(back, ((0, 0), (0, 0), (0, 128 - CAP)))
-    back = lax.dynamic_update_slice(
-        jnp.zeros((nz, near, 128), f32), back, (lax.axis_index("y") * zl, 0, 0)
-    )
     back, rows_t = lax.optimization_barrier((back, rows_t))
     back = lax.all_to_all(back, "z", 0, 0, tiled=True)[:, :, :CAP]
     back = back.transpose(1, 0, 2).reshape(1, near, nz * CAP)

time: 231 us -> 228 us (0.987)
  local copies, waits for them, and re-layouts: 32.2 us -> 28.7 us
    ppermute x6, waiting for transfers between devices: 10.4 us -> 7.97 us  [swap(): return lax.ppermute(values, 'y', [(i, partner(i)) for i in range(size)])]
  transfers between devices with their start and end apart: 18 -> 18, of which waited for: 8 -> 8; matrix products, arithmetic and copies ran while one was open for 15% -> 15% of each run, Pallas kernels for 8% -> 9%
where the time goes in v8:
time: 228 us; the launch traced here: 227 us
  starting transfers between devices  85.7 us (38%)
  waiting for transfers between devices  62.1 us (27%)
  local copies, waits for them, and re-layouts  28.7 us (13%)
  Pallas kernels  26.3 us (12%)
  between operations  14.5 us (6%)
  other arithmetic  7.96 us (3%)
    ppermute x6, starting transfers between devices, swap(): return lax.ppermute(values, 'y', [(i, partner(i)) for i in range(size)])  16.7 us
    all_to_all x1, waiting for transfers between devices, on_device(): lax.all_to_all(grad_send.reshape(ny * near, zl * CAP, feats), ('y', 'x',...  16.2 us
    all_to_all x1, waiting for transfers between devices, on_device(): lax.all_to_all(saved.reshape(ny, own_slots, 2 * hidden_part), 'y', 0, 0,...  16.2 us
    all_to_all x1, starting transfers between devices, on_device(): lax.all_to_all(jnp.stack([index_send.reshape(nz, near * CAP), weight_send...  14.9 us
    ppermute x4, starting transfers between devices, shift(): lax.ppermute(values, 'y', [(i, (i + step) % size) for i in range(size)])  13.9 us
    dynamic_update_slice x5, local copies, waits for them, and re-layouts, gather_weights(): whole = lax.dynamic_update_slice(whole, part[None], (place, row, 0))  11.5 us
    pallas_call x1, Pallas kernels, last_step(): pl.pallas_call(last_kernel, in_specs=[pl.BlockSpec(memory_space=pltpu.SME...  10.7 us
    all_to_all x1, starting transfers between devices, on_device(): back = lax.all_to_all(back, 'z', 0, 0, tiled=True)[:, :, :CAP]  8.6 us
  transfers between devices with their start and end apart: 18, of which 8 were waited for; matrix products, arithmetic and copies ran while one was open for 15% of the time, Pallas kernels for 9%

profile of v8, /device:TPU:1, one launch (start us, length us, event | category | flops | bytes accessed | tf_op | source)
XLA Modules:
  0.0 226.9 jit_solution(17675354555935062854)
XLA Ops:
  12.1 4.0 %collective-permute-start = (bf16[3584,256]{1,0:T(8,128)(2,1)S(1)}, bf16[3584,256]{1,0:T(8,128)(2,1)}, u32[]{:S(2)}, u32[]{:S(2)}) collective-permute-start(bf16[3584,256]{1,0:T(8,128)(2,1)S(1)} %bitcast.54), channel_id=1, source_target_pairs={{0,1},{1,2},{2,3},{3,0},{4,5},{5,6},{6,7},{7,4},{8,9},{9,10},{10,1... | collective-permute-start | bytes 5505032 | tf_op jit(solution)/shard_map/ppermute | solution.py:37
  16.1 3.4 %collective-permute-start.1 = (bf16[3584,256]{1,0:T(8,128)(2,1)S(1)}, bf16[3584,256]{1,0:T(8,128)(2,1)}, u32[]{:S(2)}, u32[]{:S(2)}) collective-permute-start(bf16[3584,256]{1,0:T(8,128)(2,1)S(1)} %bitcast.55), channel_id=1, source_target_pairs={{0,3},{1,0},{2,1},{3,2},{4,7},{5,4},{6,5},{7,6},{8,11},{9,8},{10,9... | collective-permute-start | bytes 5505032 | tf_op jit(solution)/shard_map/ppermute | solution.py:37
  22.2 14.9 %all-to-all-start = ((f32[16,2,48]{2,1,0:T(2,128)}), f32[16,2,48]{2,1,0:T(2,128)S(1)}, u32[]{:S(2)}, u32[]{:S(2)}) async-start(f32[16,2,48]{2,1,0:T(2,128)} %copy.52), calls=%async_computation | async-start | bytes 32768 | tf_op jit(solution)/shard_map/all_to_all | solution.py:354
  38.9 3.5 %broadcast_in_dim.80 = bf16[4,3584,256]{2,1,0:T(8,128)(2,1)} broadcast(bf16[]{:T(256)} %constant.173.clone.1), dimensions={} | broadcast | bytes 7340034 | tf_op jit(solution)/shard_map/broadcast_in_dim | solution.py:49
  43.8 4.8 %all-to-all-done = f32[16,2,48]{2,1,0:T(2,128)S(1)} async-done(((f32[16,2,48]{2,1,0:T(2,128)}), f32[16,2,48]{2,1,0:T(2,128)S(1)}, u32[]{:S(2)}, u32[]{:S(2)}) %all-to-all-start) | async-done | bytes 6176 | tf_op jit(solution)/shard_map/all_to_all | solution.py:354
  49.7 6.9 %all-to-all-start.2 = ((f32[8,1,24]{2,1,0:T(1,128)}), f32[8,1,24]{2,1,0:T(1,128)S(1)}, u32[]{:S(2)}, u32[]{:S(2)}) async-start(f32[8,1,24]{2,1,0:T(1,128)} %bitcast.16), calls=%async_computation.2 | async-start | bytes 8192 | tf_op jit(solution)/shard_map/all_to_all | solution.py:364
  57.1 4.1 %all-to-all-done.2 = f32[8,1,24]{2,1,0:T(1,128)S(1)} async-done(((f32[8,1,24]{2,1,0:T(1,128)}), f32[8,1,24]{2,1,0:T(1,128)S(1)}, u32[]{:S(2)}, u32[]{:S(2)}) %all-to-all-start.2) | async-done | bytes 800 | tf_op jit(solution)/shard_map/all_to_all | solution.py:364
  67.8 4.5 %collective-permute-start.3 = (bf16[1792,256]{1,0:T(8,128)(2,1)S(1)}, bf16[1792,256]{1,0:T(8,128)(2,1)}, u32[]{:S(2)}, u32[]{:S(2)}) collective-permute-start(bf16[1792,256]{1,0:T(8,128)(2,1)S(1)} %slice.36), channel_id=1, source_target_pairs={{0,3},{1,0},{2,1},{3,2},{4,7},{5,4},{6,5},{7,6},{8,11},{9,8},{10,9... | collective-permute-start | bytes 2752520 | tf_op jit(solution)/shard_map/ppermute | solution.py:37
  72.3 3.5 %all-to-all-start.1 = ((bf16[4,192,512]{2,1,0:T(8,128)(2,1)}), bf16[4,192,512]{2,1,0:T(8,128)(2,1)S(1)}, u32[]{:S(2)}, u32[]{:S(2)}) async-start(bf16[4,192,512]{2,1,0:T(8,128)(2,1)} %bitcast.57), calls=%async_computation.1 | async-start | bytes 1572864 | tf_op jit(solution)/shard_map/all_to_all | solution.py:380
  81.6 16.2 %all-to-all-done.1 = bf16[4,192,512]{2,1,0:T(8,128)(2,1)S(1)} async-done(((bf16[4,192,512]{2,1,0:T(8,128)(2,1)}), bf16[4,192,512]{2,1,0:T(8,128)(2,1)S(1)}, u32[]{:S(2)}, u32[]{:S(2)}) %all-to-all-start.1) | async-done | bytes 786464 | tf_op jit(solution)/shard_map/all_to_all | solution.py:380
  103.3 8.3 %all-gather.2.cloned.1.call-done = bf16[2048,1792]{1,0:T(8,128)(2,1)} async-done(((bf16[128,1792]{1,0:T(8,128)(2,1)}), bf16[2048,1792]{1,0:T(8,128)(2,1)}) %all-gather.2.cloned.1.call-update) | async-done | bytes 7340048 | tf_op jit(solution)/shard_map/all_gather | solution.py:338
  111.6 3.7 %pick_grads.1 = bf16[4,8,24,896]{3,2,1,0:T(8,128)(2,1)} custom-call(f32[4,192,1]{2,1,0:T(8,128)S(1)} %reshape.290.index_ref, bf16[4,512,1792]{2,1,0:T(8,128)(2,1)} %bitcast.52), custom_call_target="tpu_custom_call" | custom-call | tf_op jit(solution)/shard_map/pick_grads/pallas_call | solution.py:91
  115.2 7.5 %all-to-all-start.3 = ((bf16[32,24,896]{2,1,0:T(8,128)(2,1)}), bf16[32,24,896]{2,1,0:T(8,128)(2,1)S(1)}, u32[]{:S(2)}, u32[]{:S(2)}) async-start(bf16[32,24,896]{2,1,0:T(8,128)(2,1)} %bitcast.18), calls=%async_computation.3 | async-start | bytes 2752512 | tf_op jit(solution)/shard_map/all_to_all | solution.py:393
  122.8 3.7 %pick_tokens.1 = bf16[8,4,24,896]{3,2,1,0:T(8,128)(2,1)} custom-call(f32[4,192,1]{2,1,0:T(8,128)S(1)} %reshape.290.index_ref, bf16[4,512,1792]{2,1,0:T(8,128)(2,1)} %bitcast.53), custom_call_target="tpu_custom_call" | custom-call | tf_op jit(solution)/shard_map/pick_tokens/pallas_call | solution.py:91
  126.4 16.2 %all-to-all-done.3 = bf16[32,24,896]{2,1,0:T(8,128)(2,1)S(1)} async-done(((bf16[32,24,896]{2,1,0:T(8,128)(2,1)}), bf16[32,24,896]{2,1,0:T(8,128)(2,1)S(1)}, u32[]{:S(2)}, u32[]{:S(2)}) %all-to-all-start.3) | async-done | bytes 1376288 | tf_op jit(solution)/shard_map/all_to_all | solution.py:393
  142.7 5.4 %all-to-all-start.4 = ((bf16[8,96,896]{2,1,0:T(8,128)(2,1)}), bf16[8,96,896]{2,1,0:T(8,128)(2,1)S(1)}, u32[]{:S(2)}, u32[]{:S(2)}) async-start(bf16[8,96,896]{2,1,0:T(8,128)(2,1)} %bitcast.21), calls=%async_computation.4 | async-start | bytes 2752512 | tf_op jit(solution)/shard_map/all_to_all | solution.py:405
  148.1 5.7 %hidden_step.1 = (bf16[192,1024]{1,0:T(8,128)(2,1)}, f32[192,1]{1,0:T(8,128)}) custom-call(bf16[4,192,896]{2,1,0:T(8,128)(2,1)} %bitcast.56, bf16[4,3584,256]{2,1,0:T(8,128)(2,1)} %bitcast_dynamic-update-slice_fusion.3.matrix_ref, f32[4,192,256]{2,1,0:T(8,128)S(1)} %get-tuple-element.29.out_act_ref, f32[4,192,256]{2,1,0:T(8,128)} %get-tuple-element.30.dw_act_ref), custom_call_target="tpu_custom_call" | custom-call | tf_op jit(solution)/shard_map/hidden_step/pallas_call | solution.py:184
  160.2 7.4 %collective-permute-done.4.west_ref.west_hbm = bf16[192,1024]{1,0:T(8,128)(2,1)S(1)} collective-permute-done((bf16[192,1024]{1,0:T(8,128)(2,1)}, bf16[192,1024]{1,0:T(8,128)(2,1)S(1)}, u32[]{:S(2)}, u32[]{:S(2)}) %collective-permute-start.4) | collective-permute-done | bytes 393248 | tf_op jit(solution)/shard_map/ppermute | solution.py:63
  172.9 4.6 %collective-permute-start.8 = (bf16[128,2048]{1,0:T(8,128)(2,1)S(1)}, bf16[128,2048]{1,0:T(8,128)(2,1)}, u32[]{:S(2)}, u32[]{:S(2)}) collective-permute-start(bf16[128,2048]{1,0:T(8,128)(2,1)S(1)} %get-tuple-element.41), channel_id=1, source_target_pairs={{0,3},{1,2},{2,1},{3,0},{4,7},{5,6},{6,5},{7,4},{8,11},{9,10},{10,... | collective-permute-start | bytes 1572872 | tf_op jit(solution)/shard_map/ppermute | solution.py:63
  177.4 8.6 %all-to-all-start.5 = ((f32[16,8,128]{2,1,0:T(8,128)}), f32[16,8,128]{2,1,0:T(8,128)S(1)}, u32[]{:S(2)}, u32[]{:S(2)}) async-start(f32[16,8,128]{2,1,0:T(8,128)} %pad_dynamic-update-slice_fusion), calls=%async_computation.5 | async-start | bytes 131072 | tf_op jit(solution)/shard_map/all_to_all | solution.py:418
  186.1 4.0 %collective-permute-start.7 = (bf16[128,1408]{1,0:T(8,128)(2,1)S(1)}, bf16[128,1408]{1,0:T(8,128)(2,1)S(1)}, u32[]{:S(2)}, u32[]{:S(2)}) collective-permute-start(bf16[128,1408]{1,0:T(8,128)(2,1)S(1)} %slice_add_fusion.low_a), channel_id=1, source_target_pairs={{0,3},{1,2},{2,1},{3,0},{4,7},{5,6},{6,5},{7,4},{8,11},{9,10},{10,... | collective-permute-start | bytes 1081352 | tf_op jit(solution)/shard_map/ppermute | solution.py:63
  193.1 4.5 %all-to-all-done.5 = f32[16,8,128]{2,1,0:T(8,128)S(1)} async-done(((f32[16,8,128]{2,1,0:T(8,128)}), f32[16,8,128]{2,1,0:T(8,128)S(1)}, u32[]{:S(2)}, u32[]{:S(2)}) %all-to-all-start.5) | async-done | bytes 65568 | tf_op jit(solution)/shard_map/all_to_all | solution.py:418
  198.4 8.3 %all-to-all-start.6 = ((f32[32,1,96]{2,1,0:T(1,128)}), f32[32,1,96]{2,1,0:T(1,128)S(1)}, u32[]{:S(2)}, u32[]{:S(2)}) async-start(f32[32,1,96]{2,1,0:T(1,128)} %bitcast.25), calls=%async_computation.6 | async-start | bytes 32768 | tf_op jit(solution)/shard_map/all_to_all | solution.py:421
  207.5 10.7 %last_step.1 = bf16[1,896,1024]{2,1,0:T(8,128)(2,1)} custom-call(s32[1]{0:T(128)} %bitcast.27.rank_ref, bf16[896,768]{1,0:T(8,128)(2,1)} %get-tuple-element.39.rows_t_hbm, bf16[192,1024]{1,0:T(8,128)(2,1)} %get-tuple-element.31.own_hbm, bf16[128,1408]{1,0:T(8,128)(2,1)} %copy-done.4, bf16[128,1408]{1,0:T(8,128)(2,1)} %copy-done.6, ...), custom_call_target="tpu_custom_call" | custom-call | tf_op jit(solution)/shard_map/last_step/pallas_call | solution.py:302
  (100 shorter events, 48.1 us)
Async XLA Ops:
  7.2 30.0 %copy-start.11 = (bf16[1,768,256]{2,1,0:T(8,128)(2,1)S(1)}, bf16[1,768,256]{2,1,0:T(8,128)(2,1)}, u32[]{:S(2)}) copy-start(bf16[1,768,256]{2,1,0:T(8,128)(2,1)} %param.12) | copy-start | bytes 1179652
  7.2 30.0 %copy-start.10 = (bf16[1,768,256]{2,1,0:T(8,128)(2,1)S(1)}, bf16[1,768,256]{2,1,0:T(8,128)(2,1)}, u32[]{:S(2)}) copy-start(bf16[1,768,256]{2,1,0:T(8,128)(2,1)} %param.13) | copy-start | bytes 1179652
  7.2 104.4 %all-gather.2.cloned.1.call-start = ((), (), s32[]{:S(2)}) async-start(), calls=%async_computation.7 | async-start | bytes 7798784 | tf_op jit(solution)/shard_map/all_gather | solution.py:338
  12.1 50.3 %collective-permute-start = (bf16[3584,256]{1,0:T(8,128)(2,1)S(1)}, bf16[3584,256]{1,0:T(8,128)(2,1)}, u32[]{:S(2)}, u32[]{:S(2)}) collective-permute-start(bf16[3584,256]{1,0:T(8,128)(2,1)S(1)} %bitcast.54), channel_id=1, source_target_pairs={{0,1},{1,2},{2,3},{3,0},{4,5},{5,6},{6,7},{7,4},{8,9},{9,10},{10,1... | collective-permute-start | bytes 5505032 | tf_op jit(solution)/shard_map/ppermute | solution.py:37
  16.1 46.3 %collective-permute-start.1 = (bf16[3584,256]{1,0:T(8,128)(2,1)S(1)}, bf16[3584,256]{1,0:T(8,128)(2,1)}, u32[]{:S(2)}, u32[]{:S(2)}) collective-permute-start(bf16[3584,256]{1,0:T(8,128)(2,1)S(1)} %bitcast.55), channel_id=1, source_target_pairs={{0,3},{1,0},{2,1},{3,2},{4,7},{5,4},{6,5},{7,6},{8,11},{9,8},{10,9... | collective-permute-start | bytes 5505032 | tf_op jit(solution)/shard_map/ppermute | solution.py:37
  22.2 26.4 %all-to-all-start = ((f32[16,2,48]{2,1,0:T(2,128)}), f32[16,2,48]{2,1,0:T(2,128)S(1)}, u32[]{:S(2)}, u32[]{:S(2)}) async-start(f32[16,2,48]{2,1,0:T(2,128)} %copy.52), calls=%async_computation | async-start | bytes 32768 | tf_op jit(solution)/shard_map/all_to_all | solution.py:354
  49.7 11.5 %all-to-all-start.2 = ((f32[8,1,24]{2,1,0:T(1,128)}), f32[8,1,24]{2,1,0:T(1,128)S(1)}, u32[]{:S(2)}, u32[]{:S(2)}) async-start(f32[8,1,24]{2,1,0:T(1,128)} %bitcast.16), calls=%async_computation.2 | async-start | bytes 8192 | tf_op jit(solution)/shard_map/all_to_all | solution.py:364
  64.6 34.3 %collective-permute-start.2 = (bf16[1792,256]{1,0:T(8,128)(2,1)}, bf16[1792,256]{1,0:T(8,128)(2,1)}, u32[]{:S(2)}, u32[]{:S(2)}) collective-permute-start(bf16[1792,256]{1,0:T(8,128)(2,1)} %slice.35), channel_id=1, source_target_pairs={{0,1},{1,2},{2,3},{3,0},{4,5},{5,6},{6,7},{7,4},{8,9},{9,10},{10,1... | collective-permute-start | bytes 2752520 | tf_op jit(solution)/shard_map/ppermute | solution.py:37
  67.8 33.3 %collective-permute-start.3 = (bf16[1792,256]{1,0:T(8,128)(2,1)S(1)}, bf16[1792,256]{1,0:T(8,128)(2,1)}, u32[]{:S(2)}, u32[]{:S(2)}) collective-permute-start(bf16[1792,256]{1,0:T(8,128)(2,1)S(1)} %slice.36), channel_id=1, source_target_pairs={{0,3},{1,0},{2,1},{3,2},{4,7},{5,4},{6,5},{7,6},{8,11},{9,8},{10,9... | collective-permute-start | bytes 2752520 | tf_op jit(solution)/shard_map/ppermute | solution.py:37
  72.3 25.4 %all-to-all-start.1 = ((bf16[4,192,512]{2,1,0:T(8,128)(2,1)}), bf16[4,192,512]{2,1,0:T(8,128)(2,1)S(1)}, u32[]{:S(2)}, u32[]{:S(2)}) async-start(bf16[4,192,512]{2,1,0:T(8,128)(2,1)} %bitcast.57), calls=%async_computation.1 | async-start | bytes 1572864 | tf_op jit(solution)/shard_map/all_to_all | solution.py:380
  115.2 27.4 %all-to-all-start.3 = ((bf16[32,24,896]{2,1,0:T(8,128)(2,1)}), bf16[32,24,896]{2,1,0:T(8,128)(2,1)S(1)}, u32[]{:S(2)}, u32[]{:S(2)}) async-start(bf16[32,24,896]{2,1,0:T(8,128)(2,1)} %bitcast.18), calls=%async_computation.3 | async-start | bytes 2752512 | tf_op jit(solution)/shard_map/all_to_all | solution.py:393
  142.7 25.5 %all-to-all-start.4 = ((bf16[8,96,896]{2,1,0:T(8,128)(2,1)}), bf16[8,96,896]{2,1,0:T(8,128)(2,1)S(1)}, u32[]{:S(2)}, u32[]{:S(2)}) async-start(bf16[8,96,896]{2,1,0:T(8,128)(2,1)} %bitcast.21), calls=%async_computation.4 | async-start | bytes 2752512 | tf_op jit(solution)/shard_map/all_to_all | solution.py:405
  153.8 13.9 %collective-permute-start.4 = (bf16[192,1024]{1,0:T(8,128)(2,1)}, bf16[192,1024]{1,0:T(8,128)(2,1)S(1)}, u32[]{:S(2)}, u32[]{:S(2)}) collective-permute-start(bf16[192,1024]{1,0:T(8,128)(2,1)} %get-tuple-element.31.own_hbm), channel_id=1, source_target_pairs={{0,3},{1,2},{2,1},{3,0},{4,7},{5,6},{6,5},{7,4},{8,11},{9,10},{10,... | collective-permute-start | bytes 1179656 | tf_op jit(solution)/shard_map/ppermute | solution.py:63
  155.7 12.5 %collective-permute-start.5 = (bf16[192,1024]{1,0:T(8,128)(2,1)}, bf16[192,1024]{1,0:T(8,128)(2,1)S(1)}, u32[]{:S(2)}, u32[]{:S(2)}) collective-permute-start(bf16[192,1024]{1,0:T(8,128)(2,1)} %get-tuple-element.31.own_hbm), channel_id=1, source_target_pairs={{0,1},{1,0},{2,3},{3,2},{4,5},{5,4},{6,7},{7,6},{8,9},{9,8},{10,11... | collective-permute-start | bytes 1179656 | tf_op jit(solution)/shard_map/ppermute | solution.py:63
  167.7 39.0 %copy-start = (bf16[192,1024]{1,0:T(8,128)(2,1)}, bf16[192,1024]{1,0:T(8,128)(2,1)S(1)}, u32[]{:S(2)}) copy-start(bf16[192,1024]{1,0:T(8,128)(2,1)S(1)} %collective-permute-done.4.west_ref.west_hbm) | copy-start | bytes 1179652
  168.2 38.5 %copy-start.1 = (bf16[192,1024]{1,0:T(8,128)(2,1)}, bf16[192,1024]{1,0:T(8,128)(2,1)S(1)}, u32[]{:S(2)}) copy-start(bf16[192,1024]{1,0:T(8,128)(2,1)S(1)} %collective-permute-done.5.east_ref.east_hbm) | copy-start | bytes 1179652
  170.8 15.3 %collective-permute-start.6 = (bf16[128,2176]{1,0:T(8,128)(2,1)S(1)}, bf16[128,2176]{1,0:T(8,128)(2,1)S(1)}, u32[]{:S(2)}, u32[]{:S(2)}) collective-permute-start(bf16[128,2176]{1,0:T(8,128)(2,1)S(1)} %get-tuple-element.40), channel_id=1, source_target_pairs={{0,1},{1,0},{2,3},{3,2},{4,5},{5,4},{6,7},{7,6},{8,9},{9,8},{10,11... | collective-permute-start | bytes 1671176 | tf_op jit(solution)/shard_map/ppermute | solution.py:63
  172.9 17.2 %collective-permute-start.8 = (bf16[128,2048]{1,0:T(8,128)(2,1)S(1)}, bf16[128,2048]{1,0:T(8,128)(2,1)}, u32[]{:S(2)}, u32[]{:S(2)}) collective-permute-start(bf16[128,2048]{1,0:T(8,128)(2,1)S(1)} %get-tuple-element.41), channel_id=1, source_target_pairs={{0,3},{1,2},{2,1},{3,0},{4,7},{5,6},{6,5},{7,4},{8,11},{9,10},{10,... | collective-permute-start | bytes 1572872 | tf_op jit(solution)/shard_map/ppermute | solution.py:63
  177.4 20.2 %all-to-all-start.5 = ((f32[16,8,128]{2,1,0:T(8,128)}), f32[16,8,128]{2,1,0:T(8,128)S(1)}, u32[]{:S(2)}, u32[]{:S(2)}) async-start(f32[16,8,128]{2,1,0:T(8,128)} %pad_dynamic-update-slice_fusion), calls=%async_computation.5 | async-start | bytes 131072 | tf_op jit(solution)/shard_map/all_to_all | solution.py:418
  186.1 20.6 %copy-start.3 = (bf16[128,2176]{1,0:T(8,128)(2,1)}, bf16[128,2176]{1,0:T(8,128)(2,1)S(1)}, u32[]{:S(2)}) copy-start(bf16[128,2176]{1,0:T(8,128)(2,1)S(1)} %collective-permute-done.6.far_low) | copy-start | bytes 1671172
  186.1 20.6 %copy-start.4 = (bf16[128,1408]{1,0:T(8,128)(2,1)}, bf16[128,1408]{1,0:T(8,128)(2,1)S(1)}, u32[]{:S(2)}) copy-start(bf16[128,1408]{1,0:T(8,128)(2,1)S(1)} %slice_add_fusion.low_a) | copy-start | bytes 1081348
  186.1 20.5 %collective-permute-start.7 = (bf16[128,1408]{1,0:T(8,128)(2,1)S(1)}, bf16[128,1408]{1,0:T(8,128)(2,1)S(1)}, u32[]{:S(2)}, u32[]{:S(2)}) collective-permute-start(bf16[128,1408]{1,0:T(8,128)(2,1)S(1)} %slice_add_fusion.low_a), channel_id=1, source_target_pairs={{0,3},{1,2},{2,1},{3,0},{4,7},{5,6},{6,5},{7,4},{8,11},{9,10},{10,... | collective-permute-start | bytes 1081352 | tf_op jit(solution)/shard_map/ppermute | solution.py:63
  191.1 15.5 %collective-permute-start.9 = (bf16[128,1280]{1,0:T(8,128)(2,1)S(1)}, bf16[128,1280]{1,0:T(8,128)(2,1)S(1)}, u32[]{:S(2)}, u32[]{:S(2)}) collective-permute-start(bf16[128,1280]{1,0:T(8,128)(2,1)S(1)} %slice_add_fusion.1.high_a), channel_id=1, source_target_pairs={{0,1},{1,0},{2,3},{3,2},{4,5},{5,4},{6,7},{7,6},{8,9},{9,8},{10,11... | collective-permute-start | bytes 983048 | tf_op jit(solution)/shard_map/ppermute | solution.py:63
  198.4 19.8 %all-to-all-start.6 = ((f32[32,1,96]{2,1,0:T(1,128)}), f32[32,1,96]{2,1,0:T(1,128)S(1)}, u32[]{:S(2)}, u32[]{:S(2)}) async-start(f32[32,1,96]{2,1,0:T(1,128)} %bitcast.25), calls=%async_computation.6 | async-start | bytes 32768 | tf_op jit(solution)/shard_map/all_to_all | solution.py:421
  (6 other events, 47.4 us)
Sparse Core Ops, SparseCore 0:
  10.1 101.4 all-gather.1

commit v9 on v8

--- a/solution.py
+++ b/solution.py
@@ -318,7 +318,7 @@
             pltpu.SemaphoreType.DMA((14,)),
             pltpu.VMEM((hidden, slots), bf16),
         ],
-        compiler_params=pltpu.CompilerParams(vmem_limit_bytes=56 * MIB),
+        compiler_params=pltpu.CompilerParams(vmem_limit_bytes=46 * MIB),
         name="last_step",
     )(rank, rows_t, own, *packs, *ups)
 

time: 228 us -> 229 us (level)
    unnamed x28 -> x18, local copies, waits for them, and re-layouts: 4.48 us -> 5.02 us
where the time goes in v9:
time: 229 us; the launch traced here: 228 us
  starting transfers between devices  85.9 us (38%)
  waiting for transfers between devices  61 us (27%)
  local copies, waits for them, and re-layouts  29.2 us (13%)
  Pallas kernels  26.4 us (12%)
  between operations  14.4 us (6%)
  other arithmetic  8.95 us (4%)
    ppermute x6, starting transfers between devices, swap(): return lax.ppermute(values, 'y', [(i, partner(i)) for i in range(size)])  16.9 us
    all_to_all x1, waiting for transfers between devices, on_device(): lax.all_to_all(grad_send.reshape(ny * near, zl * CAP, feats), ('y', 'x',...  16.2 us
    all_to_all x1, waiting for transfers between devices, on_device(): lax.all_to_all(saved.reshape(ny, own_slots, 2 * hidden_part), 'y', 0, 0,...  16.1 us
    all_to_all x1, starting transfers between devices, on_device(): lax.all_to_all(jnp.stack([index_send.reshape(nz, near * CAP), weight_send...  14.9 us
    ppermute x4, starting transfers between devices, shift(): lax.ppermute(values, 'y', [(i, (i + step) % size) for i in range(size)])  13.9 us
    dynamic_update_slice x5, local copies, waits for them, and re-layouts, gather_weights(): whole = lax.dynamic_update_slice(whole, part[None], (place, row, 0))  11.5 us
    pallas_call x1, Pallas kernels, last_step(): pl.pallas_call(last_kernel, in_specs=[pl.BlockSpec(memory_space=pltpu.SME...  10.6 us
    all_to_all x1, starting transfers between devices, on_device(): back = lax.all_to_all(back, 'z', 0, 0, tiled=True)[:, :, :CAP]  8.62 us
  transfers between devices with their start and end apart: 18, of which 8 were waited for; matrix products, arithmetic and copies ran while one was open for 15% of the time, Pallas kernels for 9%

profile of v9, /device:TPU:1, one launch (start us, length us, event | category | flops | bytes accessed | tf_op | source)
XLA Modules:
  0.0 227.7 jit_solution(3902283390432242457)
XLA Ops:
  12.1 4.0 %collective-permute-start = (bf16[3584,256]{1,0:T(8,128)(2,1)S(1)}, bf16[3584,256]{1,0:T(8,128)(2,1)}, u32[]{:S(2)}, u32[]{:S(2)}) collective-permute-start(bf16[3584,256]{1,0:T(8,128)(2,1)S(1)} %bitcast.54), channel_id=1, source_target_pairs={{0,1},{1,2},{2,3},{3,0},{4,5},{5,6},{6,7},{7,4},{8,9},{9,10},{10,1... | collective-permute-start | bytes 5505032 | tf_op jit(solution)/shard_map/ppermute | solution.py:37
  16.1 3.4 %collective-permute-start.1 = (bf16[3584,256]{1,0:T(8,128)(2,1)S(1)}, bf16[3584,256]{1,0:T(8,128)(2,1)}, u32[]{:S(2)}, u32[]{:S(2)}) collective-permute-start(bf16[3584,256]{1,0:T(8,128)(2,1)S(1)} %bitcast.55), channel_id=1, source_target_pairs={{0,3},{1,0},{2,1},{3,2},{4,7},{5,4},{6,5},{7,6},{8,11},{9,8},{10,9... | collective-permute-start | bytes 5505032 | tf_op jit(solution)/shard_map/ppermute | solution.py:37
  22.2 14.9 %all-to-all-start = ((f32[16,2,48]{2,1,0:T(2,128)}), f32[16,2,48]{2,1,0:T(2,128)S(1)}, u32[]{:S(2)}, u32[]{:S(2)}) async-start(f32[16,2,48]{2,1,0:T(2,128)} %copy.52), calls=%async_computation | async-start | bytes 32768 | tf_op jit(solution)/shard_map/all_to_all | solution.py:354
  38.9 3.5 %broadcast_in_dim.80 = bf16[4,3584,256]{2,1,0:T(8,128)(2,1)} broadcast(bf16[]{:T(256)} %constant.173.clone.1), dimensions={} | broadcast | bytes 7340034 | tf_op jit(solution)/shard_map/broadcast_in_dim | solution.py:49
  43.9 4.8 %all-to-all-done = f32[16,2,48]{2,1,0:T(2,128)S(1)} async-done(((f32[16,2,48]{2,1,0:T(2,128)}), f32[16,2,48]{2,1,0:T(2,128)S(1)}, u32[]{:S(2)}, u32[]{:S(2)}) %all-to-all-start) | async-done | bytes 6176 | tf_op jit(solution)/shard_map/all_to_all | solution.py:354
  49.7 6.9 %all-to-all-start.2 = ((f32[8,1,24]{2,1,0:T(1,128)}), f32[8,1,24]{2,1,0:T(1,128)S(1)}, u32[]{:S(2)}, u32[]{:S(2)}) async-start(f32[8,1,24]{2,1,0:T(1,128)} %bitcast.16), calls=%async_computation.2 | async-start | bytes 8192 | tf_op jit(solution)/shard_map/all_to_all | solution.py:364
  57.1 4.1 %all-to-all-done.2 = f32[8,1,24]{2,1,0:T(1,128)S(1)} async-done(((f32[8,1,24]{2,1,0:T(1,128)}), f32[8,1,24]{2,1,0:T(1,128)S(1)}, u32[]{:S(2)}, u32[]{:S(2)}) %all-to-all-start.2) | async-done | bytes 800 | tf_op jit(solution)/shard_map/all_to_all | solution.py:364
  67.8 4.5 %collective-permute-start.3 = (bf16[1792,256]{1,0:T(8,128)(2,1)S(1)}, bf16[1792,256]{1,0:T(8,128)(2,1)}, u32[]{:S(2)}, u32[]{:S(2)}) collective-permute-start(bf16[1792,256]{1,0:T(8,128)(2,1)S(1)} %slice.36), channel_id=1, source_target_pairs={{0,3},{1,0},{2,1},{3,2},{4,7},{5,4},{6,5},{7,6},{8,11},{9,8},{10,9... | collective-permute-start | bytes 2752520 | tf_op jit(solution)/shard_map/ppermute | solution.py:37
  72.3 3.5 %all-to-all-start.1 = ((bf16[4,192,512]{2,1,0:T(8,128)(2,1)}), bf16[4,192,512]{2,1,0:T(8,128)(2,1)S(1)}, u32[]{:S(2)}, u32[]{:S(2)}) async-start(bf16[4,192,512]{2,1,0:T(8,128)(2,1)} %bitcast.57), calls=%async_computation.1 | async-start | bytes 1572864 | tf_op jit(solution)/shard_map/all_to_all | solution.py:380
  81.6 16.1 %all-to-all-done.1 = bf16[4,192,512]{2,1,0:T(8,128)(2,1)S(1)} async-done(((bf16[4,192,512]{2,1,0:T(8,128)(2,1)}), bf16[4,192,512]{2,1,0:T(8,128)(2,1)S(1)}, u32[]{:S(2)}, u32[]{:S(2)}) %all-to-all-start.1) | async-done | bytes 786464 | tf_op jit(solution)/shard_map/all_to_all | solution.py:380
  103.2 8.4 %all-gather.2.cloned.1.call-done = bf16[2048,1792]{1,0:T(8,128)(2,1)} async-done(((bf16[128,1792]{1,0:T(8,128)(2,1)}), bf16[2048,1792]{1,0:T(8,128)(2,1)}) %all-gather.2.cloned.1.call-update) | async-done | bytes 7340048 | tf_op jit(solution)/shard_map/all_gather | solution.py:338
  111.6 3.6 %pick_grads.1 = bf16[4,8,24,896]{3,2,1,0:T(8,128)(2,1)} custom-call(f32[4,192,1]{2,1,0:T(8,128)S(1)} %reshape.290.index_ref, bf16[4,512,1792]{2,1,0:T(8,128)(2,1)} %bitcast.52), custom_call_target="tpu_custom_call" | custom-call | tf_op jit(solution)/shard_map/pick_grads/pallas_call | solution.py:91
  115.2 7.5 %all-to-all-start.3 = ((bf16[32,24,896]{2,1,0:T(8,128)(2,1)}), bf16[32,24,896]{2,1,0:T(8,128)(2,1)S(1)}, u32[]{:S(2)}, u32[]{:S(2)}) async-start(bf16[32,24,896]{2,1,0:T(8,128)(2,1)} %bitcast.18), calls=%async_computation.3 | async-start | bytes 2752512 | tf_op jit(solution)/shard_map/all_to_all | solution.py:393
  122.7 3.7 %pick_tokens.1 = bf16[8,4,24,896]{3,2,1,0:T(8,128)(2,1)} custom-call(f32[4,192,1]{2,1,0:T(8,128)S(1)} %reshape.290.index_ref, bf16[4,512,1792]{2,1,0:T(8,128)(2,1)} %bitcast.53), custom_call_target="tpu_custom_call" | custom-call | tf_op jit(solution)/shard_map/pick_tokens/pallas_call | solution.py:91
  126.4 16.2 %all-to-all-done.3 = bf16[32,24,896]{2,1,0:T(8,128)(2,1)S(1)} async-done(((bf16[32,24,896]{2,1,0:T(8,128)(2,1)}), bf16[32,24,896]{2,1,0:T(8,128)(2,1)S(1)}, u32[]{:S(2)}, u32[]{:S(2)}) %all-to-all-start.3) | async-done | bytes 1376288 | tf_op jit(solution)/shard_map/all_to_all | solution.py:393
  142.6 5.4 %all-to-all-start.4 = ((bf16[8,96,896]{2,1,0:T(8,128)(2,1)}), bf16[8,96,896]{2,1,0:T(8,128)(2,1)S(1)}, u32[]{:S(2)}, u32[]{:S(2)}) async-start(bf16[8,96,896]{2,1,0:T(8,128)(2,1)} %bitcast.21), calls=%async_computation.4 | async-start | bytes 2752512 | tf_op jit(solution)/shard_map/all_to_all | solution.py:405
  148.0 5.7 %hidden_step.1 = (bf16[192,1024]{1,0:T(8,128)(2,1)}, f32[192,1]{1,0:T(8,128)}) custom-call(bf16[4,192,896]{2,1,0:T(8,128)(2,1)} %bitcast.56, bf16[4,3584,256]{2,1,0:T(8,128)(2,1)} %bitcast_dynamic-update-slice_fusion.3.matrix_ref, f32[4,192,256]{2,1,0:T(8,128)S(1)} %get-tuple-element.29.out_act_ref, f32[4,192,256]{2,1,0:T(8,128)} %get-tuple-element.30.dw_act_ref), custom_call_target="tpu_custom_call" | custom-call | tf_op jit(solution)/shard_map/hidden_step/pallas_call | solution.py:184
  160.3 7.4 %collective-permute-done.4.west_ref.west_hbm = bf16[192,1024]{1,0:T(8,128)(2,1)S(1)} collective-permute-done((bf16[192,1024]{1,0:T(8,128)(2,1)}, bf16[192,1024]{1,0:T(8,128)(2,1)S(1)}, u32[]{:S(2)}, u32[]{:S(2)}) %collective-permute-start.4) | collective-permute-done | bytes 393248 | tf_op jit(solution)/shard_map/ppermute | solution.py:63
  173.3 4.6 %collective-permute-start.8 = (bf16[128,2048]{1,0:T(8,128)(2,1)}, bf16[128,2048]{1,0:T(8,128)(2,1)S(1)}, u32[]{:S(2)}, u32[]{:S(2)}) collective-permute-start(bf16[128,2048]{1,0:T(8,128)(2,1)} %get-tuple-element.41), channel_id=1, source_target_pairs={{0,3},{1,2},{2,1},{3,0},{4,7},{5,6},{6,5},{7,4},{8,11},{9,10},{10,... | collective-permute-start | bytes 1572872 | tf_op jit(solution)/shard_map/ppermute | solution.py:63
  177.9 8.6 %all-to-all-start.5 = ((f32[16,8,128]{2,1,0:T(8,128)}), f32[16,8,128]{2,1,0:T(8,128)S(1)}, u32[]{:S(2)}, u32[]{:S(2)}) async-start(f32[16,8,128]{2,1,0:T(8,128)} %pad_dynamic-update-slice_fusion), calls=%async_computation.5 | async-start | bytes 131072 | tf_op jit(solution)/shard_map/all_to_all | solution.py:418
  187.5 4.1 %collective-permute-start.7 = (bf16[128,1408]{1,0:T(8,128)(2,1)S(1)}, bf16[128,1408]{1,0:T(8,128)(2,1)S(1)}, u32[]{:S(2)}, u32[]{:S(2)}) collective-permute-start(bf16[128,1408]{1,0:T(8,128)(2,1)S(1)} %slice_add_fusion.low_a), channel_id=1, source_target_pairs={{0,3},{1,2},{2,1},{3,0},{4,7},{5,6},{6,5},{7,4},{8,11},{9,10},{10,... | collective-permute-start | bytes 1081352 | tf_op jit(solution)/shard_map/ppermute | solution.py:63
  194.6 3.5 %all-to-all-done.5 = f32[16,8,128]{2,1,0:T(8,128)S(1)} async-done(((f32[16,8,128]{2,1,0:T(8,128)}), f32[16,8,128]{2,1,0:T(8,128)S(1)}, u32[]{:S(2)}, u32[]{:S(2)}) %all-to-all-start.5) | async-done | bytes 65568 | tf_op jit(solution)/shard_map/all_to_all | solution.py:418
  198.8 8.3 %all-to-all-start.6 = ((f32[32,1,96]{2,1,0:T(1,128)}), f32[32,1,96]{2,1,0:T(1,128)S(1)}, u32[]{:S(2)}, u32[]{:S(2)}) async-start(f32[32,1,96]{2,1,0:T(1,128)} %bitcast.25), calls=%async_computation.6 | async-start | bytes 32768 | tf_op jit(solution)/shard_map/all_to_all | solution.py:421
  208.4 10.6 %last_step.1 = bf16[1,896,1024]{2,1,0:T(8,128)(2,1)} custom-call(s32[1]{0:T(128)} %bitcast.27.rank_ref, bf16[896,768]{1,0:T(8,128)(2,1)S(1)} %copy-done, bf16[192,1024]{1,0:T(8,128)(2,1)S(1)} %copy-done.1, bf16[128,1408]{1,0:T(8,128)(2,1)S(1)} %slice_add_fusion.low_a, bf16[128,1408]{1,0:T(8,128)(2,1)S(1)} %collective-permute-done.7.low_b, ...), custom_call_target="tpu_custom_call" | custom-call | tf_op jit(solution)/shard_map/last_step/pallas_call | solution.py:302
  (90 shorter events, 50.1 us)
Async XLA Ops:
  7.2 12.4 %copy-start.3 = (s32[128,8]{0,1:T(8,128)S(1)}, s32[128,8]{0,1:T(8,128)}, u32[]{:S(2)}) copy-start(s32[128,8]{0,1:T(8,128)} %param.9) | copy-start | bytes 12292
  7.2 12.5 %copy-start.4 = (bf16[128,8]{0,1:T(8,128)(2,1)S(1)}, bf16[128,8]{0,1:T(8,128)(2,1)}, u32[]{:S(2)}) copy-start(bf16[128,8]{0,1:T(8,128)(2,1)} %param.10) | copy-start | bytes 6148
  7.2 30.0 %copy-start.6 = (bf16[1,768,256]{2,1,0:T(8,128)(2,1)S(1)}, bf16[1,768,256]{2,1,0:T(8,128)(2,1)}, u32[]{:S(2)}) copy-start(bf16[1,768,256]{2,1,0:T(8,128)(2,1)} %param.12) | copy-start | bytes 1179652
  7.2 30.0 %copy-start.5 = (bf16[1,768,256]{2,1,0:T(8,128)(2,1)S(1)}, bf16[1,768,256]{2,1,0:T(8,128)(2,1)}, u32[]{:S(2)}) copy-start(bf16[1,768,256]{2,1,0:T(8,128)(2,1)} %param.13) | copy-start | bytes 1179652
  7.2 104.4 %all-gather.2.cloned.1.call-start = ((), (), s32[]{:S(2)}) async-start(), calls=%async_computation.7 | async-start | bytes 7798784 | tf_op jit(solution)/shard_map/all_gather | solution.py:338
  12.1 50.3 %collective-permute-start = (bf16[3584,256]{1,0:T(8,128)(2,1)S(1)}, bf16[3584,256]{1,0:T(8,128)(2,1)}, u32[]{:S(2)}, u32[]{:S(2)}) collective-permute-start(bf16[3584,256]{1,0:T(8,128)(2,1)S(1)} %bitcast.54), channel_id=1, source_target_pairs={{0,1},{1,2},{2,3},{3,0},{4,5},{5,6},{6,7},{7,4},{8,9},{9,10},{10,1... | collective-permute-start | bytes 5505032 | tf_op jit(solution)/shard_map/ppermute | solution.py:37
  16.1 46.3 %collective-permute-start.1 = (bf16[3584,256]{1,0:T(8,128)(2,1)S(1)}, bf16[3584,256]{1,0:T(8,128)(2,1)}, u32[]{:S(2)}, u32[]{:S(2)}) collective-permute-start(bf16[3584,256]{1,0:T(8,128)(2,1)S(1)} %bitcast.55), channel_id=1, source_target_pairs={{0,3},{1,0},{2,1},{3,2},{4,7},{5,4},{6,5},{7,6},{8,11},{9,8},{10,9... | collective-permute-start | bytes 5505032 | tf_op jit(solution)/shard_map/ppermute | solution.py:37
  22.2 26.4 %all-to-all-start = ((f32[16,2,48]{2,1,0:T(2,128)}), f32[16,2,48]{2,1,0:T(2,128)S(1)}, u32[]{:S(2)}, u32[]{:S(2)}) async-start(f32[16,2,48]{2,1,0:T(2,128)} %copy.52), calls=%async_computation | async-start | bytes 32768 | tf_op jit(solution)/shard_map/all_to_all | solution.py:354
  49.7 11.5 %all-to-all-start.2 = ((f32[8,1,24]{2,1,0:T(1,128)}), f32[8,1,24]{2,1,0:T(1,128)S(1)}, u32[]{:S(2)}, u32[]{:S(2)}) async-start(f32[8,1,24]{2,1,0:T(1,128)} %bitcast.16), calls=%async_computation.2 | async-start | bytes 8192 | tf_op jit(solution)/shard_map/all_to_all | solution.py:364
  64.6 34.2 %collective-permute-start.2 = (bf16[1792,256]{1,0:T(8,128)(2,1)}, bf16[1792,256]{1,0:T(8,128)(2,1)}, u32[]{:S(2)}, u32[]{:S(2)}) collective-permute-start(bf16[1792,256]{1,0:T(8,128)(2,1)} %slice.35), channel_id=1, source_target_pairs={{0,1},{1,2},{2,3},{3,0},{4,5},{5,6},{6,7},{7,4},{8,9},{9,10},{10,1... | collective-permute-start | bytes 2752520 | tf_op jit(solution)/shard_map/ppermute | solution.py:37
  67.8 33.2 %collective-permute-start.3 = (bf16[1792,256]{1,0:T(8,128)(2,1)S(1)}, bf16[1792,256]{1,0:T(8,128)(2,1)}, u32[]{:S(2)}, u32[]{:S(2)}) collective-permute-start(bf16[1792,256]{1,0:T(8,128)(2,1)S(1)} %slice.36), channel_id=1, source_target_pairs={{0,3},{1,0},{2,1},{3,2},{4,7},{5,4},{6,5},{7,6},{8,11},{9,8},{10,9... | collective-permute-start | bytes 2752520 | tf_op jit(solution)/shard_map/ppermute | solution.py:37
  72.3 25.3 %all-to-all-start.1 = ((bf16[4,192,512]{2,1,0:T(8,128)(2,1)}), bf16[4,192,512]{2,1,0:T(8,128)(2,1)S(1)}, u32[]{:S(2)}, u32[]{:S(2)}) async-start(bf16[4,192,512]{2,1,0:T(8,128)(2,1)} %bitcast.57), calls=%async_computation.1 | async-start | bytes 1572864 | tf_op jit(solution)/shard_map/all_to_all | solution.py:380
  115.2 27.4 %all-to-all-start.3 = ((bf16[32,24,896]{2,1,0:T(8,128)(2,1)}), bf16[32,24,896]{2,1,0:T(8,128)(2,1)S(1)}, u32[]{:S(2)}, u32[]{:S(2)}) async-start(bf16[32,24,896]{2,1,0:T(8,128)(2,1)} %bitcast.18), calls=%async_computation.3 | async-start | bytes 2752512 | tf_op jit(solution)/shard_map/all_to_all | solution.py:393
  142.6 5.4 %copy-start.2 = (bf16[32,24,896]{2,1,0:T(8,128)(2,1)}, bf16[32,24,896]{2,1,0:T(8,128)(2,1)S(1)}, u32[]{:S(2)}) copy-start(bf16[32,24,896]{2,1,0:T(8,128)(2,1)S(1)} %all-to-all-done.3) | copy-start | bytes 4128772
  142.6 25.7 %all-to-all-start.4 = ((bf16[8,96,896]{2,1,0:T(8,128)(2,1)}), bf16[8,96,896]{2,1,0:T(8,128)(2,1)S(1)}, u32[]{:S(2)}, u32[]{:S(2)}) async-start(bf16[8,96,896]{2,1,0:T(8,128)(2,1)} %bitcast.21), calls=%async_computation.4 | async-start | bytes 2752512 | tf_op jit(solution)/shard_map/all_to_all | solution.py:405
  153.8 53.3 %copy-start.1 = (bf16[192,1024]{1,0:T(8,128)(2,1)S(1)}, bf16[192,1024]{1,0:T(8,128)(2,1)}, u32[]{:S(2)}) copy-start(bf16[192,1024]{1,0:T(8,128)(2,1)} %get-tuple-element.31.own_hbm) | copy-start | bytes 1179652
  153.8 14.0 %collective-permute-start.4 = (bf16[192,1024]{1,0:T(8,128)(2,1)}, bf16[192,1024]{1,0:T(8,128)(2,1)S(1)}, u32[]{:S(2)}, u32[]{:S(2)}) collective-permute-start(bf16[192,1024]{1,0:T(8,128)(2,1)} %get-tuple-element.31.own_hbm), channel_id=1, source_target_pairs={{0,3},{1,2},{2,1},{3,0},{4,7},{5,6},{6,5},{7,4},{8,11},{9,10},{10,... | collective-permute-start | bytes 1179656 | tf_op jit(solution)/shard_map/ppermute | solution.py:63
  155.8 12.5 %collective-permute-start.5 = (bf16[192,1024]{1,0:T(8,128)(2,1)}, bf16[192,1024]{1,0:T(8,128)(2,1)S(1)}, u32[]{:S(2)}, u32[]{:S(2)}) collective-permute-start(bf16[192,1024]{1,0:T(8,128)(2,1)} %get-tuple-element.31.own_hbm), channel_id=1, source_target_pairs={{0,1},{1,0},{2,3},{3,2},{4,5},{5,4},{6,7},{7,6},{8,9},{9,8},{10,11... | collective-permute-start | bytes 1179656 | tf_op jit(solution)/shard_map/ppermute | solution.py:63
  171.2 15.3 %collective-permute-start.6 = (bf16[128,2176]{1,0:T(8,128)(2,1)}, bf16[128,2176]{1,0:T(8,128)(2,1)S(1)}, u32[]{:S(2)}, u32[]{:S(2)}) collective-permute-start(bf16[128,2176]{1,0:T(8,128)(2,1)} %get-tuple-element.40), channel_id=1, source_target_pairs={{0,1},{1,0},{2,3},{3,2},{4,5},{5,4},{6,7},{7,6},{8,9},{9,8},{10,11... | collective-permute-start | bytes 1671176 | tf_op jit(solution)/shard_map/ppermute | solution.py:63
  173.3 18.3 %collective-permute-start.8 = (bf16[128,2048]{1,0:T(8,128)(2,1)}, bf16[128,2048]{1,0:T(8,128)(2,1)S(1)}, u32[]{:S(2)}, u32[]{:S(2)}) collective-permute-start(bf16[128,2048]{1,0:T(8,128)(2,1)} %get-tuple-element.41), channel_id=1, source_target_pairs={{0,3},{1,2},{2,1},{3,0},{4,7},{5,6},{6,5},{7,4},{8,11},{9,10},{10,... | collective-permute-start | bytes 1572872 | tf_op jit(solution)/shard_map/ppermute | solution.py:63
  177.9 20.2 %all-to-all-start.5 = ((f32[16,8,128]{2,1,0:T(8,128)}), f32[16,8,128]{2,1,0:T(8,128)S(1)}, u32[]{:S(2)}, u32[]{:S(2)}) async-start(f32[16,8,128]{2,1,0:T(8,128)} %pad_dynamic-update-slice_fusion), calls=%async_computation.5 | async-start | bytes 131072 | tf_op jit(solution)/shard_map/all_to_all | solution.py:418
  187.5 19.5 %collective-permute-start.7 = (bf16[128,1408]{1,0:T(8,128)(2,1)S(1)}, bf16[128,1408]{1,0:T(8,128)(2,1)S(1)}, u32[]{:S(2)}, u32[]{:S(2)}) collective-permute-start(bf16[128,1408]{1,0:T(8,128)(2,1)S(1)} %slice_add_fusion.low_a), channel_id=1, source_target_pairs={{0,3},{1,2},{2,1},{3,0},{4,7},{5,6},{6,5},{7,4},{8,11},{9,10},{10,... | collective-permute-start | bytes 1081352 | tf_op jit(solution)/shard_map/ppermute | solution.py:63
  192.6 14.4 %collective-permute-start.9 = (bf16[128,1280]{1,0:T(8,128)(2,1)S(1)}, bf16[128,1280]{1,0:T(8,128)(2,1)}, u32[]{:S(2)}, u32[]{:S(2)}) collective-permute-start(bf16[128,1280]{1,0:T(8,128)(2,1)S(1)} %slice_add_fusion.1.high_a), channel_id=1, source_target_pairs={{0,1},{1,0},{2,3},{3,2},{4,5},{5,4},{6,7},{7,6},{8,9},{9,8},{10,11... | collective-permute-start | bytes 983048 | tf_op jit(solution)/shard_map/ppermute | solution.py:63
  198.8 20.2 %all-to-all-start.6 = ((f32[32,1,96]{2,1,0:T(1,128)}), f32[32,1,96]{2,1,0:T(1,128)S(1)}, u32[]{:S(2)}, u32[]{:S(2)}) async-start(f32[32,1,96]{2,1,0:T(1,128)} %bitcast.25), calls=%async_computation.6 | async-start | bytes 32768 | tf_op jit(solution)/shard_map/all_to_all | solution.py:421
  (1 other events, 1.3 us)
Sparse Core Ops, SparseCore 0:
  10.1 101.4 all-gather.1
